TPU v7x, 32 devices: a whole 2x2x4 slice. The times are simulated.
32 devices in a mesh: expert: 8 (over y, x, core), tensor: 4 (over z).
Axes of the slice: x: 2, y: 2, z: 4, core: 2. Of those that a mesh axis runs over, the one named last changes fastest.
Arguments:
- tokens: bfloat16 [4096, 2048], P('expert'), may hold values from -6 to 6
- sequence_numbers: int32 [4096], P('expert'), may hold values from 0 to 7, as said below
- routes: int32 [4096, 8], P('expert'), may hold values from 0 to 15, all different within a row; in each aligned block of 512 rows (0 to 511, 512 to 1023, ...) at most 384 rows name the same one
- attn_gain: float32 [2048], replicated, may hold values from 0.5 to 1.5
- w_query: bfloat16 [2048, 4096], P(None, 'tensor'), may hold values from -0.125 to 0.125
- key_projection: bfloat16 [2048, 512], P(None, 'tensor'), may hold values from -0.125 to 0.125
- value_projection: bfloat16 [2048, 512], P(None, 'tensor'), may hold values from -0.125 to 0.125
- query_gain: float32 [128], replicated, may hold values from 0.5 to 1.5
- key_gain: float32 [128], replicated, may hold values from 0.5 to 1.5
- w_out: bfloat16 [4096, 2048], P('tensor'), may hold values from -0.5 to 0.5
- moe_gain: float32 [2048], replicated, may hold values from 0.5 to 1.5
- w_router: bfloat16 [2048, 16], replicated, may hold values from -0.0625 to 0.0625
- w_gate: bfloat16 [16, 2048, 768], P('expert', None, 'tensor'), may hold values from -0.125 to 0.125
- w_up: bfloat16 [16, 2048, 768], P('expert', None, 'tensor'), may hold values from -0.125 to 0.125
- w_down: bfloat16 [16, 768, 2048], P('expert', 'tensor'), may hold values from -0.875 to 0.875
- cotangent: bfloat16 [4096, 2048], P('expert', 'tensor'), may hold values from -6 to 6
Outputs:
- block_out: bfloat16 [4096, 2048], P('expert', 'tensor')
- input_grad: float32 [4096, 2048], P('expert', 'tensor')
- attn_gain_grad: float32 [2048], P('expert')
- query_weight_grad: float32 [2048, 4096], P('expert', 'tensor')
- key_weight_grad: float32 [2048, 512], P('expert', 'tensor')
- value_weight_grad: float32 [2048, 512], P('expert', 'tensor')
- query_gain_grad: float32 [128], P('expert')
- key_gain_grad: float32 [128], P('expert')
- out_weight_grad: float32 [4096, 2048], P('tensor', 'expert')
- moe_gain_grad: float32 [2048], P('expert')
- router_grad: float32 [2048, 16], P('expert')
- gate_grad: float32 [16, 2048, 768], P('expert', None, 'tensor')
- up_grad: float32 [16, 2048, 768], P('expert', None, 'tensor')
- down_grad: float32 [16, 768, 2048], P('expert', 'tensor')
Inputs may be any that keep to these rules, and one draw needn't show every extreme that they name: `sequence_numbers`: inside each device's 512 rows the numbers start at 0 and rise by one where a new sequence begins; a device holds 1 to 8 sequences, some device a single one of 512 tokens and some device 8. `routes`: among the rows of one device no expert is named by more than 384 rows, a bound that some block reaches.
All inputs are finite; a program needn't handle non-finite values.
Results may differ from a plain program's by a relative error of at most 0.024.
Values may be sent and summed in bfloat16 or wider, within the bound.
No kernel may reach another device: no remote copies, remote signals or barrier semaphores. Data moves between devices by JAX's collectives and lax.ppermute only.
A program may use at most 384 MiB of HBM per device.

v0:
```python
import jax
import jax.numpy as jnp
from jax import lax
from jax.sharding import PartitionSpec as P


def rms_norm(values, gain_vec):
    return values * lax.rsqrt(jnp.mean(values * values, axis=-1, keepdims=True) + 1e-06) * gain_vec


def rotate(values, cos_table, sine_table):
    half_dim = values.shape[-1] // 2
    first_half = values[..., :half_dim]
    second = values[..., half_dim:]
    return jnp.concatenate(
        [
            first_half * cos_table - second * sine_table,
            second * cos_table + first_half * sine_table,
        ],
        axis=-1,
    )


def rope_tables(positions, head_dim):
    half_dim = head_dim // 2
    frequency = jnp.power(1000000.0, -2.0 * jnp.arange(half_dim).astype(jnp.float32) / head_dim)
    angles = positions.astype(jnp.float32)[:, None] * frequency[None, :]
    return (jnp.cos(angles)[:, None, :], jnp.sin(angles)[:, None, :])


def seq_positions(sequence_numbers, block_len):
    total_len = sequence_numbers.shape[0]
    places = jnp.arange(total_len)
    previous = jnp.concatenate([sequence_numbers[:1] - 1, sequence_numbers[:-1]])
    starts = (places % block_len == 0) | (sequence_numbers != previous)
    first_place = lax.cummax(jnp.where(starts, places, 0), axis=0)
    return places - first_place


def swiglu(gate_in, up_in):
    return jax.nn.silu(gate_in) * up_in


def per_device(
    tokens,
    sequence_numbers,
    routes,
    attn_gain,
    w_query,
    key_projection,
    value_projection,
    query_gain,
    key_gain,
    w_out,
    moe_gain,
    w_router,
    w_gate,
    w_up,
    w_down,
    cotangent,
):
    tok_count, model_width = tokens.shape
    top_count = routes.shape[1]
    head_dim = query_gain.shape[0]
    q_heads = w_query.shape[1] // head_dim
    kv_heads = key_projection.shape[1] // head_dim
    group_size = q_heads // kv_heads
    tensor_size = lax.axis_size("tensor")
    tensor_pos = lax.axis_index("tensor")
    expert_size = lax.axis_size("expert")
    local_experts = w_gate.shape[0]
    experts = local_experts * expert_size
    capacity = min(tok_count, tok_count * top_count * 3 // (2 * experts))
    score_scale = head_dim ** (-0.5)
    part_width = model_width // tensor_size
    part_start = tensor_pos * part_width
    positions = seq_positions(sequence_numbers, tok_count)
    cos_table, sine_table = rope_tables(positions, head_dim)
    local_index = jnp.arange(tok_count)
    inputs = tokens.astype(jnp.float32)
    normed_one, pull_one = jax.vjp(rms_norm, inputs, attn_gain)
    first_hidden = normed_one.astype(jnp.bfloat16)
    query_rows = jnp.dot(first_hidden, w_query, preferred_element_type=jnp.float32).reshape(
        tok_count, q_heads, head_dim
    )
    key_matrix = jnp.dot(first_hidden, key_projection, preferred_element_type=jnp.float32).reshape(
        tok_count, kv_heads, head_dim
    )
    value_matrix = (
        jnp.dot(first_hidden, value_projection, preferred_element_type=jnp.float32)
        .astype(jnp.bfloat16)
        .reshape(tok_count, kv_heads, head_dim)
    )

    def prepare(values, gain_vec):
        return rotate(rms_norm(values, gain_vec), cos_table, sine_table)

    query_rot, pull_query = jax.vjp(prepare, query_rows, query_gain)
    key_rot, pull_key = jax.vjp(prepare, key_matrix, key_gain)
    query_low = query_rot.astype(jnp.bfloat16).reshape(tok_count, kv_heads, group_size, head_dim)
    key_low = key_rot.astype(jnp.bfloat16)

    def block_scores():
        scores = (
            jnp.einsum("qhgd,khd->hgqk", query_low, key_low, preferred_element_type=jnp.float32)
            * score_scale
        )
        allowed = (sequence_numbers[:, None] == sequence_numbers[None, :]) & (
            local_index[:, None] >= local_index[None, :]
        )
        return jnp.where(allowed, scores, -1e30)

    scores = block_scores()
    row_peak = jnp.max(scores, axis=-1, keepdims=True)
    exp_scores = jnp.exp(scores - row_peak)
    row_total = jnp.sum(exp_scores, axis=-1, keepdims=True)
    probabilities = exp_scores / row_total
    log_totals = row_peak + jnp.log(row_total)
    outputs = jnp.einsum(
        "hgqk,khd->qhgd",
        probabilities.astype(jnp.bfloat16),
        value_matrix,
        preferred_element_type=jnp.float32,
    )
    attended_low = outputs.reshape(tok_count, q_heads * head_dim).astype(jnp.bfloat16)
    branch = lax.psum(jnp.dot(attended_low, w_out, preferred_element_type=jnp.float32), "tensor")
    middle = inputs + branch
    normed_two, pull_two = jax.vjp(rms_norm, middle, moe_gain)
    hidden_two = normed_two.astype(jnp.bfloat16)
    logits = jnp.dot(hidden_two, w_router, preferred_element_type=jnp.float32)
    expert_ids = jnp.arange(experts)
    picked = (routes[:, :, None] == expert_ids[None, None, :]).astype(jnp.float32)

    def route_weights(logit_vals):
        probabilities = jax.nn.softmax(logit_vals, axis=-1)
        chosen = jnp.sum(picked * probabilities[:, None, :], axis=-1)
        return chosen / jnp.sum(chosen, axis=-1, keepdims=True)

    weights, pull_router = jax.vjp(route_weights, logits)
    flat_routes = routes.reshape(-1)
    onehot = (flat_routes[:, None] == expert_ids[None, :]).astype(jnp.int32)
    slot_rank = jnp.sum((jnp.cumsum(onehot, axis=0) - onehot) * onehot, axis=1)
    places = flat_routes * capacity + slot_rank
    token_of = jnp.arange(tok_count * top_count) // top_count

    def fill_slots(rows):
        buffer = jnp.zeros((experts * capacity, rows.shape[-1]), rows.dtype).at[places].set(rows)
        return buffer.reshape(expert_size, local_experts, capacity, rows.shape[-1])

    received = lax.all_to_all(
        fill_slots(hidden_two[token_of]), "expert", split_axis=0, concat_axis=0, tiled=True
    )
    gate_vals = jnp.einsum("secd,edf->secf", received, w_gate, preferred_element_type=jnp.float32)
    up_vals = jnp.einsum("secd,edf->secf", received, w_up, preferred_element_type=jnp.float32)
    activated, pull_swiglu = jax.vjp(swiglu, gate_vals, up_vals)
    act_low = activated.astype(jnp.bfloat16)
    partial_low = lax.optimization_barrier(
        jnp.einsum("secf,efd->secd", act_low, w_down, preferred_element_type=jnp.float32).astype(
            jnp.bfloat16
        )
    )
    slice_total = lax.psum_scatter(
        partial_low.astype(jnp.float32).astype(jnp.bfloat16),
        "tensor",
        scatter_dimension=3,
        tiled=True,
    ).astype(jnp.float32)
    returned = (
        lax.all_to_all(
            slice_total.astype(jnp.bfloat16), "expert", split_axis=0, concat_axis=0, tiled=True
        )
        .astype(slice_total.dtype)
        .reshape(experts * capacity, part_width)
    )
    route_rows = returned[places].reshape(tok_count, top_count, part_width)
    mixed_out = jnp.zeros((tok_count, part_width), jnp.float32)
    for slot_index in range(top_count):
        mixed_out = mixed_out + weights[:, slot_index, None] * route_rows[:, slot_index]
    block_out = (lax.dynamic_slice_in_dim(middle, part_start, part_width, 1) + mixed_out).astype(
        jnp.bfloat16
    )
    cot_part = cotangent.astype(jnp.float32)
    weight_part = jnp.sum(cot_part[:, None, :] * route_rows, axis=-1)
    grad_rows = (
        (weights[:, :, None] * cot_part[:, None, :])
        .astype(jnp.bfloat16)
        .reshape(tok_count * top_count, part_width)
    )
    grad_arrived = lax.all_to_all(
        fill_slots(grad_rows), "expert", split_axis=0, concat_axis=0, tiled=True
    )
    grad_received = lax.all_gather(grad_arrived, "tensor", axis=3, tiled=True)
    act_grad = jnp.einsum(
        "secd,efd->secf", grad_received, w_down, preferred_element_type=jnp.float32
    )
    down_grad = jnp.einsum(
        "secf,secd->efd", act_low, grad_received, preferred_element_type=jnp.float32
    )
    gate_grad_f, up_grad_f = pull_swiglu(act_grad)
    gate_low = gate_grad_f.astype(jnp.bfloat16)
    up_low = up_grad_f.astype(jnp.bfloat16)
    gate_grad = jnp.einsum("secd,secf->edf", received, gate_low, preferred_element_type=jnp.float32)
    up_grad = jnp.einsum("secd,secf->edf", received, up_low, preferred_element_type=jnp.float32)
    input_low = lax.optimization_barrier(
        (
            jnp.einsum("secf,edf->secd", gate_low, w_gate, preferred_element_type=jnp.float32)
            + jnp.einsum("secf,edf->secd", up_low, w_up, preferred_element_type=jnp.float32)
        ).astype(jnp.bfloat16)
    )
    input_total = lax.psum_scatter(
        input_low.astype(jnp.float32).astype(jnp.bfloat16),
        "tensor",
        scatter_dimension=3,
        tiled=True,
    ).astype(jnp.float32)
    grad_returned = (
        lax.all_to_all(
            input_total.astype(jnp.bfloat16), "expert", split_axis=0, concat_axis=0, tiled=True
        )
        .astype(input_total.dtype)
        .reshape(experts * capacity, part_width)
    )
    grad_routes = grad_returned[places].reshape(tok_count, top_count, part_width)
    hidden_part = jnp.zeros((tok_count, part_width), jnp.float32)
    for slot_index in range(top_count):
        hidden_part = hidden_part + grad_routes[:, slot_index]
    hidden_grad, weight_joined, cot_float = (
        lax.all_gather(hidden_part.astype(jnp.bfloat16), "tensor", axis=1, tiled=True).astype(
            hidden_part.dtype
        ),
        lax.all_gather(weight_part.astype(jnp.bfloat16), "tensor", axis=1, tiled=True).astype(
            weight_part.dtype
        ),
        lax.all_gather(cot_part.astype(jnp.bfloat16), "tensor", axis=1, tiled=True).astype(
            cot_part.dtype
        ),
    )
    weight_grad = jnp.sum(weight_joined.reshape(tok_count, tensor_size, top_count), axis=1)
    (logit_grad,) = pull_router(weight_grad)
    logit_low = logit_grad.astype(jnp.bfloat16)
    router_grad = jnp.einsum("nd,ne->de", hidden_two, logit_low, preferred_element_type=jnp.float32)
    hidden_grad = hidden_grad + jnp.einsum(
        "ne,de->nd", logit_low, w_router, preferred_element_type=jnp.float32
    )
    middle_norm_grad, moe_gain_grad = pull_two(hidden_grad)
    middle_grad = middle_norm_grad + cot_float
    branch_low = middle_grad.astype(jnp.bfloat16)
    out_weight_grad = jnp.einsum(
        "nc,nd->cd", attended_low, branch_low, preferred_element_type=jnp.float32
    )
    attended_grad = (
        jnp.einsum("nd,cd->nc", branch_low, w_out, preferred_element_type=jnp.float32)
        .astype(jnp.bfloat16)
        .reshape(tok_count, kv_heads, group_size, head_dim)
    )
    scores = block_scores()
    probabilities = jnp.exp(scores - log_totals)
    prob_grad = jnp.einsum(
        "qhgd,khd->hgqk", attended_grad, value_matrix, preferred_element_type=jnp.float32
    )
    row_delta = jnp.sum(probabilities * prob_grad, axis=-1, keepdims=True)
    score_low = (probabilities * (prob_grad - row_delta)).astype(jnp.bfloat16)
    query_grads = (
        jnp.einsum("hgqk,khd->qhgd", score_low, key_low, preferred_element_type=jnp.float32)
        * score_scale
    )
    key_grad = (
        jnp.einsum("hgqk,qhgd->khd", score_low, query_low, preferred_element_type=jnp.float32)
        * score_scale
    )
    value_grad = jnp.einsum(
        "hgqk,qhgd->khd",
        probabilities.astype(jnp.bfloat16),
        attended_grad,
        preferred_element_type=jnp.float32,
    )
    query_rot_grad = query_grads.reshape(tok_count, q_heads, head_dim)
    query_pre_grad, query_gain_part = pull_query(query_rot_grad)
    key_pre_grad, key_gain_part = pull_key(key_grad)
    query_grad_low = query_pre_grad.reshape(tok_count, q_heads * head_dim).astype(jnp.bfloat16)
    key_grad_low = key_pre_grad.reshape(tok_count, kv_heads * head_dim).astype(jnp.bfloat16)
    value_grad_low = value_grad.reshape(tok_count, kv_heads * head_dim).astype(jnp.bfloat16)
    query_weight_grad = jnp.einsum(
        "nd,nc->dc", first_hidden, query_grad_low, preferred_element_type=jnp.float32
    )
    key_weight_grad = jnp.einsum(
        "nd,nc->dc", first_hidden, key_grad_low, preferred_element_type=jnp.float32
    )
    value_weight_grad = jnp.einsum(
        "nd,nc->dc", first_hidden, value_grad_low, preferred_element_type=jnp.float32
    )
    hidden_one_part = jnp.einsum(
        "nc,dc->nd", query_grad_low, w_query, preferred_element_type=jnp.float32
    )
    hidden_one_part = hidden_one_part + jnp.einsum(
        "nc,dc->nd", key_grad_low, key_projection, preferred_element_type=jnp.float32
    )
    hidden_one_part = hidden_one_part + jnp.einsum(
        "nc,dc->nd", value_grad_low, value_projection, preferred_element_type=jnp.float32
    )
    hidden_one_grad, query_gain_grad, key_gain_grad = (
        lax.psum(hidden_one_part.astype(jnp.bfloat16), "tensor").astype(jnp.float32),
        lax.psum(query_gain_part.astype(jnp.bfloat16), "tensor").astype(jnp.float32),
        lax.psum(key_gain_part.astype(jnp.bfloat16), "tensor").astype(jnp.float32),
    )
    input_norm_grad, attn_gain_grad = pull_one(hidden_one_grad)
    input_grad = lax.dynamic_slice_in_dim(middle_grad + input_norm_grad, part_start, part_width, 1)
    summed = (
        lax.psum_scatter(
            attn_gain_grad.astype(jnp.bfloat16), "expert", scatter_dimension=0, tiled=True
        ).astype(jnp.float32),
        lax.psum_scatter(
            query_weight_grad.astype(jnp.bfloat16), "expert", scatter_dimension=0, tiled=True
        ).astype(jnp.float32),
        lax.psum_scatter(
            key_weight_grad.astype(jnp.bfloat16), "expert", scatter_dimension=0, tiled=True
        ).astype(jnp.float32),
        lax.psum_scatter(
            value_weight_grad.astype(jnp.bfloat16), "expert", scatter_dimension=0, tiled=True
        ).astype(jnp.float32),
        lax.psum_scatter(
            query_gain_grad.astype(jnp.bfloat16), "expert", scatter_dimension=0, tiled=True
        ).astype(jnp.float32),
        lax.psum_scatter(
            key_gain_grad.astype(jnp.bfloat16), "expert", scatter_dimension=0, tiled=True
        ).astype(jnp.float32),
        lax.psum_scatter(
            out_weight_grad.astype(jnp.bfloat16), "expert", scatter_dimension=1, tiled=True
        ).astype(jnp.float32),
        lax.psum_scatter(
            moe_gain_grad.astype(jnp.bfloat16), "expert", scatter_dimension=0, tiled=True
        ).astype(jnp.float32),
        lax.psum_scatter(
            router_grad.astype(jnp.bfloat16), "expert", scatter_dimension=0, tiled=True
        ).astype(jnp.float32),
    )
    return (
        block_out,
        input_grad,
        summed[0],
        summed[1],
        summed[2],
        summed[3],
        summed[4],
        summed[5],
        summed[6],
        summed[7],
        summed[8],
        gate_grad,
        up_grad,
        down_grad,
    )


def solution(mesh):
    placed = (
        P("expert", None),
        P("expert"),
        P("expert", None),
        P(),
        P(None, "tensor"),
        P(None, "tensor"),
        P(None, "tensor"),
        P(),
        P(),
        P("tensor", None),
        P(),
        P(),
        P("expert", None, "tensor"),
        P("expert", None, "tensor"),
        P("expert", "tensor", None),
        P("expert", "tensor"),
    )
    return jax.shard_map(
        per_device,
        mesh=mesh,
        in_specs=placed,
        out_specs=(
            P("expert", "tensor"),
            P("expert", "tensor"),
            P("expert"),
            P("expert", "tensor"),
            P("expert", "tensor"),
            P("expert", "tensor"),
            P("expert"),
            P("expert"),
            P("tensor", "expert"),
            P("expert"),
            P("expert", None),
            P("expert", None, "tensor"),
            P("expert", None, "tensor"),
            P("expert", "tensor", None),
        ),
        check_vma=False,
    )
```

profile of v0, /device:TPU:0, one launch (start us, length us, event | category | flops | bytes accessed | tf_op | source)
XLA Modules:
  0.0 2129.4 jit_solution(1926159250201408019)
XLA Ops:
  48.0 150.2 %all-reduce.13.cloned.1.call-done = f32[512,2048]{1,0:T(8,128)} async-done(((f32[512,2048]{1,0:T(8,128)}), f32[512,2048]{1,0:T(8,128)}) %all-reduce.13.cloned.1.call-update) | async-done | bytes 4194320 | tf_op jit(solution)/shard_map/psum | solution.py:126
  207.4 23.5 %scatter_custom_fusion.1 = bf16[6144,512]{1,0:T(8,128)(2,1)} fusion(s32[4096]{0:T(1024)S(1)} %bitcast.367, f32[512,512]{1,0:T(8,128)S(1)} %convert_element_type.235, f32[4096]{0:T(1024)S(1)} %div.143, bf16[]{:T(256)} %constant.96.clone.1), kind=kCustom, calls=%fused_computation.51 | custom fusion | flops 4194304 | bytes 7356418 | tf_op jit(solution)/shard_map/scatter | solution.py:147
  230.9 75.2 %all_to_all.20 = bf16[8,2,384,512]{3,2,1,0:T(8,128)(2,1)S(1)} all-to-all(bf16[8,2,384,512]{3,2,1,0:T(8,128)(2,1)} %bitcast.357), channel_id=1, replica_groups=mesh['expert'=8,'tensor'=4] {'expert'}, dimensions={0} | all-to-all | bytes 12582912 | tf_op jit(solution)/shard_map/all_to_all | solution.py:189
  309.6 45.0 %gather_fusion = bf16[4096,2048]{1,0:T(8,128)(2,1)} fusion(bf16[512,2048]{1,0:T(8,128)(2,1)} %copy-done.2, s32[4096]{0:T(1024)S(1)} %broadcast_clamp_fusion.1), kind=kCustom, calls=%fused_computation | custom fusion | bytes 33570816 | tf_op jit(solution)/shard_map/gather | solution.py:151
  354.5 38.3 %scatter_custom_fusion = bf16[6144,2048]{1,0:T(8,128)(2,1)} fusion(s32[4096]{0:T(1024)S(1)} %bitcast.368, bf16[4096,2048]{1,0:T(8,128)(2,1)} %gather_fusion, bf16[]{:T(256)} %constant.96.clone.1), kind=kCustom, calls=%fused_computation.12 | custom fusion | bytes 25166336 | tf_op jit(solution)/shard_map/scatter | solution.py:147
  392.8 283.2 %all_to_all.21 = bf16[8,2,384,2048]{3,2,1,0:T(8,128)(2,1)} all-to-all(bf16[8,2,384,2048]{3,2,1,0:T(8,128)(2,1)} %bitcast.353), channel_id=1, replica_groups=mesh['expert'=8,'tensor'=4] {'expert'}, dimensions={0} | all-to-all | bytes 50331648 | tf_op jit(solution)/shard_map/all_to_all | solution.py:150
  676.0 15.1 fusion.1
  691.0 14.6 fusion.3
  705.6 26.4 %all-gather.5.cloned.1.call-done = bf16[8,2,384,2048]{3,2,0,1:T(8,128)(2,1)} async-done(((bf16[8,2,384,512]{3,2,0,1:T(8,128)(2,1)}), bf16[8,2,384,2048]{3,2,0,1:T(8,128)(2,1)}) %all-gather.5.cloned.1.call-update) | async-done | bytes 25165840 | tf_op jit(solution)/shard_map/all_gather | solution.py:192
  732.0 18.7 fusion.16
  750.7 21.2 fusion.39
  771.9 27.2 %fusion = bf16[8,2,384,2048]{3,2,0,1:T(8,128)(2,1)} fusion(f32[2,8,384,2048]{3,2,1,0:T(8,128)} %fusion.39, bf16[8,2,384,192]{2,3,0,1:T(8,128)(2,1)} %get-tuple-element.32, bf16[2,2048,192]{1,2,0:T(8,128)(2,1)} %param.29), kind=kOutput, calls=%fused_computation.6 | convolution fusion | flops 4857004032 | bytes 79429632 | tf_op jit(solution)/shard_map/secf,edf->secd/dot_general | solution.py:207
  799.2 13.6 convert_bitcast_fusion
  812.8 399.0 %reduce-scatter.10.cloned.1.call-done = bf16[8,2,384,512]{3,2,0,1:T(8,128)(2,1)} async-done(((bf16[8,2,384,2048]{3,2,0,1:T(8,128)(2,1)}), bf16[8,2,384,512]{3,2,0,1:T(8,128)(2,1)}) %reduce-scatter.10.cloned.1.call-update) | async-done | bytes 6291472 | tf_op jit(solution)/shard_map/reduce_scatter | solution.py:210
  1222.8 407.6 %reduce-scatter.8.cloned.1.call-done = bf16[8,2,384,512]{3,2,0,1:T(8,128)(2,1)} async-done(((bf16[8,2,384,2048]{3,2,0,1:T(8,128)(2,1)}), bf16[8,2,384,512]{3,2,0,1:T(8,128)(2,1)}) %reduce-scatter.8.cloned.1.call-update) | async-done | bytes 6291472 | tf_op jit(solution)/shard_map/reduce_scatter | solution.py:162
  1641.1 9.1 bitcast_convert_fusion
  1650.2 22.7 %gather_fusion.2 = f32[4096,512]{1,0:T(8,128)} fusion(f32[6144,512]{1,0:T(8,128)} %bitcast_convert_fusion, s32[4096]{0:T(1024)S(1)} %broadcast_clamp_fusion), kind=kCustom, calls=%fused_computation.2 | custom fusion | bytes 16793600 | tf_op jit(solution)/shard_map/gather | solution.py:223
  1673.0 30.5 %fusion.119 = (f32[512,1,512]{2,1,0:T(1,128)S(1)}, f32[512,1,512]{2,1,0:T(1,128)S(1)}, f32[512,1,512]{2,1,0:T(1,128)}, f32[512,1,512]{2,1,0:T(1,128)}, f32[512,1...) fusion(f32[512,8,512]{2,1,0:T(8,128)} %bitcast.355), kind=kLoop, calls=%fused_computation.254 | loop fusion | bytes 16777216 | tf_op jit(solution)/shard_map/slice | solution.py:226
  1712.7 9.1 bitcast_convert_fusion.1
  1721.8 22.6 %gather_fusion.1 = f32[4096,512]{1,0:T(8,128)} fusion(f32[6144,512]{1,0:T(8,128)} %bitcast_convert_fusion.1, s32[4096]{0:T(1024)S(1)} %broadcast_clamp_fusion), kind=kCustom, calls=%fused_computation.1 | custom fusion | bytes 16793600 | tf_op jit(solution)/shard_map/gather | solution.py:175
  1748.8 15.1 all_gather.14
  1773.1 29.5 %all-gather.7.cloned.1.call-done = bf16[512,2048]{1,0:T(8,128)(2,1)} async-done(((bf16[512,512]{1,0:T(8,128)(2,1)}), bf16[512,2048]{1,0:T(8,128)(2,1)}) %all-gather.7.cloned.1.call-update) | async-done | bytes 2097168 | tf_op jit(solution)/shard_map/all_gather | solution.py:234
  1873.1 13.1 convolution_bitcast_fusion
  1890.9 13.2 convolution_bitcast_fusion.2
  1904.0 12.8 convolution_bitcast_fusion.1
  1916.8 31.0 %fusion.120 = (f32[512,1,512]{2,1,0:T(1,128)S(1)}, f32[512,1,512]{2,1,0:T(1,128)S(1)}, f32[512,1,512]{2,1,0:T(1,128)}, f32[512,1,512]{2,1,0:T(1,128)}, f32[512,1...) fusion(f32[512,8,512]{2,1,0:T(8,128)} %bitcast.354), kind=kLoop, calls=%fused_computation.255 | loop fusion | bytes 16777216 | tf_op jit(solution)/shard_map/slice | solution.py:178
  1955.8 18.7 all-reduce.15.cloned.1.call-done
  1980.5 14.1 all-reduce.8
  1994.8 15.7 reduce-scatter.16.cloned.1.call-done
  2012.0 11.7 all-reduce.9
  2028.8 36.8 %reduce-scatter.18.cloned.1.call-done = bf16[1024,256]{1,0:T(8,128)(2,1)} async-done(((bf16[1024,2048]{1,0:T(8,128)(2,1)}), bf16[1024,256]{1,0:T(8,128)(2,1)}) %reduce-scatter.18.cloned.1.call-update) | async-done | bytes 524304 | tf_op jit(solution)/shard_map/reduce_scatter | solution.py:327
  2067.7 52.5 %reduce-scatter.12.cloned.1.call-done = bf16[256,1024]{1,0:T(8,128)(2,1)} async-done(((bf16[2048,1024]{1,0:T(8,128)(2,1)}), bf16[256,1024]{1,0:T(8,128)(2,1)}) %reduce-scatter.12.cloned.1.call-update) | async-done | bytes 524304 | tf_op jit(solution)/shard_map/reduce_scatter | solution.py:312
  (341 shorter events, 194.6 us)
Async XLA Ops:
  7.2 724.8 %copy-start = (bf16[2,192,2048]{2,1,0:T(8,128)(2,1)S(1)}, bf16[2,192,2048]{2,1,0:T(8,128)(2,1)}, u32[]{:S(2)}) copy-start(bf16[2,192,2048]{2,1,0:T(8,128)(2,1)} %param.30) | copy-start | bytes 4718596
  7.2 191.0 %all-reduce.13.cloned.1.call-start = ((), (), s32[]{:S(2)}) async-start(), calls=%async_computation.11 | async-start | bytes 8388608 | tf_op jit(solution)/shard_map/psum | solution.py:126
  17.0 14.2 copy-start.56
  40.4 691.6 %all-gather.5.cloned.1.call-start = ((), (), s32[]{:S(2)}) async-start(), calls=%async_computation.13 | async-start | bytes 31457280 | tf_op jit(solution)/shard_map/all_gather | solution.py:192
  47.6 159.8 %copy-start.13 = (f32[512,512]{1,0:T(8,128)}, f32[512,512]{1,0:T(8,128)S(1)}, u32[]{:S(2)}) copy-start(f32[512,512]{1,0:T(8,128)S(1)} %convert_element_type.235) | copy-start | bytes 3145732
  48.0 306.6 %copy-start.62 = (s32[4096,1]{0,1:T(1,128)}, s32[4096,1]{0,1:T(1,128)S(1)}, u32[]{:S(2)}) copy-start(s32[4096,1]{0,1:T(1,128)S(1)} %compare_select_fusion.1) | copy-start | bytes 49156
  48.0 154.3 %copy-start.58 = (f32[2048]{0:T(1024)S(1)}, f32[2048]{0:T(1024)}, u32[]{:S(2)}) copy-start(f32[2048]{0:T(1024)} %param.26) | copy-start | bytes 24580
  207.1 99.0 %copy-start.52 = (f32[512,8]{0,1:T(8,128)}, f32[512,8]{0,1:T(8,128)S(1)}, u32[]{:S(2)}) copy-start(f32[512,8]{0,1:T(8,128)S(1)} %broadcast_divide_fusion) | copy-start | bytes 49156
  309.5 902.4 %reduce-scatter.10.cloned.1.call-start = ((), (), s32[]{:S(2)}) async-start(), calls=%async_computation.14 | async-start | bytes 31457280 | tf_op jit(solution)/shard_map/reduce_scatter | solution.py:210
  676.0 15.1 copy-start.31
  799.2 831.2 %reduce-scatter.8.cloned.1.call-start = ((), (), s32[]{:S(2)}) async-start(), calls=%async_computation.12 | async-start | bytes 31457280 | tf_op jit(solution)/shard_map/reduce_scatter | solution.py:162
  1217.8 418.5 %all-to-all-start.3 = ((bf16[8,2,384,512]{3,2,1,0:T(8,128)(2,1)}), bf16[8,2,384,512]{3,2,1,0:T(8,128)(2,1)}, u32[]{:S(2)}, u32[]{:S(2)}) async-start(bf16[8,2,384,512]{3,2,1,0:T(8,128)(2,1)} %copy.244), calls=%async_computation.5 | async-start | bytes 12582912 | tf_op jit(solution)/shard_map/all_to_all | solution.py:217
  1636.4 76.3 %all-to-all-start.1 = ((bf16[8,2,384,512]{3,2,1,0:T(8,128)(2,1)}), bf16[8,2,384,512]{3,2,1,0:T(8,128)(2,1)}, u32[]{:S(2)}, u32[]{:S(2)}) async-start(bf16[8,2,384,512]{3,2,1,0:T(8,128)(2,1)} %copy.233), calls=%async_computation.2 | async-start | bytes 12582912 | tf_op jit(solution)/shard_map/all_to_all | solution.py:169
  1641.1 125.8 %all-gather.9.cloned.1.call-start = ((), (), s32[]{:S(2)}) async-start(), calls=%async_computation.22 | async-start | bytes 2621440 | tf_op jit(solution)/shard_map/all_gather | solution.py:228
  1707.9 94.7 %all-gather.7.cloned.1.call-start = ((), (), s32[]{:S(2)}) async-start(), calls=%async_computation.15 | async-start | bytes 2621440 | tf_op jit(solution)/shard_map/all_gather | solution.py:234
  1708.5 244.4 %reduce-scatter.20.cloned.1.call-start = ((), (), s32[]{:S(2)}) async-start(), calls=%async_computation.21 | async-start | bytes 73728 | tf_op jit(solution)/shard_map/reduce_scatter | solution.py:333
  1721.8 22.6 %copy-start.14 = (f32[512,512]{1,0:T(8,128)S(1)}, f32[512,512]{1,0:T(8,128)}, u32[]{:S(2)}) copy-start(f32[512,512]{1,0:T(8,128)} %copy-done.13) | copy-start | bytes 3145732
  1744.4 19.5 copy-start.55
  1744.4 19.5 copy-start.47
  1744.4 19.6 copy-start.34
  1744.4 19.6 copy-start.65
  1744.4 22.5 %copy-start.45 = (bf16[2048,16]{0,1:T(8,128)(2,1)S(1)}, bf16[2048,16]{0,1:T(8,128)(2,1)}, u32[]{:S(2)}) copy-start(bf16[2048,16]{0,1:T(8,128)(2,1)} %param.27) | copy-start | bytes 196612
  1744.5 22.5 %copy-start.59 = (f32[2048]{0:T(1024)S(1)}, f32[2048]{0:T(1024)}, u32[]{:S(2)}) copy-start(f32[2048]{0:T(1024)} %param.26) | copy-start | bytes 24580
  1744.5 22.5 %copy-start.75 = (f32[512]{0:T(512)S(1)}, f32[512]{0:T(512)}, u32[]{:S(2)}) copy-start(f32[512]{0:T(512)} %copy-done.74) | copy-start | bytes 6148
  1766.8 187.4 %reduce-scatter.14.cloned.1.call-start = ((), (), s32[]{:S(2)}) async-start(), calls=%async_computation.18 | async-start | bytes 589824 | tf_op jit(solution)/shard_map/reduce_scatter | solution.py:315
  1852.4 122.1 %all-reduce.15.cloned.1.call-start = ((), (), s32[]{:S(2)}) async-start(), calls=%async_computation.16 | async-start | bytes 4194304 | tf_op jit(solution)/shard_map/psum | solution.py:302
  1856.7 153.8 %reduce-scatter.16.cloned.1.call-start = ((), (), s32[]{:S(2)}) async-start(), calls=%async_computation.19 | async-start | bytes 589824 | tf_op jit(solution)/shard_map/reduce_scatter | solution.py:318
  1860.3 205.3 %reduce-scatter.18.cloned.1.call-start = ((), (), s32[]{:S(2)}) async-start(), calls=%async_computation.20 | async-start | bytes 4718592 | tf_op jit(solution)/shard_map/reduce_scatter | solution.py:327
  1866.9 253.2 %reduce-scatter.12.cloned.1.call-start = ((), (), s32[]{:S(2)}) async-start(), calls=%async_computation.17 | async-start | bytes 4718592 | tf_op jit(solution)/shard_map/reduce_scatter | solution.py:312
  1890.8 13.2 copy-start.20
  1955.8 69.6 %copy-start.77 = (f32[512]{0:T(512)S(1)}, f32[512]{0:T(512)}, u32[]{:S(2)}) copy-start(f32[512]{0:T(512)} %copy-done.76) | copy-start | bytes 6148
  1974.4 147.9 %copy-start.1 = (bf16[2,192,2048]{2,1,0:T(8,128)(2,1)S(1)}, bf16[2,192,2048]{2,1,0:T(8,128)(2,1)}, u32[]{:S(2)}) copy-start(bf16[2,192,2048]{2,1,0:T(8,128)(2,1)} %param.30) | copy-start | bytes 4718596
  (78 other events, 344.3 us)
Sparse Core Ops, SparseCore 0:
  40.5 157.6 all-reduce.12
  309.6 422.3 all-gather.4
  799.3 412.5 reduce-scatter.9
  1214.1 416.1 reduce-scatter.7
  1708.1 48.3 all-gather.8
  1758.0 44.5 all-gather.6
  1805.9 30.1 reduce-scatter.19
  1852.5 32.8 reduce-scatter.13
  1887.9 86.5 all-reduce.14
  1977.4 33.0 reduce-scatter.15
  2014.2 51.3 reduce-scatter.17
  2068.8 51.3 reduce-scatter.11
where the time goes:
time: 2140 us; the launch traced here: 2130 us
  waiting for transfers between devices  1140 us (53%)
  blocking collectives  399 us (19%)
  local copies, waits for them, and re-layouts  234 us (11%)
  matrix products  210 us (10%)
  other arithmetic  117 us (5%)
    reduce_scatter x1, waiting for transfers between devices, per_device(): lax.psum_scatter(partial_low.astype(jnp.float32).astype(jnp.bfloat16), 't...  408 us
    reduce_scatter x1, waiting for transfers between devices, per_device(): lax.psum_scatter(input_low.astype(jnp.float32).astype(jnp.bfloat16), 'ten...  399 us
    all_to_all x1, blocking collectives, per_device(): lax.all_to_all(fill_slots(hidden_two[token_of]), 'expert', split_axis=0,...  283 us
    psum x1, waiting for transfers between devices, per_device(): lax.psum(jnp.dot(attended_low, w_out, preferred_element_type=jnp.float32)...  150 us
    all_to_all x1, blocking collectives, per_device(): lax.all_to_all(fill_slots(grad_rows), 'expert', split_axis=0, concat_axis...  75.2 us
    reduce_scatter x1, waiting for transfers between devices, per_device(): lax.psum_scatter(query_weight_grad.astype(jnp.bfloat16), 'expert', scatte...  52.5 us
    gather x1, local copies, waits for them, and re-layouts, per_device(): hidden_two[token_of]  45 us
  transfers between devices with their start and end apart: 14, of which 10 were waited for; matrix products, arithmetic and copies ran while one was open for 20% of the time, Pallas kernels for 0%

commit v1 on v0

v1 whole, which is shorter than its diff:
```python
import functools

import jax
import jax.numpy as jnp
from jax import lax
from jax.experimental import pallas as pl
from jax.experimental.pallas import tpu as pltpu
from jax.sharding import PartitionSpec as P


def rms_norm(values, gain_vec):
    return values * lax.rsqrt(jnp.mean(values * values, axis=-1, keepdims=True) + 1e-06) * gain_vec


def rotate(values, cos_table, sine_table):
    half_dim = values.shape[-1] // 2
    first_half = values[..., :half_dim]
    second = values[..., half_dim:]
    return jnp.concatenate(
        [
            first_half * cos_table - second * sine_table,
            second * cos_table + first_half * sine_table,
        ],
        axis=-1,
    )


def rope_tables(positions, head_dim):
    half_dim = head_dim // 2
    frequency = jnp.power(1000000.0, -2.0 * jnp.arange(half_dim).astype(jnp.float32) / head_dim)
    angles = positions.astype(jnp.float32)[:, None] * frequency[None, :]
    return (jnp.cos(angles)[:, None, :], jnp.sin(angles)[:, None, :])


def seq_positions(sequence_numbers, block_len):
    total_len = sequence_numbers.shape[0]
    places = jnp.arange(total_len)
    previous = jnp.concatenate([sequence_numbers[:1] - 1, sequence_numbers[:-1]])
    starts = (places % block_len == 0) | (sequence_numbers != previous)
    first_place = lax.cummax(jnp.where(starts, places, 0), axis=0)
    return places - first_place


F32 = jnp.float32
B16 = jnp.bfloat16


def swap(values, axis, mask):
    count = lax.axis_size(axis)
    return lax.ppermute(values, axis, [(i, i ^ mask) for i in range(count)])


def bits_of(axis):
    return lax.axis_size(axis).bit_length() - 1


def gather_blocks(block, axis, dim):
    count = lax.axis_size(axis)
    me = lax.axis_index(axis)
    held = [(0, block)]
    for bit in reversed(range(bits_of(axis))):
        mask = 1 << bit
        held = held + [(d ^ mask, swap(v, axis, mask)) for d, v in held]
    size = block.shape[dim]
    shape = list(block.shape)
    shape[dim] = size * count
    whole = jnp.zeros(shape, block.dtype)
    for d, v in held:
        whole = lax.dynamic_update_slice_in_dim(whole, v, (me ^ d) * size, dim)
    return whole


def scatter_sum(pick, axis):
    count = lax.axis_size(axis)
    me = lax.axis_index(axis)
    held = {d: pick(me ^ d) for d in range(count)}
    for bit in range(bits_of(axis)):
        mask = 1 << bit
        keep = {d: v for d, v in held.items() if not d & mask}
        for d in keep:
            came = swap(held[d ^ mask].astype(B16), axis, mask)
            keep[d] = keep[d] + came.astype(F32)
        held = keep
    return held[0]


def swap_columns(rows, axis):
    count = lax.axis_size(axis)
    me = lax.axis_index(axis)
    height, width = rows.shape[0], rows.shape[1] // count
    whole = jnp.zeros((height * count, width), rows.dtype)
    for d in range(count):
        piece = lax.dynamic_slice_in_dim(rows, (me ^ d) * width, width, 1)
        if d:
            piece = swap(piece, axis, d)
        whole = lax.dynamic_update_slice_in_dim(whole, piece, (me ^ d) * height, 0)
    return whole


def sum_everywhere(values, axis):
    for bit in range(bits_of(axis)):
        values = values + swap(values, axis, 1 << bit)
    return values


def nt_dot(left, right):
    return lax.dot_general(left, right, (((1,), (1,)), ((), ())), preferred_element_type=F32)


def tn_dot(left, right):
    return lax.dot_general(left, right, (((0,), (0,)), ((), ())), preferred_element_type=F32)


def expert_kernel(
    row_tile, hidden, experts,
    ids_ref, packed_ref, dy_ref, gate_up_ref, down_ref,
    back_ref, dgu_ref, act_ref, total, route_total,
):
    step = pl.program_id(0)
    rows, width = dy_ref.shape
    pair = 2 * hidden
    extra = packed_ref.shape[1] - width

    @pl.when(step == 0)
    def _():
        total[...] = jnp.zeros_like(total)
        route_total[...] = jnp.zeros_like(route_total)

    gate_up = gate_up_ref[0]
    down = down_ref[0]
    id_a = ids_ref[2 * step]
    id_b = ids_ref[2 * step + 1]
    for tile in range(rows // row_tile):
        at = pl.ds(tile * row_tile, row_tile)
        both = nt_dot(packed_ref[at, :width], gate_up)
        gate, up = both[:, :pair], both[:, pair:]
        shares = packed_ref[at, width:].astype(F32)
        lane = lax.broadcasted_iota(jnp.int32, (row_tile, extra), 1)

        def share_of(expert):
            mine = (lane == expert) | (lane == expert + experts)
            return jnp.sum(jnp.where(mine, shares, 0.0), axis=1, keepdims=True)

        hidden_lane = lax.broadcasted_iota(jnp.int32, (row_tile, pair), 1)
        first = hidden_lane < hidden
        share = jnp.where(first, share_of(id_a), share_of(id_b))
        sig = 1.0 / (1.0 + jnp.exp(-gate))
        silu = gate * sig
        act = (silu * up).astype(B16).astype(F32)
        raw = nt_dot(dy_ref[at, :], down)
        product = act * raw
        part_a = jnp.sum(jnp.where(first, product, 0.0), axis=1, keepdims=True)
        part_b = jnp.sum(jnp.where(first, 0.0, product), axis=1, keepdims=True)
        route_total[at, :] += jnp.where(lane == id_a, part_a, 0.0) + jnp.where(
            lane == id_b, part_b, 0.0
        )
        dact = share * raw
        dgate = dact * up * (sig * (1.0 + gate * (1.0 - sig)))
        dup = dact * silu
        dgu = jnp.concatenate([dgate.astype(B16), dup.astype(B16)], axis=1)
        dgu_ref[0, at, :] = dgu
        act_ref[0, at, :] = (share * act).astype(B16)
        total[at, :] += jnp.dot(dgu, gate_up, preferred_element_type=F32)

    @pl.when(step == pl.num_programs(0) - 1)
    def _():
        back_ref[:, :width] = total[...].astype(B16)
        back_ref[:, width:] = route_total[...].astype(B16)


def expert_pass(ids, packed, dy, gate_up, down, experts):
    rows, full = packed.shape
    width = dy.shape[1]
    groups, pair2, _ = gate_up.shape
    pair = pair2 // 2
    return pl.pallas_call(
        functools.partial(expert_kernel, min(rows, 256), pair // 2, experts),
        grid_spec=pltpu.PrefetchScalarGridSpec(
            num_scalar_prefetch=1,
            grid=(groups,),
            in_specs=[
                pl.BlockSpec((rows, full), lambda d, ids: (0, 0)),
                pl.BlockSpec((rows, width), lambda d, ids: (0, 0)),
                pl.BlockSpec((1, pair2, width), lambda d, ids: (d, 0, 0)),
                pl.BlockSpec((1, pair, width), lambda d, ids: (d, 0, 0)),
            ],
            out_specs=[
                pl.BlockSpec((rows, full), lambda d, ids: (0, 0)),
                pl.BlockSpec((1, rows, pair2), lambda d, ids: (d, 0, 0)),
                pl.BlockSpec((1, rows, pair), lambda d, ids: (d, 0, 0)),
            ],
            scratch_shapes=[
                pltpu.VMEM((rows, width), F32),
                pltpu.VMEM((rows, full - width), F32),
            ],
        ),
        out_shape=[
            jax.ShapeDtypeStruct((rows, full), B16),
            jax.ShapeDtypeStruct((groups, rows, pair2), B16),
            jax.ShapeDtypeStruct((groups, rows, pair), B16),
        ],
        compiler_params=pltpu.CompilerParams(vmem_limit_bytes=56 << 20),
        cost_estimate=pl.CostEstimate(
            flops=2 * rows * width * groups * (2 * pair2 + pair),
            bytes_accessed=2 * (groups * (pair2 + pair) * (width + rows) + 4 * rows * width),
            transcendentals=rows * groups * pair,
        ),
    )(ids, packed, dy, gate_up, down)


def per_device(
    tokens,
    sequence_numbers,
    routes,
    attn_gain,
    w_query,
    key_projection,
    value_projection,
    query_gain,
    key_gain,
    w_out,
    moe_gain,
    w_router,
    w_gate,
    w_up,
    w_down,
    cotangent,
):
    tok_count, model_width = tokens.shape
    head_dim = query_gain.shape[0]
    q_heads = w_query.shape[1] // head_dim
    kv_heads = key_projection.shape[1] // head_dim
    group_size = q_heads // kv_heads
    tensor_size = lax.axis_size("tensor")
    tensor_pos = lax.axis_index("tensor")
    expert_size = lax.axis_size("expert")
    expert_pos = lax.axis_index("expert")
    local_experts = w_gate.shape[0]
    experts = local_experts * expert_size
    hidden = w_gate.shape[2]
    pair = local_experts * hidden
    score_scale = head_dim ** (-0.5)
    own_rows = tok_count // tensor_size
    row_start = tensor_pos * own_rows
    group = 2 << ((expert_size // 2).bit_length() // 2)
    rounds = expert_size // group

    def own(values):
        return lax.dynamic_slice_in_dim(values, row_start, own_rows, 0)

    gate_up_own = jnp.concatenate(
        [
            jnp.swapaxes(w_gate, 1, 2).reshape(pair, model_width),
            jnp.swapaxes(w_up, 1, 2).reshape(pair, model_width),
        ],
        axis=0,
    )
    weights_held = [(gate_up_own, w_down.reshape(pair, model_width))]
    mask = group // 2
    while mask:
        pass_on = [(swap(a, "expert", mask), swap(b, "expert", mask)) for a, b in weights_held]
        weights_held = [v for both in zip(weights_held, pass_on) for v in both]
        mask //= 2
    gate_up = jnp.stack([a for a, _ in weights_held])
    down = jnp.stack([b for _, b in weights_held])
    ids = jnp.concatenate(
        [(expert_pos ^ d) * local_experts + jnp.arange(local_experts) for d in range(group)]
    ).astype(jnp.int32)
    dy_own = gather_blocks(cotangent, "tensor", 1)
    dy_of = [dy_own] + [swap(dy_own, "expert", group * r) for r in range(1, rounds)]

    positions = seq_positions(sequence_numbers, tok_count)
    cos_table, sine_table = rope_tables(positions, head_dim)
    local_index = jnp.arange(tok_count)
    inputs = tokens.astype(F32)
    first_hidden = rms_norm(inputs, attn_gain).astype(B16)
    query_rows = jnp.dot(first_hidden, w_query, preferred_element_type=F32).reshape(
        tok_count, q_heads, head_dim
    )
    key_matrix = jnp.dot(first_hidden, key_projection, preferred_element_type=F32).reshape(
        tok_count, kv_heads, head_dim
    )
    value_matrix = (
        jnp.dot(first_hidden, value_projection, preferred_element_type=F32)
        .astype(B16)
        .reshape(tok_count, kv_heads, head_dim)
    )

    def prepare(values, gain_vec):
        return rotate(rms_norm(values, gain_vec), cos_table, sine_table)

    query_rot, pull_query = jax.vjp(prepare, query_rows, query_gain)
    key_rot, pull_key = jax.vjp(prepare, key_matrix, key_gain)
    query_low = query_rot.astype(B16).reshape(tok_count, kv_heads, group_size, head_dim)
    key_low = key_rot.astype(B16)

    def block_scores():
        scores = (
            jnp.einsum("qhgd,khd->hgqk", query_low, key_low, preferred_element_type=F32)
            * score_scale
        )
        allowed = (sequence_numbers[:, None] == sequence_numbers[None, :]) & (
            local_index[:, None] >= local_index[None, :]
        )
        return jnp.where(allowed, scores, -1e30)

    scores = block_scores()
    row_peak = jnp.max(scores, axis=-1, keepdims=True)
    exp_scores = jnp.exp(scores - row_peak)
    row_total = jnp.sum(exp_scores, axis=-1, keepdims=True)
    probabilities = exp_scores / row_total
    log_totals = row_peak + jnp.log(row_total)
    outputs = jnp.einsum(
        "hgqk,khd->qhgd", probabilities.astype(B16), value_matrix, preferred_element_type=F32
    )
    attended_low = outputs.reshape(tok_count, q_heads * head_dim).astype(B16)
    branch_part = jnp.dot(attended_low, w_out, preferred_element_type=F32).astype(B16)
    branch = scatter_sum(
        lambda z: lax.dynamic_slice_in_dim(branch_part, z * own_rows, own_rows, 0).astype(F32),
        "tensor",
    )
    middle = own(inputs) + branch
    normed_two, pull_two = jax.vjp(rms_norm, middle, moe_gain)
    hidden_rows = normed_two.astype(B16)
    logits = jnp.dot(hidden_rows, w_router, preferred_element_type=F32)
    expert_ids = jnp.arange(experts)
    picked = (own(routes)[:, :, None] == expert_ids[None, None, :]).astype(F32)

    def route_weights(logit_vals):
        probabilities = jax.nn.softmax(logit_vals, axis=-1)
        chosen = jnp.sum(picked * probabilities[:, None, :], axis=-1)
        return chosen / jnp.sum(chosen, axis=-1, keepdims=True)

    weights, pull_router = jax.vjp(route_weights, logits)
    combine = jnp.sum(picked * weights[:, :, None], axis=1)
    high = combine.astype(B16)
    low = (combine - high.astype(F32)).astype(B16)
    spare = -(2 * experts) % 128
    packed_rows = jnp.concatenate(
        [hidden_rows, high, low, jnp.zeros((own_rows, spare), B16)], axis=1
    )
    packed_own = gather_blocks(packed_rows, "tensor", 0)
    packed_of = [packed_own] + [swap(packed_own, "expert", group * r) for r in range(1, rounds)]

    passes = [expert_pass(ids, p, d, gate_up, down, experts) for p, d in zip(packed_of, dy_of)]
    backs = [passes[0][0]] + [swap(passes[r][0], "expert", group * r) for r in range(1, rounds)]

    def sum_rows(parts, z):
        pieces = [
            lax.dynamic_slice_in_dim(p, z * own_rows, own_rows, 0).astype(F32) for p in parts
        ]
        return functools.reduce(jnp.add, pieces)

    back = scatter_sum(lambda z: sum_rows(backs, z), "tensor")

    out_parts = []
    for _, _, act in passes:
        terms = [
            jnp.dot(act[d], down[d], preferred_element_type=F32) for d in range(group)
        ]
        out_parts.append(functools.reduce(jnp.add, terms).astype(B16))
    out_parts = out_parts[:1] + [
        swap(out_parts[r], "expert", group * r) for r in range(1, rounds)
    ]
    mixed = scatter_sum(lambda z: sum_rows(out_parts, z), "tensor")
    block_out = swap_columns((middle + mixed).astype(B16), "tensor")

    held = {}
    for d in reversed(range(group)):
        gu = [tn_dot(p[1][d], packed[:, :model_width]) for p, packed in zip(passes, packed_of)]
        dn = [tn_dot(p[2][d], dy) for p, dy in zip(passes, dy_of)]
        held[d] = (functools.reduce(jnp.add, gu), functools.reduce(jnp.add, dn))
    mask = 1
    while mask < group:
        keep = {}
        for d in sorted(held):
            if d & mask:
                continue
            keep[d] = tuple(
                mine + swap(theirs.astype(B16), "expert", mask).astype(F32)
                for mine, theirs in zip(held[d], held[d ^ mask])
            )
        held = keep
        mask *= 2
    gate_up_grad, down_grad_flat = held[0]
    shape = (local_experts, hidden, model_width)
    gate_grad = jnp.swapaxes(gate_up_grad[:pair].reshape(shape), 1, 2)
    up_grad = jnp.swapaxes(gate_up_grad[pair:].reshape(shape), 1, 2)
    down_grad = down_grad_flat.reshape(shape)

    hidden_grad = back[:, :model_width]
    combine_grad = back[:, model_width : model_width + experts]
    weight_grad = jnp.sum(picked * combine_grad[:, None, :], axis=-1)
    (logit_grad,) = pull_router(weight_grad)
    logit_low = logit_grad.astype(B16)
    router_grad = tn_dot(logit_low, hidden_rows)
    hidden_grad = hidden_grad + nt_dot(logit_low, w_router)
    middle_norm_grad, moe_gain_grad = pull_two(hidden_grad)
    middle_grad = middle_norm_grad + own(dy_own).astype(F32)
    branch_low = gather_blocks(middle_grad.astype(B16), "tensor", 0)

    out_weight_grad = tn_dot(attended_low, branch_low)
    attended_grad = (
        nt_dot(branch_low, w_out).astype(B16).reshape(tok_count, kv_heads, group_size, head_dim)
    )
    scores = block_scores()
    probabilities = jnp.exp(scores - log_totals)
    prob_grad = jnp.einsum(
        "qhgd,khd->hgqk", attended_grad, value_matrix, preferred_element_type=F32
    )
    row_delta = jnp.sum(probabilities * prob_grad, axis=-1, keepdims=True)
    score_low = (probabilities * (prob_grad - row_delta)).astype(B16)
    query_grads = (
        jnp.einsum("hgqk,khd->qhgd", score_low, key_low, preferred_element_type=F32) * score_scale
    )
    key_grad = (
        jnp.einsum("hgqk,qhgd->khd", score_low, query_low, preferred_element_type=F32)
        * score_scale
    )
    value_grad = jnp.einsum(
        "hgqk,qhgd->khd", probabilities.astype(B16), attended_grad, preferred_element_type=F32
    )
    query_pre_grad, query_gain_part = pull_query(query_grads.reshape(tok_count, q_heads, head_dim))
    key_pre_grad, key_gain_part = pull_key(key_grad)
    query_grad_low = query_pre_grad.reshape(tok_count, q_heads * head_dim).astype(B16)
    key_grad_low = key_pre_grad.reshape(tok_count, kv_heads * head_dim).astype(B16)
    value_grad_low = value_grad.reshape(tok_count, kv_heads * head_dim).astype(B16)

    hidden_one = nt_dot(query_grad_low, w_query)
    hidden_one = hidden_one + nt_dot(key_grad_low, key_projection)
    hidden_one = hidden_one + nt_dot(value_grad_low, value_projection)
    scale = lax.rsqrt(jnp.mean(inputs * inputs, axis=-1, keepdims=True) + 1e-06)
    gained = hidden_one * attn_gain
    along_part = jnp.sum(gained * inputs, axis=-1)
    attn_gain_part = jnp.sum(hidden_one * (inputs * scale), axis=0)
    along = sum_everywhere(along_part, "tensor")
    hidden_one_low = hidden_one.astype(B16)
    width = model_width // tensor_size

    def columns(values, z):
        return lax.dynamic_slice_in_dim(values, z * width, width, values.ndim - 1)

    hidden_one_cols = scatter_sum(lambda z: columns(hidden_one_low, z).astype(F32), "tensor")
    gain_cols = columns(attn_gain, tensor_pos)
    input_cols = columns(inputs, tensor_pos)
    input_grad = columns(branch_low, tensor_pos).astype(F32) + scale * (
        hidden_one_cols * gain_cols
        - input_cols * (scale * scale * (along / model_width)[:, None])
    )
    query_weight_grad = tn_dot(first_hidden, query_grad_low)
    key_weight_grad = tn_dot(first_hidden, key_grad_low)
    value_weight_grad = tn_dot(first_hidden, value_grad_low)

    def over_experts(values, dim):
        return lax.psum_scatter(
            values.astype(B16), "expert", scatter_dimension=dim, tiled=True
        ).astype(F32)

    def share_of_sum(values):
        total = sum_everywhere(sum_everywhere(values, "tensor"), "expert")
        size = total.shape[-1] // expert_size
        return lax.dynamic_slice_in_dim(total, expert_pos * size, size, total.ndim - 1)

    router_and_gain = share_of_sum(jnp.concatenate([router_grad, moe_gain_grad[None]], axis=0))
    attn_gain_grad = share_of_sum(attn_gain_part)
    head_gains = share_of_sum(jnp.stack([query_gain_part, key_gain_part]))
    return (
        block_out,
        input_grad,
        attn_gain_grad,
        over_experts(query_weight_grad, 0),
        over_experts(key_weight_grad, 0),
        over_experts(value_weight_grad, 0),
        head_gains[0],
        head_gains[1],
        over_experts(out_weight_grad, 1),
        router_and_gain[experts],
        jnp.swapaxes(router_and_gain[:experts], 0, 1),
        gate_grad,
        up_grad,
        down_grad,
    )


def solution(mesh):
    placed = (
        P("expert", None),
        P("expert"),
        P("expert", None),
        P(),
        P(None, "tensor"),
        P(None, "tensor"),
        P(None, "tensor"),
        P(),
        P(),
        P("tensor", None),
        P(),
        P(),
        P("expert", None, "tensor"),
        P("expert", None, "tensor"),
        P("expert", "tensor", None),
        P("expert", "tensor"),
    )
    return jax.shard_map(
        per_device,
        mesh=mesh,
        in_specs=placed,
        out_specs=(
            P("expert", "tensor"),
            P("expert", "tensor"),
            P("expert"),
            P("expert", "tensor"),
            P("expert", "tensor"),
            P("expert", "tensor"),
            P("expert"),
            P("expert"),
            P("tensor", "expert"),
            P("expert"),
            P("expert", None),
            P("expert", None, "tensor"),
            P("expert", None, "tensor"),
            P("expert", "tensor", None),
        ),
        check_vma=False,
    )
```

time: 2140 us -> 825 us (0.39)
  waiting for transfers between devices: 1140 us -> 421 us
  blocking collectives: 399 us -> 0 us
  local copies, waits for them, and re-layouts: 234 us -> 49.6 us
  matrix products: 210 us -> 116 us
  Pallas kernels: 0 us -> 58.5 us
  starting transfers between devices: 10.1 us -> 44.6 us
    reduce_scatter x7 -> x4, waiting for transfers between devices: 912 us -> 0.01 us  [over_experts(): lax.psum_scatter(values.astype(B16), 'expert', scatter_dimension=dim, til...]
    ppermute x0 -> x57, waiting for transfers between devices: none -> 421 us  [swap(): return lax.ppermute(values, axis, [(i, i ^ mask) for i in range(count)])]
    all_to_all x2 -> x0, blocking collectives: 358 us -> none  [the longest x1 283 us: per_device(): lax.all_to_all(fill_slots(hidden_two[token_of]), 'expert', split_axis=0,...]
    psum x2 -> x0, waiting for transfers between devices: 169 us -> none  [the longest x1 150 us: per_device(): lax.psum(jnp.dot(attended_low, w_out, preferred_element_type=jnp.float32)...]
    dot_general x28 -> x43, matrix products: 206 us -> 111 us  [the longest x21 67.2 us: tn_dot(): lax.dot_general(left, right, (((0,), (0,)), ((), ())), preferred_element_...]
    gather x3 -> x0, local copies, waits for them, and re-layouts: 90.3 us -> none  [the longest x1 45 us: per_device(): hidden_two[token_of]]
    pallas_call x0 -> x2, Pallas kernels: none -> 58.5 us  [expert_pass(): pl.pallas_call(functools.partial(expert_kernel, min(rows, 256), pair // 2...]
    all_gather x3 -> x0, waiting for transfers between devices: 55.9 us -> none  [the longest x1 29.5 us: per_device(): lax.all_gather(cot_part.astype(jnp.bfloat16), 'tensor', axis=1, tiled=True)]
  transfers between devices with their start and end apart: 14 -> 61, of which waited for: 10 -> 31; matrix products, arithmetic and copies ran while one was open for 20% -> 29% of each run, Pallas kernels for 0% -> 4%
where the time goes in v1:
time: 825 us; the launch traced here: 818 us
  waiting for transfers between devices  421 us (51%)
  matrix products  116 us (14%)
  other arithmetic  112 us (14%)
  Pallas kernels  58.5 us (7%)
  local copies, waits for them, and re-layouts  49.6 us (6%)
  starting transfers between devices  44.6 us (5%)
  between operations  16.5 us (2%)
    ppermute x57, waiting for transfers between devices, swap(): return lax.ppermute(values, axis, [(i, i ^ mask) for i in range(count)])  421 us
    dot_general x21, matrix products, tn_dot(): lax.dot_general(left, right, (((0,), (0,)), ((), ())), preferred_element_...  67.2 us
    pallas_call x2, Pallas kernels, expert_pass(): pl.pallas_call(functools.partial(expert_kernel, min(rows, 256), pair // 2...  58.5 us
    ppermute x57, starting transfers between devices, swap(): return lax.ppermute(values, axis, [(i, i ^ mask) for i in range(count)])  44.1 us
    add x2, other arithmetic, per_device(): mine + swap(theirs.astype(B16), 'expert', mask).astype(F32)  17.8 us
    dot_general x8, matrix products, per_device(): jnp.dot(act[d], down[d], preferred_element_type=F32)  16.6 us
  transfers between devices with their start and end apart: 61, of which 31 were waited for; matrix products, arithmetic and copies ran while one was open for 29% of the time, Pallas kernels for 4%

profile of v1, /device:TPU:0, one launch (start us, length us, event | category | flops | bytes accessed | tf_op | source)
XLA Modules:
  0.0 818.3 jit_solution(1102146857274366256)
XLA Ops:
  57.5 9.9 %collective-permute-done.1 = bf16[128,2048]{1,0:T(8,128)(2,1)S(1)} collective-permute-done((bf16[128,2048]{1,0:T(8,128)(2,1)}, bf16[128,2048]{1,0:T(8,128)(2,1)S(1)}, u32[]{:S(2)}, u32[]{:S(2)}) %collective-permute-start.1) | collective-permute-done | bytes 524320 | tf_op jit(solution)/shard_map/ppermute | solution.py:50
  73.6 26.8 %collective-permute-done = bf16[128,2048]{1,0:T(8,128)(2,1)} collective-permute-done((bf16[128,2048]{1,0:T(8,128)(2,1)}, bf16[128,2048]{1,0:T(8,128)(2,1)}, u32[]{:S(2)}, u32[]{:S(2)}) %collective-permute-start) | collective-permute-done | bytes 524320 | tf_op jit(solution)/shard_map/ppermute | solution.py:50
  111.8 12.5 %collective-permute-done.10 = bf16[768,2048]{1,0:T(8,128)(2,1)} collective-permute-done((bf16[768,2048]{1,0:T(8,128)(2,1)}, bf16[768,2048]{1,0:T(8,128)(2,1)}, u32[]{:S(2)}, u32[]{:S(2)}) %collective-permute-start.10) | collective-permute-done | bytes 3145760 | tf_op jit(solution)/shard_map/ppermute | solution.py:50
  134.3 21.4 %collective-permute-done.13 = bf16[384,2048]{1,0:T(8,128)(2,1)} collective-permute-done((bf16[384,2048]{1,0:T(8,128)(2,1)}, bf16[384,2048]{1,0:T(8,128)(2,1)}, u32[]{:S(2)}, u32[]{:S(2)}) %collective-permute-start.13) | collective-permute-done | bytes 1572896 | tf_op jit(solution)/shard_map/ppermute | solution.py:50
  158.4 10.1 %collective-permute-done.4 = bf16[128,2176]{1,0:T(8,128)(2,1)S(1)} collective-permute-done((bf16[128,2176]{1,0:T(8,128)(2,1)}, bf16[128,2176]{1,0:T(8,128)(2,1)S(1)}, u32[]{:S(2)}, u32[]{:S(2)}) %collective-permute-start.4) | collective-permute-done | bytes 557088 | tf_op jit(solution)/shard_map/ppermute | solution.py:50
  170.2 10.0 %collective-permute-done.5 = bf16[128,2176]{1,0:T(8,128)(2,1)S(1)} collective-permute-done((bf16[128,2176]{1,0:T(8,128)(2,1)}, bf16[128,2176]{1,0:T(8,128)(2,1)S(1)}, u32[]{:S(2)}, u32[]{:S(2)}) %collective-permute-start.5) | collective-permute-done | bytes 557088 | tf_op jit(solution)/shard_map/ppermute | solution.py:50
  182.4 6.7 pad_maximum_fusion.1.down_ref
  189.1 9.5 %pad_maximum_fusion.gate_up_ref = bf16[4,768,2048]{2,1,0:T(8,128)(2,1)} fusion(bf16[1,768,2048]{2,1,0:T(8,128)(2,1)} %bitcast.20, bf16[1,768,2048]{2,1,0:T(8,128)(2,1)} %bitcast.19, bf16[1,768,2048]{2,1,0:T(8,128)(2,1)} %bitcast.18, bf16[1,768,2048]{2,1,0:T(8,128)(2,1)S(1)} %copy-done.26), kind=kLoop, calls=%fused_computation | loop fusion | flops 18874368 | bytes 25165824 | tf_op jit(solution)/shard_map/stack | solution.py:264
  198.6 29.1 %shard_map.263 = (bf16[512,2176]{1,0:T(8,128)(2,1)}, bf16[4,512,768]{2,1,0:T(8,128)(2,1)}, bf16[4,512,384]{2,1,0:T(8,128)(2,1)}) custom-call(s32[8]{0:T(128)} %pad_add_fusion.2.ids_ref, bf16[512,2176]{1,0:T(8,128)(2,1)} %copy-done.4, bf16[512,2048]{1,0:T(8,128)(2,1)} %copy-done.2, bf16[4,768,2048]{2,1,0:T(8,128)(2,1)} %pad_maximum_fusion.gate_up_ref, ...), custom_call_target="tpu_custom_call" | custom-call | flops 16106127360 | bytes 31981568 | tf_op jit(solution)/shard_map/pallas_call | solution.py:176
  228.8 42.8 %collective-permute-done.15.packed_ref = bf16[512,2176]{1,0:T(8,128)(2,1)} collective-permute-done((bf16[512,2176]{1,0:T(8,128)(2,1)S(1)}, bf16[512,2176]{1,0:T(8,128)(2,1)}, u32[]{:S(2)}, u32[]{:S(2)}) %collective-permute-start.15) | collective-permute-done | bytes 2228256 | tf_op jit(solution)/shard_map/ppermute | solution.py:50
  271.6 29.3 %shard_map.264 = (bf16[512,2176]{1,0:T(8,128)(2,1)}, bf16[4,512,768]{2,1,0:T(8,128)(2,1)}, bf16[4,512,384]{2,1,0:T(8,128)(2,1)}) custom-call(s32[8]{0:T(128)} %pad_add_fusion.2.ids_ref, bf16[512,2176]{1,0:T(8,128)(2,1)} %collective-permute-done.15.packed_ref, bf16[512,2048]{1,0:T(8,128)(2,1)} %copy-done.8, ...), custom_call_target="tpu_custom_call" | custom-call | flops 16106127360 | bytes 31981568 | tf_op jit(solution)/shard_map/pallas_call | solution.py:176
  333.6 19.1 %collective-permute-done.24 = bf16[512,2176]{1,0:T(8,128)(2,1)S(1)} collective-permute-done((bf16[512,2176]{1,0:T(8,128)(2,1)}, bf16[512,2176]{1,0:T(8,128)(2,1)S(1)}, u32[]{:S(2)}, u32[]{:S(2)}) %collective-permute-start.24) | collective-permute-done | bytes 2228256 | tf_op jit(solution)/shard_map/ppermute | solution.py:50
  354.7 36.9 %collective-permute-done.17 = bf16[512,2048]{1,0:T(8,128)(2,1)S(1)} collective-permute-done((bf16[512,2048]{1,0:T(8,128)(2,1)S(1)}, bf16[512,2048]{1,0:T(8,128)(2,1)S(1)}, u32[]{:S(2)}, u32[]{:S(2)}) %collective-permute-start.17) | collective-permute-done | bytes 2097184 | tf_op jit(solution)/shard_map/ppermute | solution.py:50
  398.4 17.5 %collective-permute-done.19 = bf16[128,2048]{1,0:T(8,128)(2,1)S(1)} collective-permute-done((bf16[128,2048]{1,0:T(8,128)(2,1)S(1)}, bf16[128,2048]{1,0:T(8,128)(2,1)S(1)}, u32[]{:S(2)}, u32[]{:S(2)}) %collective-permute-start.19) | collective-permute-done | bytes 524320 | tf_op jit(solution)/shard_map/ppermute | solution.py:50
  417.0 12.4 %collective-permute-done.25 = bf16[128,2176]{1,0:T(8,128)(2,1)S(1)} collective-permute-done((bf16[128,2176]{1,0:T(8,128)(2,1)S(1)}, bf16[128,2176]{1,0:T(8,128)(2,1)S(1)}, u32[]{:S(2)}, u32[]{:S(2)}) %collective-permute-start.25) | collective-permute-done | bytes 557088 | tf_op jit(solution)/shard_map/ppermute | solution.py:50
  430.7 12.9 %collective-permute-done.18 = bf16[128,2048]{1,0:T(8,128)(2,1)} collective-permute-done((bf16[128,2048]{1,0:T(8,128)(2,1)}, bf16[128,2048]{1,0:T(8,128)(2,1)}, u32[]{:S(2)}, u32[]{:S(2)}) %collective-permute-start.18) | collective-permute-done | bytes 524320 | tf_op jit(solution)/shard_map/ppermute | solution.py:50
  443.6 7.8 collective-permute-done.20
  464.8 15.7 %collective-permute-done.28 = bf16[128,2048]{1,0:T(8,128)(2,1)S(1)} collective-permute-done((bf16[128,2048]{1,0:T(8,128)(2,1)S(1)}, bf16[128,2048]{1,0:T(8,128)(2,1)S(1)}, u32[]{:S(2)}, u32[]{:S(2)}) %collective-permute-start.28) | collective-permute-done | bytes 524320 | tf_op jit(solution)/shard_map/ppermute | solution.py:50
  482.7 6.3 collective-permute-done.29
  489.1 10.8 %collective-permute-done.30 = bf16[128,2048]{1,0:T(8,128)(2,1)S(1)} collective-permute-done((bf16[128,2048]{1,0:T(8,128)(2,1)S(1)}, bf16[128,2048]{1,0:T(8,128)(2,1)S(1)}, u32[]{:S(2)}, u32[]{:S(2)}) %collective-permute-start.30) | collective-permute-done | bytes 524320 | tf_op jit(solution)/shard_map/ppermute | solution.py:50
  516.4 8.1 copy.134
  547.9 6.4 convolution_convert_fusion.1
  570.5 6.0 fusion.17
  576.6 6.2 fusion.21
  590.4 7.5 add_convert_fusion
  608.6 17.5 %collective-permute-done.56 = bf16[384,2048]{1,0:T(8,128)(2,1)S(1)} collective-permute-done((bf16[384,2048]{1,0:T(8,128)(2,1)}, bf16[384,2048]{1,0:T(8,128)(2,1)S(1)}, u32[]{:S(2)}, u32[]{:S(2)}) %collective-permute-start.56) | collective-permute-done | bytes 1572896 | tf_op jit(solution)/shard_map/ppermute | solution.py:50
  626.2 6.2 convert_add_fusion.1
  634.4 89.0 %collective-permute-done.49 = f32[17,2048]{1,0:T(8,128)S(1)} collective-permute-done((f32[17,2048]{1,0:T(8,128)S(1)}, f32[17,2048]{1,0:T(8,128)S(1)}, u32[]{:S(2)}, u32[]{:S(2)}) %collective-permute-start.49) | collective-permute-done | bytes 139296 | tf_op jit(solution)/shard_map/ppermute | solution.py:50
  741.4 6.2 collective-permute-done.36
  773.4 13.1 %collective-permute-done.33 = bf16[512,512]{1,0:T(8,128)(2,1)} collective-permute-done((bf16[512,512]{1,0:T(8,128)(2,1)}, bf16[512,512]{1,0:T(8,128)(2,1)}, u32[]{:S(2)}, u32[]{:S(2)}) %collective-permute-start.33) | collective-permute-done | bytes 524320 | tf_op jit(solution)/shard_map/ppermute | solution.py:50
  789.4 11.6 %convert_add_fusion = f32[768,2048]{1,0:T(8,128)} fusion(bf16[768,2048]{1,0:T(8,128)(2,1)} %collective-permute-done.53, bf16[768,2048]{1,0:T(8,128)(2,1)} %collective-permute-done.51, f32[768,2048]{1,0:T(8,128)} %fusion.27, f32[768,2048]{1,0:T(8,128)} %fusion.21), kind=kLoop, calls=%fused_computation.13 | loop fusion | flops 7864320 | bytes 25165824 | tf_op jit(solution)/shard_map/add | solution.py:380
  801.0 6.3 fusion.140
  (525 shorter events, 269.8 us)
Async XLA Ops:
  7.2 763.2 %reduce-scatter.7.cloned.1.call-start = ((), (), s32[]{:S(2)}) async-start(), calls=%async_computation.5 | async-start | bytes 589824 | tf_op jit(solution)/shard_map/reduce_scatter | solution.py:455
  43.3 57.2 %collective-permute-start.6 = (bf16[512,512]{1,0:T(8,128)(2,1)}, bf16[512,512]{1,0:T(8,128)(2,1)}, u32[]{:S(2)}, u32[]{:S(2)}) collective-permute-start(bf16[512,512]{1,0:T(8,128)(2,1)} %param.31), channel_id=1, source_target_pairs={{0,2},{1,3},{2,0},{3,1},{4,6},{5,7},{6,4},{7,5},{8,10},{9,11},{10,... | collective-permute-start | bytes 1572872 | tf_op jit(solution)/shard_map/ppermute | solution.py:50
  45.9 82.4 %collective-permute-start.7 = (bf16[512,512]{1,0:T(8,128)(2,1)}, bf16[512,512]{1,0:T(8,128)(2,1)}, u32[]{:S(2)}, u32[]{:S(2)}) collective-permute-start(bf16[512,512]{1,0:T(8,128)(2,1)} %param.31), channel_id=1, source_target_pairs={{0,1},{1,0},{2,3},{3,2},{4,5},{5,4},{6,7},{7,6},{8,9},{9,8},{10,11... | collective-permute-start | bytes 1572872 | tf_op jit(solution)/shard_map/ppermute | solution.py:50
  46.3 54.1 %collective-permute-start = (bf16[128,2048]{1,0:T(8,128)(2,1)}, bf16[128,2048]{1,0:T(8,128)(2,1)}, u32[]{:S(2)}, u32[]{:S(2)}) collective-permute-start(bf16[128,2048]{1,0:T(8,128)(2,1)} %get-tuple-element.57), channel_id=1, source_target_pairs={{0,1},{1,0},{2,3},{3,2},{4,5},{5,4},{6,7},{7,6},{8,9},{9,8},{10,11... | collective-permute-start | bytes 1572872 | tf_op jit(solution)/shard_map/ppermute | solution.py:50
  53.0 71.4 %collective-permute-start.10 = (bf16[768,2048]{1,0:T(8,128)(2,1)}, bf16[768,2048]{1,0:T(8,128)(2,1)}, u32[]{:S(2)}, u32[]{:S(2)}) collective-permute-start(bf16[768,2048]{1,0:T(8,128)(2,1)} %get-tuple-element.50), channel_id=1, source_target_pairs={{0,8},{4,12},{8,0},{12,4},{16,24},{20,28},{24,16},{28,20},{1,9},{5... | collective-permute-start | bytes 9437192 | tf_op jit(solution)/shard_map/ppermute | solution.py:50
  68.6 33.7 %collective-permute-start.2 = (bf16[128,2048]{1,0:T(8,128)(2,1)S(1)}, bf16[128,2048]{1,0:T(8,128)(2,1)S(1)}, u32[]{:S(2)}, u32[]{:S(2)}) collective-permute-start(bf16[128,2048]{1,0:T(8,128)(2,1)S(1)} %add_convert_fusion.17), channel_id=1, source_target_pairs={{0,2},{1,3},{2,0},{3,1},{4,6},{5,7},{6,4},{7,5},{8,10},{9,11},{10,... | collective-permute-start | bytes 1572872 | tf_op jit(solution)/shard_map/ppermute | solution.py:50
  100.5 88.6 %collective-permute-start.9 = (bf16[768,2048]{1,0:T(8,128)(2,1)}, bf16[768,2048]{1,0:T(8,128)(2,1)}, u32[]{:S(2)}, u32[]{:S(2)}) collective-permute-start(bf16[768,2048]{1,0:T(8,128)(2,1)} %get-tuple-element.50), channel_id=1, source_target_pairs={{0,4},{4,0},{8,12},{12,8},{16,20},{20,16},{24,28},{28,24},{1,5},{5... | collective-permute-start | bytes 9437192 | tf_op jit(solution)/shard_map/ppermute | solution.py:50
  100.5 55.2 %collective-permute-start.13 = (bf16[384,2048]{1,0:T(8,128)(2,1)}, bf16[384,2048]{1,0:T(8,128)(2,1)}, u32[]{:S(2)}, u32[]{:S(2)}) collective-permute-start(bf16[384,2048]{1,0:T(8,128)(2,1)} %bitcast.22), channel_id=1, source_target_pairs={{0,8},{4,12},{8,0},{12,4},{16,24},{20,28},{24,16},{28,20},{1,9},{5... | collective-permute-start | bytes 4718600 | tf_op jit(solution)/shard_map/ppermute | solution.py:50
  102.2 31.9 %collective-permute-start.8 = (bf16[512,512]{1,0:T(8,128)(2,1)}, bf16[512,512]{1,0:T(8,128)(2,1)}, u32[]{:S(2)}, u32[]{:S(2)}) collective-permute-start(bf16[512,512]{1,0:T(8,128)(2,1)} %collective-permute-done.6), channel_id=1, source_target_pairs={{0,1},{1,0},{2,3},{3,2},{4,5},{5,4},{6,7},{7,6},{8,9},{9,8},{10,11... | collective-permute-start | bytes 1572872 | tf_op jit(solution)/shard_map/ppermute | solution.py:50
  124.3 64.8 %collective-permute-start.11 = (bf16[768,2048]{1,0:T(8,128)(2,1)}, bf16[768,2048]{1,0:T(8,128)(2,1)}, u32[]{:S(2)}, u32[]{:S(2)}) collective-permute-start(bf16[768,2048]{1,0:T(8,128)(2,1)} %collective-permute-done.10), channel_id=1, source_target_pairs={{0,4},{4,0},{8,12},{12,8},{16,20},{20,16},{24,28},{28,24},{1,5},{5... | collective-permute-start | bytes 9437192 | tf_op jit(solution)/shard_map/ppermute | solution.py:50
  128.3 28.2 %collective-permute-start.3 = (bf16[128,2176]{1,0:T(8,128)(2,1)}, bf16[128,2176]{1,0:T(8,128)(2,1)}, u32[]{:S(2)}, u32[]{:S(2)}) collective-permute-start(bf16[128,2176]{1,0:T(8,128)(2,1)} %concatenate.40), channel_id=1, source_target_pairs={{0,2},{1,3},{2,0},{3,1},{4,6},{5,7},{6,4},{7,5},{8,10},{9,11},{10,... | collective-permute-start | bytes 1671176 | tf_op jit(solution)/shard_map/ppermute | solution.py:50
  134.1 47.7 %collective-permute-start.12 = (bf16[384,2048]{1,0:T(8,128)(2,1)}, bf16[384,2048]{1,0:T(8,128)(2,1)S(1)}, u32[]{:S(2)}, u32[]{:S(2)}) collective-permute-start(bf16[384,2048]{1,0:T(8,128)(2,1)} %bitcast.22), channel_id=1, source_target_pairs={{0,4},{4,0},{8,12},{12,8},{16,20},{20,16},{24,28},{28,24},{1,5},{5... | collective-permute-start | bytes 4718600 | tf_op jit(solution)/shard_map/ppermute | solution.py:50
  180.2 48.6 %collective-permute-start.16 = (bf16[512,2048]{1,0:T(8,128)(2,1)S(1)}, bf16[512,2048]{1,0:T(8,128)(2,1)S(1)}, u32[]{:S(2)}, u32[]{:S(2)}) collective-permute-start(bf16[512,2048]{1,0:T(8,128)(2,1)S(1)} %constant_dynamic-update-slice_fusion.7.dy_ref), channel_id=1, source_target_pairs={{0,16},{4,20},{8,24},{12,28},{16,0},{20,4},{24,8},{28,12},{1,17},{... | collective-permute-start | bytes 6291464 | tf_op jit(solution)/shard_map/ppermute | solution.py:50
  181.8 89.8 %collective-permute-start.15 = (bf16[512,2176]{1,0:T(8,128)(2,1)S(1)}, bf16[512,2176]{1,0:T(8,128)(2,1)}, u32[]{:S(2)}, u32[]{:S(2)}) collective-permute-start(bf16[512,2176]{1,0:T(8,128)(2,1)S(1)} %constant_dynamic-update-slice_fusion.11.packed_ref), channel_id=1, source_target_pairs={{0,16},{4,20},{8,24},{12,28},{16,0},{20,4},{24,8},{28,12},{1,17},{... | collective-permute-start | bytes 6684680 | tf_op jit(solution)/shard_map/ppermute | solution.py:50
  301.0 51.7 %collective-permute-start.24 = (bf16[512,2176]{1,0:T(8,128)(2,1)}, bf16[512,2176]{1,0:T(8,128)(2,1)S(1)}, u32[]{:S(2)}, u32[]{:S(2)}) collective-permute-start(bf16[512,2176]{1,0:T(8,128)(2,1)} %get-tuple-element.23), channel_id=1, source_target_pairs={{0,16},{4,20},{8,24},{12,28},{16,0},{20,4},{24,8},{28,12},{1,17},{... | collective-permute-start | bytes 6684680 | tf_op jit(solution)/shard_map/ppermute | solution.py:50
  311.0 80.7 %collective-permute-start.17 = (bf16[512,2048]{1,0:T(8,128)(2,1)S(1)}, bf16[512,2048]{1,0:T(8,128)(2,1)S(1)}, u32[]{:S(2)}, u32[]{:S(2)}) collective-permute-start(bf16[512,2048]{1,0:T(8,128)(2,1)S(1)} %add_convert_fusion.3), channel_id=1, source_target_pairs={{0,16},{4,20},{8,24},{12,28},{16,0},{20,4},{24,8},{28,12},{1,17},{... | collective-permute-start | bytes 6291464 | tf_op jit(solution)/shard_map/ppermute | solution.py:50
  318.9 271.6 %collective-permute-start.52 = (bf16[768,2048]{1,0:T(8,128)(2,1)}, bf16[768,2048]{1,0:T(8,128)(2,1)}, u32[]{:S(2)}, u32[]{:S(2)}) collective-permute-start(bf16[768,2048]{1,0:T(8,128)(2,1)} %add_convert_fusion.1), channel_id=1, source_target_pairs={{0,4},{4,0},{8,12},{12,8},{16,20},{20,16},{24,28},{28,24},{1,5},{5... | collective-permute-start | bytes 9437192 | tf_op jit(solution)/shard_map/ppermute | solution.py:50
  325.9 463.4 %collective-permute-start.51 = (bf16[768,2048]{1,0:T(8,128)(2,1)}, bf16[768,2048]{1,0:T(8,128)(2,1)}, u32[]{:S(2)}, u32[]{:S(2)}) collective-permute-start(bf16[768,2048]{1,0:T(8,128)(2,1)} %add_convert_fusion.2), channel_id=1, source_target_pairs={{0,4},{4,0},{8,12},{12,8},{16,20},{20,16},{24,28},{28,24},{1,5},{5... | collective-permute-start | bytes 9437192 | tf_op jit(solution)/shard_map/ppermute | solution.py:50
  352.9 42.3 %collective-permute-start.26 = (bf16[128,2176]{1,0:T(8,128)(2,1)S(1)}, bf16[128,2176]{1,0:T(8,128)(2,1)S(1)}, u32[]{:S(2)}, u32[]{:S(2)}) collective-permute-start(bf16[128,2176]{1,0:T(8,128)(2,1)S(1)} %get-tuple-element.45), channel_id=1, source_target_pairs={{0,1},{1,0},{2,3},{3,2},{4,5},{5,4},{6,7},{7,6},{8,9},{9,8},{10,11... | collective-permute-start | bytes 1671176 | tf_op jit(solution)/shard_map/ppermute | solution.py:50
  393.5 35.9 %collective-permute-start.25 = (bf16[128,2176]{1,0:T(8,128)(2,1)S(1)}, bf16[128,2176]{1,0:T(8,128)(2,1)S(1)}, u32[]{:S(2)}, u32[]{:S(2)}) collective-permute-start(bf16[128,2176]{1,0:T(8,128)(2,1)S(1)} %get-tuple-element.44), channel_id=1, source_target_pairs={{0,1},{1,0},{2,3},{3,2},{4,5},{5,4},{6,7},{7,6},{8,9},{9,8},{10,11... | collective-permute-start | bytes 1671176 | tf_op jit(solution)/shard_map/ppermute | solution.py:50
  395.4 34.5 %collective-permute-start.27 = (bf16[128,2176]{1,0:T(8,128)(2,1)S(1)}, bf16[128,2176]{1,0:T(8,128)(2,1)S(1)}, u32[]{:S(2)}, u32[]{:S(2)}) collective-permute-start(bf16[128,2176]{1,0:T(8,128)(2,1)S(1)} %add_convert_fusion.9), channel_id=1, source_target_pairs={{0,2},{1,3},{2,0},{3,1},{4,6},{5,7},{6,4},{7,5},{8,10},{9,11},{10,... | collective-permute-start | bytes 1671176 | tf_op jit(solution)/shard_map/ppermute | solution.py:50
  461.1 122.0 %collective-permute-start.55 = (bf16[384,2048]{1,0:T(8,128)(2,1)}, bf16[384,2048]{1,0:T(8,128)(2,1)}, u32[]{:S(2)}, u32[]{:S(2)}) collective-permute-start(bf16[384,2048]{1,0:T(8,128)(2,1)} %add_convert_fusion.6), channel_id=1, source_target_pairs={{0,4},{4,0},{8,12},{12,8},{16,20},{20,16},{24,28},{28,24},{1,5},{5... | collective-permute-start | bytes 4718600 | tf_op jit(solution)/shard_map/ppermute | solution.py:50
  489.0 117.1 %collective-permute-start.54 = (bf16[384,2048]{1,0:T(8,128)(2,1)}, bf16[384,2048]{1,0:T(8,128)(2,1)}, u32[]{:S(2)}, u32[]{:S(2)}) collective-permute-start(bf16[384,2048]{1,0:T(8,128)(2,1)} %add_convert_fusion.7), channel_id=1, source_target_pairs={{0,4},{4,0},{8,12},{12,8},{16,20},{20,16},{24,28},{28,24},{1,5},{5... | collective-permute-start | bytes 4718600 | tf_op jit(solution)/shard_map/ppermute | solution.py:50
  532.9 239.0 %reduce-scatter.9.cloned.1.call-start = ((), (), s32[]{:S(2)}) async-start(), calls=%async_computation.6 | async-start | bytes 589824 | tf_op jit(solution)/shard_map/reduce_scatter | solution.py:455
  541.0 266.4 %reduce-scatter.5.cloned.1.call-start = ((), (), s32[]{:S(2)}) async-start(), calls=%async_computation.4 | async-start | bytes 4718592 | tf_op jit(solution)/shard_map/reduce_scatter | solution.py:455
  554.3 255.2 %reduce-scatter.11.cloned.1.call-start = ((), (), s32[]{:S(2)}) async-start(), calls=%async_computation.7 | async-start | bytes 4718592 | tf_op jit(solution)/shard_map/reduce_scatter | solution.py:455
  586.6 39.6 %collective-permute-start.56 = (bf16[384,2048]{1,0:T(8,128)(2,1)}, bf16[384,2048]{1,0:T(8,128)(2,1)S(1)}, u32[]{:S(2)}, u32[]{:S(2)}) collective-permute-start(bf16[384,2048]{1,0:T(8,128)(2,1)} %add_convert_fusion.5), channel_id=1, source_target_pairs={{0,8},{4,12},{8,0},{12,4},{16,24},{20,28},{24,16},{28,20},{1,9},{5... | collective-permute-start | bytes 4718600 | tf_op jit(solution)/shard_map/ppermute | solution.py:50
  597.9 191.4 %collective-permute-start.53 = (bf16[768,2048]{1,0:T(8,128)(2,1)}, bf16[768,2048]{1,0:T(8,128)(2,1)}, u32[]{:S(2)}, u32[]{:S(2)}) collective-permute-start(bf16[768,2048]{1,0:T(8,128)(2,1)} %add_convert_fusion), channel_id=1, source_target_pairs={{0,8},{4,12},{8,0},{12,4},{16,24},{20,28},{24,16},{28,20},{1,9},{5... | collective-permute-start | bytes 9437192 | tf_op jit(solution)/shard_map/ppermute | solution.py:50
  600.4 33.8 %collective-permute-start.21 = (bf16[128,512]{1,0:T(8,128)(2,1)}, bf16[128,512]{1,0:T(8,128)(2,1)S(1)}, u32[]{:S(2)}, u32[]{:S(2)}) collective-permute-start(bf16[128,512]{1,0:T(8,128)(2,1)} %get-tuple-element.62), channel_id=1, source_target_pairs={{0,1},{1,0},{2,3},{3,2},{4,5},{5,4},{6,7},{7,6},{8,9},{9,8},{10,11... | collective-permute-start | bytes 393224 | tf_op jit(solution)/shard_map/ppermute | solution.py:50
  606.1 28.2 %collective-permute-start.22 = (bf16[128,512]{1,0:T(8,128)(2,1)}, bf16[128,512]{1,0:T(8,128)(2,1)S(1)}, u32[]{:S(2)}, u32[]{:S(2)}) collective-permute-start(bf16[128,512]{1,0:T(8,128)(2,1)} %get-tuple-element.61), channel_id=1, source_target_pairs={{0,2},{1,3},{2,0},{3,1},{4,6},{5,7},{6,4},{7,5},{8,10},{9,11},{10,... | collective-permute-start | bytes 393224 | tf_op jit(solution)/shard_map/ppermute | solution.py:50
  632.3 105.8 %collective-permute-start.23 = (bf16[128,512]{1,0:T(8,128)(2,1)S(1)}, bf16[128,512]{1,0:T(8,128)(2,1)S(1)}, u32[]{:S(2)}, u32[]{:S(2)}) collective-permute-start(bf16[128,512]{1,0:T(8,128)(2,1)S(1)} %copy-done.73), channel_id=1, source_target_pairs={{0,3},{1,2},{2,1},{3,0},{4,7},{5,6},{6,5},{7,4},{8,11},{9,10},{10,... | collective-permute-start | bytes 393224 | tf_op jit(solution)/shard_map/ppermute | solution.py:50
  634.3 89.2 %collective-permute-start.49 = (f32[17,2048]{1,0:T(8,128)S(1)}, f32[17,2048]{1,0:T(8,128)S(1)}, u32[]{:S(2)}, u32[]{:S(2)}) collective-permute-start(f32[17,2048]{1,0:T(8,128)S(1)} %add.448), channel_id=1, source_target_pairs={{0,8},{4,12},{8,0},{12,4},{16,24},{20,28},{24,16},{28,20},{1,9},{5... | collective-permute-start | bytes 417800 | tf_op jit(solution)/shard_map/ppermute | solution.py:50
  (153 other events, 2066.5 us)
Sparse Core Ops, SparseCore 0:
  533.0 32.6 reduce-scatter.6
  569.1 35.6 reduce-scatter.8
  608.2 68.2 reduce-scatter.4
  680.0 59.2 reduce-scatter.10

commit v2 on v1

v2 whole, which is shorter than its diff:
```python
import functools

import jax
import jax.numpy as jnp
import ml_dtypes
import numpy as np
from jax import lax
from jax.experimental import pallas as pl
from jax.experimental.pallas import tpu as pltpu
from jax.sharding import PartitionSpec as P

F32 = jnp.float32
B16 = jnp.bfloat16
EPS = 1e-06


def swap(values, axis, mask):
    count = lax.axis_size(axis)
    return lax.ppermute(values, axis, [(i, i ^ mask) for i in range(count)])


def bits_of(axis):
    return lax.axis_size(axis).bit_length() - 1


def gather_pieces(block, axis):
    held = {0: block}
    for bit in reversed(range(bits_of(axis))):
        mask = 1 << bit
        held.update({d ^ mask: swap(v, axis, mask) for d, v in list(held.items())})
    return [held[d] for d in range(lax.axis_size(axis))]


def gather_columns(block, axis):
    me = lax.axis_index(axis)
    size = block.shape[1]
    whole = jnp.zeros((block.shape[0], size * lax.axis_size(axis)), block.dtype)
    for d, v in enumerate(gather_pieces(block, axis)):
        whole = lax.dynamic_update_slice_in_dim(whole, v, (me ^ d) * size, 1)
    return whole


def scatter_terms(pieces, axis):
    return [pieces[0]] + scatter_terms_of(pieces, axis)


def scatter_terms_of(pieces, axis):
    held = {d: v for d, v in enumerate(pieces)}
    terms = []
    for bit in range(bits_of(axis)):
        mask = 1 << bit
        came = {d: swap(held[d ^ mask], axis, mask) for d in held if not d & mask}
        terms.append(came[0])
        held = {d: add_low(held[d], v) if d else None for d, v in came.items()}
    return terms


def after(values, *others):
    return lax.optimization_barrier((values, others))[0]


def add_low(*values):
    return functools.reduce(jnp.add, [v.astype(F32) for v in values]).astype(B16)


def swap_columns(rows, axis):
    count = lax.axis_size(axis)
    me = lax.axis_index(axis)
    height, width = rows.shape[0], rows.shape[1] // count
    whole = jnp.zeros((height * count, width), rows.dtype)
    for d in range(count):
        piece = lax.dynamic_slice_in_dim(rows, (me ^ d) * width, width, 1)
        if d:
            piece = swap(piece, axis, d)
        whole = lax.dynamic_update_slice_in_dim(whole, piece, (me ^ d) * height, 0)
    return whole


def sum_everywhere(values, axis):
    for bit in range(bits_of(axis)):
        values = values + swap(values, axis, 1 << bit)
    return values


def nn_dot(left, right):
    return jnp.dot(left, right, preferred_element_type=F32)


def nt_dot(left, right):
    return lax.dot_general(left, right, (((1,), (1,)), ((), ())), preferred_element_type=F32)


def tn_dot(left, right):
    return lax.dot_general(left, right, (((0,), (0,)), ((), ())), preferred_element_type=F32)


def vmem(*count):
    return [pl.BlockSpec(memory_space=pltpu.VMEM) for _ in range(count[0])]


def hbm(count):
    return [pl.BlockSpec(memory_space=pl.ANY) for _ in range(count)]


SMEM_SPEC = pl.BlockSpec(memory_space=pltpu.SMEM)


def params(mib=56):
    return pltpu.CompilerParams(vmem_limit_bytes=mib << 20)


def cost():
    return pl.CostEstimate(flops=1 << 20, bytes_accessed=1 << 16, transcendentals=0)


def shaped(shape, dtype):
    return jax.ShapeDtypeStruct(shape, dtype)


def rope_table(length, head_dim):
    half = head_dim // 2
    frequency = np.power(1000000.0, -2.0 * np.arange(half, dtype=np.float32) / head_dim)
    angles = np.arange(length, dtype=np.float32)[:, None] * frequency.astype(np.float32)[None, :]
    angles = angles.astype(np.float64)
    rest = np.concatenate(
        [np.cos(angles), np.cos(angles), -np.sin(angles), np.sin(angles)], axis=1
    )
    terms = []
    for _ in range(3):
        term = rest.astype(np.float32).astype(ml_dtypes.bfloat16)
        terms.append(term)
        rest = rest - term.astype(np.float64)
    return np.concatenate(terms, axis=1)


def norm_scale(values):
    return lax.rsqrt(jnp.mean(values * values, axis=-1, keepdims=True) + EPS)


def turned(values, cos, sine):
    return values * cos + pltpu.roll(values, values.shape[-1] // 2, 1) * sine


def turned_back(grads, cos, sine):
    return grads * cos + pltpu.roll(grads * sine, grads.shape[-1] // 2, 1)


def forward_kernel(
    tile, z_ref,
    seq_col, seq_row, table, x, gain, wk, wv, q_gain, k_gain, wq, wo,
    *refs,
):
    pieces, refs = refs[:-11], refs[-11:]
    h1, q_pre, q_low, k_pre, k_low, v_low, att, lse, turns, bias, acc = refs
    step = pl.program_id(0)
    rows = x.shape[0]
    head = wk.shape[1]
    per_step = wq.shape[1] // head

    @pl.when(step == 0)
    def _():
        values = x[...].astype(F32)
        h1[...] = (values * norm_scale(values) * gain[...]).astype(B16)
        query = lax.broadcasted_iota(jnp.int32, (rows, rows), 0)
        key = lax.broadcasted_iota(jnp.int32, (rows, rows), 1)
        same = seq_col[...] == seq_row[...]
        position = jnp.sum(jnp.where(same & (key < query), 1.0, 0.0), axis=1, keepdims=True)
        bias[...] = jnp.where(same & (key <= query), 0.0, -1e30)
        chosen = jnp.where(key == position.astype(jnp.int32), 1.0, 0.0).astype(B16)
        three = nn_dot(chosen, table[...])
        wide = 2 * head
        turns[...] = three[:, :wide] + three[:, wide : 2 * wide] + three[:, 2 * wide :]
        keys = nn_dot(h1[...], wk[...])
        k_pre[...] = keys
        k_low[...] = turned(
            keys * norm_scale(keys) * k_gain[...], turns[:, :head], turns[:, head:]
        ).astype(B16)
        v_low[...] = nn_dot(h1[...], wv[...]).astype(B16)
        lse[...] = jnp.zeros_like(lse)
        acc[...] = jnp.zeros_like(acc)

    queries = nn_dot(h1[...], wq[...])
    q_pre[...] = queries
    lane = lax.broadcasted_iota(jnp.int32, (tile, lse.shape[1]), 1)
    for i in range(per_step):
        at = slice(i * head, (i + 1) * head)
        mine = queries[:, at]
        q_low[:, at] = turned(
            mine * norm_scale(mine) * q_gain[...], turns[:, :head], turns[:, head:]
        ).astype(B16)
        for t in range(rows // tile):
            band = slice(t * tile, (t + 1) * tile)
            seen = (t + 1) * tile
            scores = nt_dot(q_low[band, at], k_low[:seen, :]) * head ** (-0.5) + bias[band, :seen]
            peak = jnp.max(scores, axis=1, keepdims=True)
            shares = jnp.exp(scores - peak)
            total = jnp.sum(shares, axis=1, keepdims=True)
            att[band, at] = nn_dot((shares / total).astype(B16), v_low[:seen, :]).astype(B16)
            lse[band, :] += jnp.where(lane == step * per_step + i, peak + jnp.log(total), 0.0)
    acc[...] += nn_dot(att[...], wo[...])

    @pl.when(step == pl.num_programs(0) - 1)
    def _():
        size = pieces[0].shape[0]
        for d, piece in enumerate(pieces):
            piece[...] = acc[pl.ds(pl.multiple_of((z_ref[0] ^ d) * size, size), size), :].astype(B16)


def attention_forward(z, seq, x, gain, wq, wk, wv, q_gain, k_gain, wo, parts):
    rows, width = x.shape
    head = wk.shape[1]
    block = min(2 * head, wq.shape[1])
    steps = wq.shape[1] // block
    table = jnp.asarray(rope_table(rows, head))
    whole = lambda *shape: pl.BlockSpec(shape, lambda g, z: (0,) * len(shape))
    column = lambda height: pl.BlockSpec((height, block), lambda g, z: (0, g))
    own = rows // parts
    outs = [shaped((own, width), B16)] * parts + [
        shaped((rows, width), B16),
        shaped((rows, wq.shape[1]), F32),
        shaped((rows, wq.shape[1]), B16),
        shaped((rows, head), F32),
        shaped((rows, head), B16),
        shaped((rows, head), B16),
        shaped((rows, wq.shape[1]), B16),
        shaped((rows, 128), F32),
        shaped((rows, 2 * head), F32),
    ]
    out = pl.pallas_call(
        functools.partial(forward_kernel, min(rows, 256)),
        grid_spec=pltpu.PrefetchScalarGridSpec(
            num_scalar_prefetch=1,
            grid=(steps,),
            in_specs=[
                whole(rows, 1), whole(1, rows), whole(*table.shape), whole(rows, width),
                whole(1, width), whole(width, head), whole(width, head), whole(1, head),
                whole(1, head), column(width), pl.BlockSpec((block, width), lambda g, z: (g, 0)),
            ],
            out_specs=[whole(own, width)] * parts + [
                whole(rows, width), column(rows), column(rows), whole(rows, head),
                whole(rows, head), whole(rows, head), column(rows), whole(rows, 128),
                whole(rows, 2 * head),
            ],
            scratch_shapes=[pltpu.VMEM((rows, rows), F32), pltpu.VMEM((rows, width), F32)],
        ),
        out_shape=outs,
        compiler_params=params(),
        cost_estimate=cost(),
    )(
        z, seq.reshape(rows, 1), seq.reshape(1, rows), table, x, gain.reshape(1, width),
        wk, wv, q_gain.reshape(1, head), k_gain.reshape(1, head), wq, wo,
    )
    return out[:parts], out[parts:]


def norm_back(grads, values, gain):
    scale = norm_scale(values)
    unit = values * scale
    gained = grads * gain
    back = scale * (gained - unit * jnp.mean(gained * unit, axis=-1, keepdims=True))
    return back, jnp.sum(grads * unit, axis=0, keepdims=True)


def backward_kernel(
    tile, parts, z_ref,
    seq_col, seq_row, x, gain, wk, wv, q_gain, k_gain, wq, wo,
    q_pre, q_low, k_pre, k_low, v_low, lse, turns, *refs,
):
    came, refs = refs[:parts], refs[parts:]
    cols, refs = refs[:parts], refs[parts:]
    branch, low, along, gains, bias, acc, dkey, dvalue = refs
    step = pl.program_id(0)
    last = pl.num_programs(0) - 1
    rows, width = x.shape
    head = wk.shape[1]
    per_step = wq.shape[1] // head
    cos, sine = turns[:, :head], turns[:, head:]

    @pl.when(step == 0)
    def _():
        size = came[0].shape[0]
        for d, piece in enumerate(came):
            branch[pl.ds(pl.multiple_of((z_ref[0] ^ d) * size, size), size), :] = piece[...]
        query = lax.broadcasted_iota(jnp.int32, (rows, rows), 0)
        key = lax.broadcasted_iota(jnp.int32, (rows, rows), 1)
        same = seq_col[...] == seq_row[...]
        bias[...] = jnp.where(same & (key <= query), 0.0, -1e30)
        acc[...] = jnp.zeros_like(acc)
        dkey[...] = jnp.zeros_like(dkey)
        dvalue[...] = jnp.zeros_like(dvalue)
        gains[...] = jnp.zeros_like(gains)

    @pl.when(step < last)
    def _():
        datt = nt_dot(branch[...], wo[...]).astype(B16)
        lane = lax.broadcasted_iota(jnp.int32, (tile, lse.shape[1]), 1)
        for i in range(per_step):
            at = slice(i * head, (i + 1) * head)
            parts_q = []
            for t in range(rows // tile):
                band = slice(t * tile, (t + 1) * tile)
                seen = (t + 1) * tile
                logsum = jnp.sum(
                    jnp.where(lane == step * per_step + i, lse[band, :], 0.0),
                    axis=1, keepdims=True,
                )
                scores = (
                    nt_dot(q_low[band, at], k_low[:seen, :]) * head ** (-0.5) + bias[band, :seen]
                )
                p = jnp.exp(scores - logsum)
                dout = datt[band, at]
                dp = nt_dot(dout, v_low[:seen, :])
                delta = jnp.sum(p * dp, axis=1, keepdims=True)
                ds = (p * (dp - delta)).astype(B16)
                parts_q.append(nn_dot(ds, k_low[:seen, :]) * head ** (-0.5))
                dkey[:seen, :] += tn_dot(ds, q_low[band, at]) * head ** (-0.5)
                dvalue[:seen, :] += tn_dot(p.astype(B16), dout)
            dq = turned_back(jnp.concatenate(parts_q, axis=0), cos, sine)
            back, gain_part = norm_back(dq, q_pre[:, at], q_gain[...])
            low[:, at] = back.astype(B16)
            gains[1:2, :head] += gain_part
        acc[...] += nt_dot(low[...], wq[...])

    @pl.when(step == last)
    def _():
        dk = turned_back(dkey[...], cos, sine)
        back, gain_part = norm_back(dk, k_pre[...], k_gain[...])
        gains[2:3, :head] = gain_part
        low[:, :head] = back.astype(B16)
        low[:, head : 2 * head] = dvalue[...].astype(B16)
        acc[...] += nt_dot(low[:, :head], wk[...]) + nt_dot(low[:, head : 2 * head], wv[...])
        values = x[...].astype(F32)
        total = acc[...]
        along[...] = jnp.sum(total * gain[...] * values, axis=1, keepdims=True)
        gains[0:1, :] = jnp.sum(total * (values * norm_scale(values)), axis=0, keepdims=True)
        size = cols[0].shape[1]
        for d, piece in enumerate(cols):
            piece[...] = acc[:, pl.ds(pl.multiple_of((z_ref[0] ^ d) * size, size), size)].astype(B16)


def attention_backward(z, seq, x, gain, wq, wk, wv, q_gain, k_gain, wo, kept, came):
    rows, width = x.shape
    head = wk.shape[1]
    block = 2 * head
    steps = wq.shape[1] // block
    parts = len(came)
    q_pre, q_low, k_pre, k_low, v_low, lse, turns = kept
    whole = lambda *shape: pl.BlockSpec(shape, lambda g, z: (0,) * len(shape))
    column = lambda height: pl.BlockSpec(
        (height, block), lambda g, z: (0, jnp.minimum(g, steps - 1))
    )
    outs = [shaped((rows, width // parts), B16)] * parts + [
        shaped((rows, width), B16),
        shaped((rows, block * (steps + 1)), B16),
        shaped((rows, 1), F32),
        shaped((8, width), F32),
    ]
    out = pl.pallas_call(
        functools.partial(backward_kernel, min(rows, 256), parts),
        grid_spec=pltpu.PrefetchScalarGridSpec(
            num_scalar_prefetch=1,
            grid=(steps + 1,),
            in_specs=[
                whole(rows, 1), whole(1, rows), whole(rows, width), whole(1, width),
                whole(width, head), whole(width, head), whole(1, head), whole(1, head),
                column(width),
                pl.BlockSpec((block, width), lambda g, z: (jnp.minimum(g, steps - 1), 0)),
                column(rows), column(rows), whole(rows, head), whole(rows, head),
                whole(rows, head), whole(rows, 128), whole(rows, 2 * head),
            ] + [whole(rows // parts, width)] * parts,
            out_specs=[whole(rows, width // parts)] * parts + [
                whole(rows, width),
                pl.BlockSpec((rows, block), lambda g, z: (0, g)),
                whole(rows, 1),
                whole(8, width),
            ],
            scratch_shapes=[
                pltpu.VMEM((rows, rows), F32), pltpu.VMEM((rows, width), F32),
                pltpu.VMEM((rows, head), F32), pltpu.VMEM((rows, head), F32),
            ],
        ),
        out_shape=outs,
        compiler_params=params(),
        cost_estimate=cost(),
    )(
        z, seq.reshape(rows, 1), seq.reshape(1, rows), x, gain.reshape(1, width), wk, wv,
        q_gain.reshape(1, head), k_gain.reshape(1, head), wq, wo,
        q_pre, q_low, k_pre, k_low, v_low, lse, turns, *came,
    )
    return out[:parts], out[parts:]


def router_kernel(terms, experts, *refs):
    parts, (x, routes, gain, router, middle, packed, shares) = refs[:terms], refs[terms:]
    total = x[...].astype(F32)
    branch = parts[0][...].astype(F32)
    for part in parts[1:]:
        branch = branch + part[...].astype(F32)
    total = total + branch
    middle[...] = total
    width = total.shape[1]
    hidden = (total * norm_scale(total) * gain[...]).astype(B16)
    packed[:, :width] = hidden
    logits = nt_dot(hidden, router[...])
    lane = lax.broadcasted_iota(jnp.int32, logits.shape, 1)
    twin = jnp.where(lane < experts, lane, lane - experts)
    chosen = jnp.zeros(logits.shape, jnp.bool_)
    for k in range(routes.shape[1]):
        chosen = chosen | (twin == routes[:, k : k + 1])
    chosen = chosen & (lane < 2 * experts)
    peak = jnp.max(jnp.where(chosen, logits, -1e30), axis=1, keepdims=True)
    raised = jnp.where(chosen, jnp.exp(jnp.minimum(logits - peak, 0.0)), 0.0)
    share = raised / jnp.sum(jnp.where(lane < experts, raised, 0.0), axis=1, keepdims=True)
    shares[...] = share
    high = share.astype(B16).astype(F32)
    packed[:, width:] = jnp.where(lane < experts, high, share - high).astype(B16)


def row_block(height, width):
    return pl.BlockSpec((height, width), lambda g, z: (z[0], 0))


def route_rows(z, terms, x, routes, gain, router, experts):
    own, width = terms[0].shape
    extra = router.shape[0]
    whole = lambda *shape: pl.BlockSpec(shape, lambda g, z: (0,) * len(shape))
    count = len(terms)

    def kernel(z_ref, *refs):
        router_kernel(count, experts, *refs)

    return pl.pallas_call(
        kernel,
        grid_spec=pltpu.PrefetchScalarGridSpec(
            num_scalar_prefetch=1,
            grid=(1,),
            in_specs=[whole(own, width)] * count + [
                row_block(own, width), row_block(own, routes.shape[1]), whole(1, width),
                whole(extra, width),
            ],
            out_specs=[whole(own, width), whole(own, width + extra), whole(own, extra)],
        ),
        out_shape=[
            shaped((own, width), F32), shaped((own, width + extra), B16), shaped((own, extra), F32),
        ],
        compiler_params=params(),
        cost_estimate=cost(),
    )(z, *terms, x, routes, gain.reshape(1, width), router)


def rows_back_kernel(count, experts, *refs):
    terms, (dy, middle, shares, gain, router, dbranch, sums) = refs[:count], refs[count:]
    width = middle.shape[1]
    total = terms[0][...].astype(F32)
    for term in terms[1:]:
        total = total + term[...].astype(F32)
    values = middle[...]
    share = shares[...]
    lane = lax.broadcasted_iota(jnp.int32, share.shape, 1)
    dshare = total[:, width:]
    share = jnp.where(lane < experts, share, 0.0)
    mean = jnp.sum(share * dshare, axis=1, keepdims=True)
    dlogits = (share * (dshare - mean)).astype(B16)
    scale = norm_scale(values)
    unit = values * scale
    hidden = (unit * gain[...]).astype(B16)
    dhidden = total[:, :width] + nn_dot(dlogits, router[...])
    gained = dhidden * gain[...]
    back = scale * (gained - unit * jnp.mean(gained * unit, axis=-1, keepdims=True))
    dbranch[...] = (back + dy[...].astype(F32)).astype(B16)
    grads = tn_dot(dlogits, hidden)
    sums[:experts, :] = grads[:experts, :]
    sums[experts:, :] = jnp.broadcast_to(
        jnp.sum(dhidden * unit, axis=0, keepdims=True), (8, width)
    )


def rows_back(z, terms, dy, middle, shares, gain, router, experts):
    own, width = middle.shape
    extra = router.shape[0]
    whole = lambda *shape: pl.BlockSpec(shape, lambda g, z: (0,) * len(shape))
    count = len(terms)

    def kernel(z_ref, *refs):
        rows_back_kernel(count, experts, *refs)

    return pl.pallas_call(
        kernel,
        grid_spec=pltpu.PrefetchScalarGridSpec(
            num_scalar_prefetch=1,
            grid=(1,),
            in_specs=[whole(own, width + extra)] * count + [
                row_block(own, width), whole(own, width), whole(own, extra), whole(1, width),
                whole(extra, width),
            ],
            out_specs=[whole(own, width), whole(experts + 8, width)],
        ),
        out_shape=[shaped((own, width), B16), shaped((experts + 8, width), F32)],
        compiler_params=params(),
        cost_estimate=cost(),
    )(z, *terms, dy, middle, shares, gain.reshape(1, width), router)


def expert_kernel(parts, group, slots, hidden, experts, *refs):
    z_ref, ids_ref, refs = refs[0], refs[1], refs[2:]
    packed, refs = refs[:parts], refs[parts:]
    dy, refs = refs[0], refs[1:]
    weights, refs = refs[: 2 * group], refs[2 * group :]
    backs, refs = refs[:parts], refs[parts:]
    held, dgu_out, act_out, gate_up, down, dgu_buf, act_buf, total, sems, out_sems = refs
    rows, width = dy.shape
    pair = 2 * hidden

    def fetch(d):
        slot = d % slots
        return [
            pltpu.make_async_copy(weights[2 * d], gate_up.at[slot], sems.at[0, slot]),
            pltpu.make_async_copy(weights[2 * d + 1], down.at[slot], sems.at[1, slot]),
        ]

    def store(d):
        return [
            pltpu.make_async_copy(dgu_buf.at[d % 2], dgu_out.at[d], out_sems.at[0, d % 2]),
            pltpu.make_async_copy(act_buf.at[d % 2], act_out.at[d], out_sems.at[1, d % 2]),
        ]

    for d in range(min(slots, group)):
        for copy in fetch(d):
            copy.start()
    size = packed[0].shape[0]
    extra = packed[0].shape[1] - width

    def rows_of(d):
        return pl.ds(pl.multiple_of((z_ref[0] ^ d) * size, size), size)

    for d in range(parts):
        held[rows_of(d), :] = packed[d][...]
    shares = held[:, width:].astype(F32)
    lane = lax.broadcasted_iota(jnp.int32, (rows, extra), 1)
    first = lax.broadcasted_iota(jnp.int32, (rows, pair), 1) < hidden

    def share_of(expert):
        mine = (lane == expert) | (lane == expert + experts)
        return jnp.sum(jnp.where(mine, shares, 0.0), axis=1, keepdims=True)

    dshares = jnp.zeros((rows, extra), F32)
    for d in range(group):
        slot = d % slots
        for copy in fetch(d):
            copy.wait()
        id_a, id_b = ids_ref[2 * d], ids_ref[2 * d + 1]
        both = nt_dot(held[:, :width], gate_up[slot])
        raw = nt_dot(dy[...], down[slot])
        gate, up = both[:, :pair], both[:, pair:]
        share = jnp.where(first, share_of(id_a), share_of(id_b))
        sig = 1.0 / (1.0 + jnp.exp(-gate))
        silu = gate * sig
        act = (silu * up).astype(B16).astype(F32)
        product = act * raw
        part_a = jnp.sum(jnp.where(first, product, 0.0), axis=1, keepdims=True)
        part_b = jnp.sum(jnp.where(first, 0.0, product), axis=1, keepdims=True)
        dshares = dshares + jnp.where(lane == id_a, part_a, 0.0)
        dshares = dshares + jnp.where(lane == id_b, part_b, 0.0)
        dact = share * raw
        dgate = dact * up * (sig * (1.0 + gate * (1.0 - sig)))
        dup = dact * silu
        if d >= 2:
            for copy in store(d - 2):
                copy.wait()
        dgu_buf[d % 2, :, :pair] = dgate.astype(B16)
        dgu_buf[d % 2, :, pair:] = dup.astype(B16)
        act_buf[d % 2] = (share * act).astype(B16)
        for copy in store(d):
            copy.start()
        term = nn_dot(dgu_buf[d % 2], gate_up[slot])
        total[...] = term if d == 0 else total[...] + term
        if d + slots < group:
            for copy in fetch(d + slots):
                copy.start()
    for d in range(parts):
        backs[d][:, :width] = total[rows_of(d), :].astype(B16)
    held_share = dshares.astype(B16)
    total[:, :extra] = held_share.astype(F32)
    for d in range(parts):
        backs[d][:, width:] = total[rows_of(d), :extra].astype(B16)
    for d in range(max(0, group - 2), group):
        for copy in store(d):
            copy.wait()


def expert_pass(z, ids, packed, dy, weights, experts):
    rows, width = dy.shape
    parts = len(packed)
    size, full = packed[0].shape
    group = len(weights)
    pair = weights[0][1].shape[0]
    slots = min(group, 4)
    out = pl.pallas_call(
        functools.partial(expert_kernel, parts, group, slots, pair // 2, experts),
        in_specs=[SMEM_SPEC, SMEM_SPEC] + vmem(parts + 1) + hbm(2 * group),
        out_specs=vmem(parts + 1) + hbm(2),
        out_shape=[shaped((size, full), B16)] * parts + [
            shaped((rows, full), B16),
            shaped((group, rows, 2 * pair), B16),
            shaped((group, rows, pair), B16),
        ],
        scratch_shapes=[
            pltpu.VMEM((slots, 2 * pair, width), B16),
            pltpu.VMEM((slots, pair, width), B16),
            pltpu.VMEM((2, rows, 2 * pair), B16),
            pltpu.VMEM((2, rows, pair), B16),
            pltpu.VMEM((rows, width), F32),
            pltpu.SemaphoreType.DMA((2, slots)),
            pltpu.SemaphoreType.DMA((2, 2)),
        ],
        compiler_params=params(58),
        cost_estimate=cost(),
    )(z, ids, *packed, dy, *[w for two in weights for w in two])
    return out[:parts], out[parts:]


def outputs_kernel(parts, sources, group, z_ref, *refs):
    acts, refs = refs[:sources], refs[sources:]
    downs, refs = refs[:group], refs[group:]
    outs, total = refs[:-1], refs[-1]
    size = outs[0].shape[0]
    for s in range(sources):
        value = nn_dot(acts[s][0], downs[0][...])
        for d in range(1, group):
            value = value + nn_dot(acts[s][d], downs[d][...])
        total[...] = value
        for d in range(parts):
            at = pl.ds(pl.multiple_of((z_ref[0] ^ d) * size, size), size)
            outs[s * parts + d][...] = total[at, :].astype(B16)


def expert_outputs(z, acts, downs, parts):
    group, rows, pair = acts[0].shape
    width = downs[0].shape[1]
    out = pl.pallas_call(
        functools.partial(outputs_kernel, parts, len(acts), group),
        grid=(1,),
        in_specs=[SMEM_SPEC]
        + [pl.BlockSpec((group, rows, pair), lambda g: (0, 0, 0)) for _ in acts]
        + [pl.BlockSpec((pair, width), lambda g: (0, 0)) for _ in downs],
        out_specs=[pl.BlockSpec((rows // parts, width), lambda g: (0, 0))] * (len(acts) * parts),
        out_shape=[shaped((rows // parts, width), B16)] * (len(acts) * parts),
        scratch_shapes=[pltpu.VMEM((rows, width), F32)],
        compiler_params=params(),
        cost_estimate=cost(),
    )(z, *acts, *downs)
    return [out[s * parts : (s + 1) * parts] for s in range(len(acts))]


def grads_kernel(sources, *refs):
    ins, refs = refs[: 4 * sources], refs[4 * sources :]
    came, out = refs[:-1], refs[-1]
    step = pl.program_id(0)
    width = out.shape[1]

    def write(part):
        total = came[0][...].astype(F32) if came else 0.0
        for s in range(sources):
            held, dy, dgu, act = ins[4 * s : 4 * s + 4]
            if part < 2:
                total = total + tn_dot(dgu[0], held[:, :width])
            else:
                total = total + tn_dot(act[0], dy[...])
        out[...] = total.astype(B16)

    @pl.when(step < 2)
    def _():
        write(0)

    @pl.when(step == 2)
    def _():
        write(2)


def expert_grads(distance, sources, came):
    held, dy, dgu, act = sources[0]
    rows, full = held.shape
    width = dy.shape[1]
    pair = act.shape[2]
    whole = lambda *shape: pl.BlockSpec(shape, lambda g: (0,) * len(shape))
    line = pl.BlockSpec((pair, width), lambda g: (g, 0))
    return pl.pallas_call(
        functools.partial(grads_kernel, len(sources)),
        grid=(3,),
        in_specs=[
            whole(rows, full),
            whole(rows, width),
            pl.BlockSpec((1, rows, pair), lambda g: (distance, 0, jnp.minimum(g, 1))),
            pl.BlockSpec((1, rows, pair), lambda g: (distance, 0, 0)),
        ] * len(sources) + [line] * len(came),
        out_specs=line,
        out_shape=shaped((3 * pair, width), B16),
        compiler_params=params(),
        cost_estimate=cost(),
    )(*[v for source in sources for v in source], *came)


def per_device(
    tokens,
    sequence_numbers,
    routes,
    attn_gain,
    w_query,
    key_projection,
    value_projection,
    query_gain,
    key_gain,
    w_out,
    moe_gain,
    w_router,
    w_gate,
    w_up,
    w_down,
    cotangent,
):
    tok_count, model_width = tokens.shape
    head_dim = query_gain.shape[0]
    tensor_size = lax.axis_size("tensor")
    tensor_pos = lax.axis_index("tensor")
    expert_size = lax.axis_size("expert")
    expert_pos = lax.axis_index("expert")
    local_experts, _, hidden = w_gate.shape
    experts = local_experts * expert_size
    pair = local_experts * hidden
    group = 2 << ((expert_size // 2).bit_length() // 2)
    rounds = expert_size // group
    z = tensor_pos.astype(jnp.int32).reshape(1)

    gate_up = {
        0: jnp.concatenate(
            [
                jnp.swapaxes(w_gate, 1, 2).reshape(pair, model_width),
                jnp.swapaxes(w_up, 1, 2).reshape(pair, model_width),
            ],
            axis=0,
        )
    }
    down = {0: w_down.reshape(pair, model_width)}
    for bit in reversed(range(1, group.bit_length() - 1)):
        for held in (gate_up, down):
            held.update({d ^ (1 << bit): swap(v, "expert", 1 << bit) for d, v in list(held.items())})
    ids = jnp.concatenate(
        [(expert_pos ^ d) * local_experts + jnp.arange(local_experts) for d in range(group)]
    ).astype(jnp.int32)
    dy_own = lax.all_gather(cotangent, "tensor", axis=1, tiled=True)
    dy_of = [dy_own] + [swap(dy_own, "expert", group * r) for r in range(1, rounds)]

    attention = (
        z, sequence_numbers, tokens, attn_gain, w_query, key_projection, value_projection,
        query_gain, key_gain, w_out,
    )
    branch_parts, kept = attention_forward(*attention, tensor_size)
    first_hidden, attended_low = kept[0], kept[6]
    kept = kept[1:6] + kept[7:]
    terms = scatter_terms(branch_parts, "tensor")

    router_rows = jnp.swapaxes(w_router, 0, 1)
    spare = -(2 * experts) % 128
    router_rows = jnp.concatenate(
        [router_rows, router_rows, jnp.zeros((spare, model_width), B16)], axis=0
    )
    middle, packed_rows, shares = route_rows(
        z, terms, tokens, routes, moe_gain, router_rows, experts
    )
    gate_up = after(gate_up, packed_rows)
    gate_up.update({d ^ 1: swap(v, "expert", 1) for d, v in list(gate_up.items())})
    packed_own = {0: packed_rows}
    packed_of = [{0: swap(packed_rows, "expert", group * r)} for r in range(1, rounds)]
    for bit in reversed(range(bits_of("tensor"))):
        came = {d ^ (1 << bit): swap(v, "tensor", 1 << bit) for d, v in packed_own.items()}
        came = after(came, packed_of)
        packed_own.update(came)
        for r in range(1, rounds):
            packed_of[r - 1].update({d: swap(v, "expert", group * r) for d, v in came.items()})
    down = after(down, packed_own)
    down.update({d ^ 1: swap(v, "expert", 1) for d, v in list(down.items())})
    weights = [(gate_up[d], down[d]) for d in range(group)]
    packed_of = [[p[d] for d in range(tensor_size)] for p in [packed_own] + packed_of]
    passes = [expert_pass(z, ids, p, d, weights, experts) for p, d in zip(packed_of, dy_of)]
    back_parts = [passes[0][0]] + [
        [swap(v, "expert", group * r) for v in passes[r][0]] for r in range(1, rounds)
    ]
    joined = [add_low(*several) for several in zip(*back_parts)]
    joined[0] = None
    back_terms = [part[0] for part in back_parts] + scatter_terms_of(joined, "tensor")

    sources = [(p[1][0], dy, p[1][1], p[1][2]) for p, dy in zip(passes, dy_of)]
    odd = {d: expert_grads(d, sources, ()) for d in range(group - 1, 0, -2)}
    odd = {d: swap(v, "expert", 1) for d, v in odd.items()}
    sums = {d: expert_grads(d, sources, (odd[d + 1],)) for d in range(group - 2, -1, -2)}
    local_sums = list(sums.values())
    mask = 2
    while mask < group:
        came = {d: swap(sums[d ^ mask], "expert", mask) for d in sums if not d & mask}
        sums = {
            d: sums[d].astype(F32) + v.astype(F32) if mask * 2 == group else add_low(sums[d], v)
            for d, v in came.items()
        }
        mask *= 2
    shape = (local_experts, hidden, model_width)
    gate_grad = jnp.swapaxes(sums[0][:pair].reshape(shape), 1, 2)
    up_grad = jnp.swapaxes(sums[0][pair : 2 * pair].reshape(shape), 1, 2)
    down_grad = sums[0][2 * pair :].reshape(shape)

    out_parts = expert_outputs(z, [p[1][2] for p in passes], [w[1] for w in weights], tensor_size)

    back_terms = after(back_terms, local_sums, out_parts)
    dbranch, row_sums = rows_back(
        z, back_terms, dy_own, middle, shares, moe_gain, router_rows, experts
    )
    dbranch_pieces = gather_pieces(dbranch, "tensor")
    branch_low = jnp.zeros((tok_count, model_width), B16)
    for d, v in enumerate(dbranch_pieces):
        at = (tensor_pos ^ d) * v.shape[0]
        branch_low = lax.dynamic_update_slice_in_dim(branch_low, v, at, 0)
    out_grad = tn_dot(attended_low, branch_low).astype(B16)
    dbranch_pieces = after(dbranch_pieces, out_grad)
    col_parts, (_, low, along, gains) = attention_backward(*attention, kept, dbranch_pieces)
    col_terms = scatter_terms(col_parts, "tensor")
    along = sum_everywhere(along, "tensor")
    width = model_width // tensor_size
    inputs = tokens.astype(F32)
    scale = lax.rsqrt(jnp.mean(inputs * inputs, axis=-1, keepdims=True) + EPS)

    def columns(values):
        return lax.dynamic_slice_in_dim(values, tensor_pos * width, width, values.ndim - 1)

    cols = functools.reduce(jnp.add, [t.astype(F32) for t in col_terms])
    input_grad = columns(branch_low).astype(F32) + scale * (
        cols * columns(attn_gain)
        - columns(inputs) * (scale * scale * (along * (1.0 / model_width)))
    )

    out_parts = after(out_parts, dbranch_pieces)
    out_parts = out_parts[:1] + [
        [swap(v, "expert", group * r) for v in out_parts[r]] for r in range(1, rounds)
    ]
    joined = [add_low(*several) for several in zip(*out_parts)]
    joined[0] = None
    out_terms = [part[0] for part in out_parts] + scatter_terms_of(joined, "tensor")
    mixed = functools.reduce(jnp.add, [t.astype(F32) for t in out_terms])
    block_out = swap_columns((middle + mixed).astype(B16), "tensor")

    def over_experts(values, dim):
        return lax.psum_scatter(
            values.astype(B16), "expert", scatter_dimension=dim, tiled=True
        ).astype(F32)

    out_weight_grad = over_experts(out_grad, 1)
    qkv = over_experts(tn_dot(first_hidden, low), 0)
    q_size = w_query.shape[1]

    columns_each = model_width // expert_size
    head_each = head_dim // expert_size
    spread = jnp.pad(
        gains[1:3, :head_dim].reshape(2, expert_size, head_each),
        ((0, 0), (0, 0), (0, columns_each - head_each)),
    )
    small = jnp.concatenate(
        [row_sums[: experts + 1], gains[:1], spread.reshape(2, model_width)], axis=0
    )
    small = small.reshape((small.shape[0],) + (2,) * bits_of("expert") + (columns_each,))
    for bit in range(bits_of("expert")):
        dim = small.ndim - 2
        mine = (expert_pos >> bit) & 1
        send = lax.dynamic_index_in_dim(small, 1 - mine, dim, False)
        keep = lax.dynamic_index_in_dim(small, mine, dim, False)
        small = keep + swap(send, "expert", 1 << bit)
    small = sum_everywhere(small, "tensor")

    return (
        block_out,
        input_grad,
        small[experts + 1],
        qkv[:, :q_size],
        qkv[:, q_size : q_size + head_dim],
        qkv[:, q_size + head_dim :],
        small[experts + 2, :head_each],
        small[experts + 3, :head_each],
        out_weight_grad,
        small[experts],
        jnp.swapaxes(small[:experts], 0, 1),
        gate_grad,
        up_grad,
        down_grad,
    )


def solution(mesh):
    placed = (
        P("expert", None),
        P("expert"),
        P("expert", None),
        P(),
        P(None, "tensor"),
        P(None, "tensor"),
        P(None, "tensor"),
        P(),
        P(),
        P("tensor", None),
        P(),
        P(),
        P("expert", None, "tensor"),
        P("expert", None, "tensor"),
        P("expert", "tensor", None),
        P("expert", "tensor"),
    )
    return jax.shard_map(
        per_device,
        mesh=mesh,
        in_specs=placed,
        out_specs=(
            P("expert", "tensor"),
            P("expert", "tensor"),
            P("expert"),
            P("expert", "tensor"),
            P("expert", "tensor"),
            P("expert", "tensor"),
            P("expert"),
            P("expert"),
            P("tensor", "expert"),
            P("expert"),
            P("expert", None),
            P("expert", None, "tensor"),
            P("expert", None, "tensor"),
            P("expert", "tensor", None),
        ),
        check_vma=False,
    )
```

time: 825 us -> 611 us (0.74)
  waiting for transfers between devices: 421 us -> 289 us
  Pallas kernels: 58.5 us -> 183 us
  matrix products: 116 us -> 11.7 us
  other arithmetic: 112 us -> 22.7 us
  local copies, waits for them, and re-layouts: 49.6 us -> 23.8 us
  starting transfers between devices: 44.6 us -> 59.6 us
    ppermute x57 -> x50, waiting for transfers between devices: 421 us -> 289 us  [swap(): return lax.ppermute(values, axis, [(i, i ^ mask) for i in range(count)])]
    pallas_call x2 -> x11, Pallas kernels: 58.5 us -> 183 us  [the longest x2 63 us: expert_pass(): pl.pallas_call(functools.partial(expert_kernel, parts, group, slots, pair...]
    dot_general x21 -> x2, matrix products: 67.2 us -> 11.7 us  [tn_dot(): lax.dot_general(left, right, (((0,), (0,)), ((), ())), preferred_element_...]
    dot_general x24 -> x0, matrix products: 48.5 us -> none  [the longest x8 16.6 us: per_device(): jnp.dot(act[d], down[d], preferred_element_type=F32)]
    another operation x8 -> x0, other arithmetic: 26.5 us -> none  [the longest x2 14.6 us: per_device(): gate_up = jnp.stack([a for a, _ in weights_held])]
    convert_element_type x15 -> x9, other arithmetic: 23.1 us -> 3.86 us  [the longest x8 3.45 us: add_low(): functools.reduce(jnp.add, [v.astype(F32) for v in values]).astype(B16)]
    ppermute x57 -> x50, starting transfers between devices: 44.1 us -> 59.5 us  [swap(): return lax.ppermute(values, axis, [(i, i ^ mask) for i in range(count)])]
    add x5, other arithmetic: 21.5 us -> 7.2 us  [the longest x1 4.37 us: per_device(): sums[d].astype(F32) + v.astype(F32)]
  transfers between devices with their start and end apart: 61 -> 53, of which waited for: 31 -> 27; matrix products, arithmetic and copies ran while one was open for 29% -> 6% of each run, Pallas kernels for 4% -> 23%
where the time goes in v2:
time: 611 us; the launch traced here: 605 us
  waiting for transfers between devices  289 us (47%)
  Pallas kernels  183 us (30%)
  starting transfers between devices  59.6 us (10%)
  local copies, waits for them, and re-layouts  23.8 us (4%)
  other arithmetic  22.7 us (4%)
  between operations  14.6 us (2%)
  matrix products  11.7 us (2%)
    ppermute x50, waiting for transfers between devices, swap(): return lax.ppermute(values, axis, [(i, i ^ mask) for i in range(count)])  289 us
    pallas_call x2, Pallas kernels, expert_pass(): pl.pallas_call(functools.partial(expert_kernel, parts, group, slots, pair...  63 us
    ppermute x50, starting transfers between devices, swap(): return lax.ppermute(values, axis, [(i, i ^ mask) for i in range(count)])  59.5 us
    pallas_call x4, Pallas kernels, expert_grads(): pl.pallas_call(functools.partial(grads_kernel, len(sources)), grid=(3,),...  44.4 us
    pallas_call x1, Pallas kernels, attention_backward(): pl.pallas_call(functools.partial(backward_kernel, min(rows, 256), parts),...  28.5 us
    pallas_call x1, Pallas kernels, attention_forward(): pl.pallas_call(functools.partial(forward_kernel, min(rows, 256)), grid_sp...  26 us
    pallas_call x1, Pallas kernels, expert_outputs(): pl.pallas_call(functools.partial(outputs_kernel, parts, len(acts), group)...  14 us
  transfers between devices with their start and end apart: 53, of which 27 were waited for; matrix products, arithmetic and copies ran while one was open for 6% of the time, Pallas kernels for 23%

profile of v2, /device:TPU:0, one launch (start us, length us, event | category | flops | bytes accessed | tf_op | source)
XLA Modules:
  0.0 605.1 jit_solution(17334502307703914058)
XLA Ops:
  15.1 26.0 %shard_map.272 = (bf16[128,2048]{1,0:T(8,128)(2,1)}, bf16[128,2048]{1,0:T(8,128)(2,1)}, bf16[128,2048]{1,0:T(8,128)(2,1)}, bf16[128,2048]{1,0:T(8,128)(2,1)}, bf...) custom-call(s32[1]{0:T(128)} %bitcast.z_ref.refs_0_, ...), custom_call_target="tpu_custom_call" | custom-call | flops 1048576 | bytes 65536 | tf_op jit(solution)/shard_map/pallas_call | solution.py:229
  43.2 27.2 %collective-permute-done.1 = bf16[128,2048]{1,0:T(8,128)(2,1)S(1)} collective-permute-done((bf16[128,2048]{1,0:T(8,128)(2,1)}, bf16[128,2048]{1,0:T(8,128)(2,1)S(1)}, u32[]{:S(2)}, u32[]{:S(2)}) %collective-permute-start.1) | collective-permute-done | bytes 524320 | tf_op jit(solution)/shard_map/ppermute | solution.py:19
  75.1 14.7 %collective-permute-done.refs_1_ = bf16[128,2048]{1,0:T(8,128)(2,1)S(1)} collective-permute-done((bf16[128,2048]{1,0:T(8,128)(2,1)}, bf16[128,2048]{1,0:T(8,128)(2,1)S(1)}, u32[]{:S(2)}, u32[]{:S(2)}) %collective-permute-start) | collective-permute-done | bytes 524320 | tf_op jit(solution)/shard_map/ppermute | solution.py:19
  89.8 7.3 %collective-permute-done.2.refs_2_ = bf16[128,2048]{1,0:T(8,128)(2,1)S(1)} collective-permute-done((bf16[128,2048]{1,0:T(8,128)(2,1)S(1)}, bf16[128,2048]{1,0:T(8,128)(2,1)S(1)}, u32[]{:S(2)}, u32[]{:S(2)}) %collective-permute-start.2) | collective-permute-done | bytes 524320 | tf_op jit(solution)/shard_map/ppermute | solution.py:19
  105.8 21.8 %collective-permute-done.4.refs_4_ = bf16[128,2176]{1,0:T(8,128)(2,1)S(1)} collective-permute-done((bf16[128,2176]{1,0:T(8,128)(2,1)}, bf16[128,2176]{1,0:T(8,128)(2,1)S(1)}, u32[]{:S(2)}, u32[]{:S(2)}) %collective-permute-start.4) | collective-permute-done | bytes 557088 | tf_op jit(solution)/shard_map/ppermute | solution.py:19
  129.5 13.2 %collective-permute-done.6.refs_5_ = bf16[128,2176]{1,0:T(8,128)(2,1)S(1)} collective-permute-done((bf16[128,2176]{1,0:T(8,128)(2,1)S(1)}, bf16[128,2176]{1,0:T(8,128)(2,1)S(1)}, u32[]{:S(2)}, u32[]{:S(2)}) %collective-permute-start.6) | collective-permute-done | bytes 557088 | tf_op jit(solution)/shard_map/ppermute | solution.py:19
  151.7 31.3 %shard_map.274 = (bf16[128,2176]{1,0:T(8,128)(2,1)}, bf16[128,2176]{1,0:T(8,128)(2,1)}, bf16[128,2176]{1,0:T(8,128)(2,1)}, bf16[128,2176]{1,0:T(8,128)(2,1)}, bf...) custom-call(s32[1]{0:T(128)} %bitcast.z_ref.refs_0_, s32[8]{0:T(128)} %pad_add_fusion.refs_1_, ...), custom_call_target="tpu_custom_call" | custom-call | flops 1048576 | bytes 65536 | tf_op jit(solution)/shard_map/pallas_call | solution.py:598
  183.1 21.8 %collective-permute-done.14.refs_3_ = bf16[128,2176]{1,0:T(8,128)(2,1)} collective-permute-done((bf16[128,2176]{1,0:T(8,128)(2,1)}, bf16[128,2176]{1,0:T(8,128)(2,1)}, u32[]{:S(2)}, u32[]{:S(2)}) %collective-permute-start.14) | collective-permute-done | bytes 557088 | tf_op jit(solution)/shard_map/ppermute | solution.py:19
  205.0 11.0 %collective-permute-done.15.refs_5_ = bf16[128,2176]{1,0:T(8,128)(2,1)} collective-permute-done((bf16[128,2176]{1,0:T(8,128)(2,1)}, bf16[128,2176]{1,0:T(8,128)(2,1)}, u32[]{:S(2)}, u32[]{:S(2)}) %collective-permute-start.15) | collective-permute-done | bytes 557088 | tf_op jit(solution)/shard_map/ppermute | solution.py:19
  217.3 31.7 %shard_map.275 = (bf16[128,2176]{1,0:T(8,128)(2,1)}, bf16[128,2176]{1,0:T(8,128)(2,1)}, bf16[128,2176]{1,0:T(8,128)(2,1)}, bf16[128,2176]{1,0:T(8,128)(2,1)}, bf...) custom-call(s32[1]{0:T(128)} %bitcast.z_ref.refs_0_, s32[8]{0:T(128)} %pad_add_fusion.refs_1_, ...), custom_call_target="tpu_custom_call" | custom-call | flops 1048576 | bytes 65536 | tf_op jit(solution)/shard_map/pallas_call | solution.py:598
  249.0 10.7 %shard_map.277 = bf16[1152,2048]{1,0:T(8,128)(2,1)} custom-call(bf16[512,2176]{1,0:T(8,128)(2,1)} %get-tuple-element.115.refs_0_, bf16[512,2048]{1,0:T(8,128)(2,1)} %all-gather.2.cloned.1.call-done.refs_6_.refs_1_.refs_4_, bf16[4,512,768]{2,1,0:T(8,128)(2,1)} %get-tuple-element.116.refs_2_, bf16[4,512,384]{2,1,0:T(8,128)(2,1)} %get-tuple-element.97.refs_0_.refs_3_, ...), custom_call_target="tpu_custom_call" | custom-call | flops 1048576 | bytes 65536 | tf_op jit(solution)/shard_map/pallas_call | solution.py:687
  259.8 10.8 %shard_map.279 = bf16[1152,2048]{1,0:T(8,128)(2,1)} custom-call(bf16[512,2176]{1,0:T(8,128)(2,1)} %get-tuple-element.115.refs_0_, bf16[512,2048]{1,0:T(8,128)(2,1)} %all-gather.2.cloned.1.call-done.refs_6_.refs_1_.refs_4_, bf16[4,512,768]{2,1,0:T(8,128)(2,1)} %get-tuple-element.116.refs_2_, bf16[4,512,384]{2,1,0:T(8,128)(2,1)} %get-tuple-element.97.refs_0_.refs_3_, ...), custom_call_target="tpu_custom_call" | custom-call | flops 1048576 | bytes 65536 | tf_op jit(solution)/shard_map/pallas_call | solution.py:687
  274.4 12.2 %collective-permute-done.21 = bf16[128,2176]{1,0:T(8,128)(2,1)S(1)} collective-permute-done((bf16[128,2176]{1,0:T(8,128)(2,1)}, bf16[128,2176]{1,0:T(8,128)(2,1)S(1)}, u32[]{:S(2)}, u32[]{:S(2)}) %collective-permute-start.21) | collective-permute-done | bytes 557088 | tf_op jit(solution)/shard_map/ppermute | solution.py:19
  288.2 22.3 %collective-permute-done.18 = bf16[128,2176]{1,0:T(8,128)(2,1)S(1)} collective-permute-done((bf16[128,2176]{1,0:T(8,128)(2,1)S(1)}, bf16[128,2176]{1,0:T(8,128)(2,1)S(1)}, u32[]{:S(2)}, u32[]{:S(2)}) %collective-permute-start.18) | collective-permute-done | bytes 557088 | tf_op jit(solution)/shard_map/ppermute | solution.py:19
  312.2 9.4 %collective-permute-done.20 = bf16[128,2176]{1,0:T(8,128)(2,1)S(1)} collective-permute-done((bf16[128,2176]{1,0:T(8,128)(2,1)S(1)}, bf16[128,2176]{1,0:T(8,128)(2,1)S(1)}, u32[]{:S(2)}, u32[]{:S(2)}) %collective-permute-start.20) | collective-permute-done | bytes 557088 | tf_op jit(solution)/shard_map/ppermute | solution.py:19
  325.2 14.0 %shard_map.276 = (bf16[128,2048]{1,0:T(8,128)(2,1)}, bf16[128,2048]{1,0:T(8,128)(2,1)}, bf16[128,2048]{1,0:T(8,128)(2,1)}, bf16[128,2048]{1,0:T(8,128)(2,1)}, bf...) custom-call(s32[1]{0:T(128)} %bitcast.z_ref.refs_0_, ...), custom_call_target="tpu_custom_call" | custom-call | flops 1048576 | bytes 65536 | tf_op jit(solution)/shard_map/pallas_call | solution.py:640
  339.2 11.3 %shard_map.278 = bf16[1152,2048]{1,0:T(8,128)(2,1)} custom-call(bf16[512,2176]{1,0:T(8,128)(2,1)} %get-tuple-element.115.refs_0_, bf16[512,2048]{1,0:T(8,128)(2,1)} %all-gather.2.cloned.1.call-done.refs_6_.refs_1_.refs_4_, bf16[4,512,768]{2,1,0:T(8,128)(2,1)} %get-tuple-element.116.refs_2_, bf16[4,512,384]{2,1,0:T(8,128)(2,1)} %get-tuple-element.97.refs_0_.refs_3_, ...), custom_call_target="tpu_custom_call" | custom-call | flops 1048576 | bytes 65536 | tf_op jit(solution)/shard_map/pallas_call | solution.py:687
  352.7 11.7 %shard_map.280 = bf16[1152,2048]{1,0:T(8,128)(2,1)} custom-call(bf16[512,2176]{1,0:T(8,128)(2,1)} %get-tuple-element.115.refs_0_, bf16[512,2048]{1,0:T(8,128)(2,1)} %all-gather.2.cloned.1.call-done.refs_6_.refs_1_.refs_4_, bf16[4,512,768]{2,1,0:T(8,128)(2,1)} %get-tuple-element.116.refs_2_, bf16[4,512,384]{2,1,0:T(8,128)(2,1)} %get-tuple-element.97.refs_0_.refs_3_, ...), custom_call_target="tpu_custom_call" | custom-call | flops 1048576 | bytes 65536 | tf_op jit(solution)/shard_map/pallas_call | solution.py:687
  372.7 20.6 %collective-permute-done.27.refs_2_ = bf16[128,2048]{1,0:T(8,128)(2,1)S(1)} collective-permute-done((bf16[128,2048]{1,0:T(8,128)(2,1)}, bf16[128,2048]{1,0:T(8,128)(2,1)S(1)}, u32[]{:S(2)}, u32[]{:S(2)}) %collective-permute-start.27) | collective-permute-done | bytes 524320 | tf_op jit(solution)/shard_map/ppermute | solution.py:19
  394.2 12.0 %collective-permute-done.28.refs_3_ = bf16[128,2048]{1,0:T(8,128)(2,1)S(1)} collective-permute-done((bf16[128,2048]{1,0:T(8,128)(2,1)S(1)}, bf16[128,2048]{1,0:T(8,128)(2,1)S(1)}, u32[]{:S(2)}, u32[]{:S(2)}) %collective-permute-start.28) | collective-permute-done | bytes 524320 | tf_op jit(solution)/shard_map/ppermute | solution.py:19
  407.6 4.4 convolution_convert_fusion.1
  413.1 28.5 %shard_map.282 = (bf16[512,512]{1,0:T(8,128)(2,1)}, bf16[512,512]{1,0:T(8,128)(2,1)}, bf16[512,512]{1,0:T(8,128)(2,1)}, bf16[512,512]{1,0:T(8,128)(2,1)}, bf16[5...) custom-call(s32[1]{0:T(128)} %bitcast.z_ref.refs_0_, ...), custom_call_target="tpu_custom_call" | custom-call | flops 1048576 | bytes 65536 | tf_op jit(solution)/shard_map/pallas_call | solution.py:358
  443.5 7.3 %convolution_convert_fusion = bf16[2048,1280]{1,0:T(8,128)(2,1)} fusion(bf16[512,2048]{1,0:T(8,128)(2,1)} %get-tuple-element.152, bf16[512,1280]{1,0:T(8,128)(2,1)} %get-tuple-element.153), kind=kOutput, calls=%fused_computation.1 | convolution fusion | flops 2686976000 | bytes 8650752 | tf_op jit(solution)/shard_map/dot_general | solution.py:94
  470.4 5.5 collective-permute-done.43
  483.1 14.6 %collective-permute-done.30 = bf16[128,2048]{1,0:T(8,128)(2,1)S(1)} collective-permute-done((bf16[128,2048]{1,0:T(8,128)(2,1)}, bf16[128,2048]{1,0:T(8,128)(2,1)S(1)}, u32[]{:S(2)}, u32[]{:S(2)}) %collective-permute-start.30) | collective-permute-done | bytes 524320 | tf_op jit(solution)/shard_map/ppermute | solution.py:19
  504.8 19.2 %collective-permute-done.40 = bf16[512,512]{1,0:T(8,128)(2,1)S(1)} collective-permute-done((bf16[512,512]{1,0:T(8,128)(2,1)}, bf16[512,512]{1,0:T(8,128)(2,1)S(1)}, u32[]{:S(2)}, u32[]{:S(2)}) %collective-permute-start.40) | collective-permute-done | bytes 524320 | tf_op jit(solution)/shard_map/ppermute | solution.py:19
  528.0 17.0 %collective-permute-done.31 = bf16[128,2048]{1,0:T(8,128)(2,1)S(1)} collective-permute-done((bf16[128,2048]{1,0:T(8,128)(2,1)S(1)}, bf16[128,2048]{1,0:T(8,128)(2,1)S(1)}, u32[]{:S(2)}, u32[]{:S(2)}) %collective-permute-start.31) | collective-permute-done | bytes 524320 | tf_op jit(solution)/shard_map/ppermute | solution.py:19
  545.6 5.3 collective-permute-start.37
  551.0 8.1 %collective-permute-done.39 = bf16[512,512]{1,0:T(8,128)(2,1)S(1)} collective-permute-done((bf16[512,512]{1,0:T(8,128)(2,1)S(1)}, bf16[512,512]{1,0:T(8,128)(2,1)S(1)}, u32[]{:S(2)}, u32[]{:S(2)}) %collective-permute-start.39) | collective-permute-done | bytes 524320 | tf_op jit(solution)/shard_map/ppermute | solution.py:19
  561.8 4.3 collective-permute-start.38
  569.1 15.1 %collective-permute-done.49 = bf16[1152,2048]{1,0:T(8,128)(2,1)} collective-permute-done((bf16[1152,2048]{1,0:T(8,128)(2,1)}, bf16[1152,2048]{1,0:T(8,128)(2,1)}, u32[]{:S(2)}, u32[]{:S(2)}) %collective-permute-start.49) | collective-permute-done | bytes 4718624 | tf_op jit(solution)/shard_map/ppermute | solution.py:19
  584.2 4.4 convert_add_fusion
  (235 shorter events, 115.7 us)
Async XLA Ops:
  7.2 137.0 %all-gather.2.cloned.1.call-start = ((), (), s32[]{:S(2)}) async-start(), calls=%async_computation.2 | async-start | bytes 2621440 | tf_op jit(solution)/shard_map/all_gather | solution.py:750
  11.2 94.6 %collective-permute-start.8 = (bf16[768,2048]{1,0:T(8,128)(2,1)}, bf16[768,2048]{1,0:T(8,128)(2,1)}, u32[]{:S(2)}, u32[]{:S(2)}) collective-permute-start(bf16[768,2048]{1,0:T(8,128)(2,1)} %pad_maximum_fusion.refs_7_), channel_id=1, source_target_pairs={{0,8},{4,12},{8,0},{12,4},{16,24},{20,28},{24,16},{28,20},{1,9},{5... | collective-permute-start | bytes 9437192 | tf_op jit(solution)/shard_map/ppermute | solution.py:19
  14.2 578.4 %reduce-scatter.5.cloned.1.call-start = ((), (), s32[]{:S(2)}) async-start(), calls=%async_computation.4 | async-start | bytes 4718592 | tf_op jit(solution)/shard_map/reduce_scatter | solution.py:850
  41.1 29.3 %collective-permute-start.1 = (bf16[128,2048]{1,0:T(8,128)(2,1)}, bf16[128,2048]{1,0:T(8,128)(2,1)S(1)}, u32[]{:S(2)}, u32[]{:S(2)}) collective-permute-start(bf16[128,2048]{1,0:T(8,128)(2,1)} %get-tuple-element.87), channel_id=1, source_target_pairs={{0,1},{1,0},{2,3},{3,2},{4,5},{5,4},{6,7},{7,6},{8,9},{9,8},{10,11... | collective-permute-start | bytes 1572872 | tf_op jit(solution)/shard_map/ppermute | solution.py:19
  42.7 47.1 %collective-permute-start = (bf16[128,2048]{1,0:T(8,128)(2,1)}, bf16[128,2048]{1,0:T(8,128)(2,1)S(1)}, u32[]{:S(2)}, u32[]{:S(2)}) collective-permute-start(bf16[128,2048]{1,0:T(8,128)(2,1)} %get-tuple-element.85), channel_id=1, source_target_pairs={{0,1},{1,0},{2,3},{3,2},{4,5},{5,4},{6,7},{7,6},{8,9},{9,8},{10,11... | collective-permute-start | bytes 1572872 | tf_op jit(solution)/shard_map/ppermute | solution.py:19
  71.5 25.6 %collective-permute-start.2 = (bf16[128,2048]{1,0:T(8,128)(2,1)S(1)}, bf16[128,2048]{1,0:T(8,128)(2,1)S(1)}, u32[]{:S(2)}, u32[]{:S(2)}) collective-permute-start(bf16[128,2048]{1,0:T(8,128)(2,1)S(1)} %add_convert_fusion.10), channel_id=1, source_target_pairs={{0,2},{1,3},{2,0},{3,1},{4,6},{5,7},{6,4},{7,5},{8,10},{9,11},{10,... | collective-permute-start | bytes 1572872 | tf_op jit(solution)/shard_map/ppermute | solution.py:19
  72.1 70.7 %collective-permute-start.9 = (bf16[384,2048]{1,0:T(8,128)(2,1)}, bf16[384,2048]{1,0:T(8,128)(2,1)}, u32[]{:S(2)}, u32[]{:S(2)}) collective-permute-start(bf16[384,2048]{1,0:T(8,128)(2,1)} %bitcast.12.refs_8_.refs_2_), channel_id=1, source_target_pairs={{0,8},{4,12},{8,0},{12,4},{16,24},{20,28},{24,16},{28,20},{1,9},{5... | collective-permute-start | bytes 4718600 | tf_op jit(solution)/shard_map/ppermute | solution.py:19
  101.3 26.3 %collective-permute-start.4 = (bf16[128,2176]{1,0:T(8,128)(2,1)}, bf16[128,2176]{1,0:T(8,128)(2,1)S(1)}, u32[]{:S(2)}, u32[]{:S(2)}) collective-permute-start(bf16[128,2176]{1,0:T(8,128)(2,1)} %get-tuple-element.89.refs_2_), channel_id=1, source_target_pairs={{0,2},{1,3},{2,0},{3,1},{4,6},{5,7},{6,4},{7,5},{8,10},{9,11},{10,... | collective-permute-start | bytes 1671176 | tf_op jit(solution)/shard_map/ppermute | solution.py:19
  101.3 26.3 %collective-permute-start.5 = (bf16[128,2176]{1,0:T(8,128)(2,1)}, bf16[128,2176]{1,0:T(8,128)(2,1)S(1)}, u32[]{:S(2)}, u32[]{:S(2)}) collective-permute-start(bf16[128,2176]{1,0:T(8,128)(2,1)} %get-tuple-element.89.refs_2_), channel_id=1, source_target_pairs={{0,16},{4,20},{8,24},{12,28},{16,0},{20,4},{24,8},{28,12},{1,17},{... | collective-permute-start | bytes 1671176 | tf_op jit(solution)/shard_map/ppermute | solution.py:19
  102.8 26.2 %collective-permute-start.3 = (bf16[128,2176]{1,0:T(8,128)(2,1)}, bf16[128,2176]{1,0:T(8,128)(2,1)S(1)}, u32[]{:S(2)}, u32[]{:S(2)}) collective-permute-start(bf16[128,2176]{1,0:T(8,128)(2,1)} %get-tuple-element.89.refs_2_), channel_id=1, source_target_pairs={{0,1},{1,0},{2,3},{3,2},{4,5},{5,4},{6,7},{7,6},{8,9},{9,8},{10,11... | collective-permute-start | bytes 1671176 | tf_op jit(solution)/shard_map/ppermute | solution.py:19
  105.8 45.9 %collective-permute-start.10 = (bf16[768,2048]{1,0:T(8,128)(2,1)}, bf16[768,2048]{1,0:T(8,128)(2,1)}, u32[]{:S(2)}, u32[]{:S(2)}) collective-permute-start(bf16[768,2048]{1,0:T(8,128)(2,1)} %pad_maximum_fusion.refs_7_), channel_id=1, source_target_pairs={{0,4},{4,0},{8,12},{12,8},{16,20},{20,16},{24,28},{28,24},{1,5},{5... | collective-permute-start | bytes 9437192 | tf_op jit(solution)/shard_map/ppermute | solution.py:19
  144.2 71.8 %collective-permute-start.16 = (bf16[512,2048]{1,0:T(8,128)(2,1)}, bf16[512,2048]{1,0:T(8,128)(2,1)S(1)}, u32[]{:S(2)}, u32[]{:S(2)}) collective-permute-start(bf16[512,2048]{1,0:T(8,128)(2,1)} %all-gather.2.cloned.1.call-done.refs_6_.refs_1_.refs_4_), channel_id=1, source_target_pairs={{0,16},{4,20},{8,24},{12,28},{16,0},{20,4},{24,8},{28,12},{1,17},{... | collective-permute-start | bytes 6291464 | tf_op jit(solution)/shard_map/ppermute | solution.py:19
  147.4 57.5 %collective-permute-start.14 = (bf16[128,2176]{1,0:T(8,128)(2,1)}, bf16[128,2176]{1,0:T(8,128)(2,1)}, u32[]{:S(2)}, u32[]{:S(2)}) collective-permute-start(bf16[128,2176]{1,0:T(8,128)(2,1)} %copy-done.11), channel_id=1, source_target_pairs={{0,16},{4,20},{8,24},{12,28},{16,0},{20,4},{24,8},{28,12},{1,17},{... | collective-permute-start | bytes 1671176 | tf_op jit(solution)/shard_map/ppermute | solution.py:19
  149.7 66.3 %collective-permute-start.15 = (bf16[128,2176]{1,0:T(8,128)(2,1)}, bf16[128,2176]{1,0:T(8,128)(2,1)}, u32[]{:S(2)}, u32[]{:S(2)}) collective-permute-start(bf16[128,2176]{1,0:T(8,128)(2,1)} %copy-done.13), channel_id=1, source_target_pairs={{0,16},{4,20},{8,24},{12,28},{16,0},{20,4},{24,8},{28,12},{1,17},{... | collective-permute-start | bytes 1671176 | tf_op jit(solution)/shard_map/ppermute | solution.py:19
  259.7 79.5 %collective-permute-start.24 = (bf16[1152,2048]{1,0:T(8,128)(2,1)}, bf16[1152,2048]{1,0:T(8,128)(2,1)}, u32[]{:S(2)}, u32[]{:S(2)}) collective-permute-start(bf16[1152,2048]{1,0:T(8,128)(2,1)} %shard_map.277), channel_id=1, source_target_pairs={{0,4},{4,0},{8,12},{12,8},{16,20},{20,16},{24,28},{28,24},{1,5},{5... | collective-permute-start | bytes 14155784 | tf_op jit(solution)/shard_map/ppermute | solution.py:19
  270.6 79.9 %collective-permute-start.25 = (bf16[1152,2048]{1,0:T(8,128)(2,1)}, bf16[1152,2048]{1,0:T(8,128)(2,1)S(1)}, u32[]{:S(2)}, u32[]{:S(2)}) collective-permute-start(bf16[1152,2048]{1,0:T(8,128)(2,1)} %shard_map.279), channel_id=1, source_target_pairs={{0,4},{4,0},{8,12},{12,8},{16,20},{20,16},{24,28},{28,24},{1,5},{5... | collective-permute-start | bytes 14155784 | tf_op jit(solution)/shard_map/ppermute | solution.py:19
  272.4 92.0 %collective-permute-start.17 = (bf16[128,2176]{1,0:T(8,128)(2,1)S(1)}, bf16[128,2176]{1,0:T(8,128)(2,1)S(1)}, u32[]{:S(2)}, u32[]{:S(2)}) collective-permute-start(bf16[128,2176]{1,0:T(8,128)(2,1)S(1)} %copy-done.34), channel_id=1, source_target_pairs={{0,16},{4,20},{8,24},{12,28},{16,0},{20,4},{24,8},{28,12},{1,17},{... | collective-permute-start | bytes 1671176 | tf_op jit(solution)/shard_map/ppermute | solution.py:19
  273.0 37.5 %collective-permute-start.18 = (bf16[128,2176]{1,0:T(8,128)(2,1)S(1)}, bf16[128,2176]{1,0:T(8,128)(2,1)S(1)}, u32[]{:S(2)}, u32[]{:S(2)}) collective-permute-start(bf16[128,2176]{1,0:T(8,128)(2,1)S(1)} %copy-done.36), channel_id=1, source_target_pairs={{0,16},{4,20},{8,24},{12,28},{16,0},{20,4},{24,8},{28,12},{1,17},{... | collective-permute-start | bytes 1671176 | tf_op jit(solution)/shard_map/ppermute | solution.py:19
  286.6 35.0 %collective-permute-start.20 = (bf16[128,2176]{1,0:T(8,128)(2,1)S(1)}, bf16[128,2176]{1,0:T(8,128)(2,1)S(1)}, u32[]{:S(2)}, u32[]{:S(2)}) collective-permute-start(bf16[128,2176]{1,0:T(8,128)(2,1)S(1)} %copy-done.35), channel_id=1, source_target_pairs={{0,16},{4,20},{8,24},{12,28},{16,0},{20,4},{24,8},{28,12},{1,17},{... | collective-permute-start | bytes 1671176 | tf_op jit(solution)/shard_map/ppermute | solution.py:19
  321.7 42.7 %collective-permute-start.19 = (bf16[128,2176]{1,0:T(8,128)(2,1)S(1)}, bf16[128,2176]{1,0:T(8,128)(2,1)S(1)}, u32[]{:S(2)}, u32[]{:S(2)}) collective-permute-start(bf16[128,2176]{1,0:T(8,128)(2,1)S(1)} %add_convert_fusion.3), channel_id=1, source_target_pairs={{0,1},{1,0},{2,3},{3,2},{4,5},{5,4},{6,7},{7,6},{8,9},{9,8},{10,11... | collective-permute-start | bytes 1671176 | tf_op jit(solution)/shard_map/ppermute | solution.py:19
  323.8 40.6 %collective-permute-start.23 = (bf16[128,2176]{1,0:T(8,128)(2,1)S(1)}, bf16[128,2176]{1,0:T(8,128)(2,1)S(1)}, u32[]{:S(2)}, u32[]{:S(2)}) collective-permute-start(bf16[128,2176]{1,0:T(8,128)(2,1)S(1)} %add_convert_fusion), channel_id=1, source_target_pairs={{0,2},{1,3},{2,0},{3,1},{4,6},{5,7},{6,4},{7,5},{8,10},{9,11},{10,... | collective-permute-start | bytes 1671176 | tf_op jit(solution)/shard_map/ppermute | solution.py:19
  412.0 182.6 %reduce-scatter.3.cloned.1.call-start = ((), (), s32[]{:S(2)}) async-start(), calls=%async_computation.3 | async-start | bytes 5898240 | tf_op jit(solution)/shard_map/reduce_scatter | solution.py:850
  453.3 130.9 %collective-permute-start.49 = (bf16[1152,2048]{1,0:T(8,128)(2,1)}, bf16[1152,2048]{1,0:T(8,128)(2,1)}, u32[]{:S(2)}, u32[]{:S(2)}) collective-permute-start(bf16[1152,2048]{1,0:T(8,128)(2,1)} %shard_map.278), channel_id=1, source_target_pairs={{0,8},{4,12},{8,0},{12,4},{16,24},{20,28},{24,16},{28,20},{1,9},{5... | collective-permute-start | bytes 14155784 | tf_op jit(solution)/shard_map/ppermute | solution.py:19
  457.8 24.5 %collective-permute-start.33 = (bf16[128,2048]{1,0:T(8,128)(2,1)}, bf16[128,2048]{1,0:T(8,128)(2,1)S(1)}, u32[]{:S(2)}, u32[]{:S(2)}) collective-permute-start(bf16[128,2048]{1,0:T(8,128)(2,1)} %get-tuple-element.137), channel_id=1, source_target_pairs={{0,16},{4,20},{8,24},{12,28},{16,0},{20,4},{24,8},{28,12},{1,17},{... | collective-permute-start | bytes 1572872 | tf_op jit(solution)/shard_map/ppermute | solution.py:19
  468.4 30.8 %collective-permute-start.32 = (bf16[128,2048]{1,0:T(8,128)(2,1)}, bf16[128,2048]{1,0:T(8,128)(2,1)S(1)}, u32[]{:S(2)}, u32[]{:S(2)}) collective-permute-start(bf16[128,2048]{1,0:T(8,128)(2,1)} %get-tuple-element.135), channel_id=1, source_target_pairs={{0,16},{4,20},{8,24},{12,28},{16,0},{20,4},{24,8},{28,12},{1,17},{... | collective-permute-start | bytes 1572872 | tf_op jit(solution)/shard_map/ppermute | solution.py:19
  469.8 27.9 %collective-permute-start.30 = (bf16[128,2048]{1,0:T(8,128)(2,1)}, bf16[128,2048]{1,0:T(8,128)(2,1)S(1)}, u32[]{:S(2)}, u32[]{:S(2)}) collective-permute-start(bf16[128,2048]{1,0:T(8,128)(2,1)} %get-tuple-element.133), channel_id=1, source_target_pairs={{0,16},{4,20},{8,24},{12,28},{16,0},{20,4},{24,8},{28,12},{1,17},{... | collective-permute-start | bytes 1572872 | tf_op jit(solution)/shard_map/ppermute | solution.py:19
  480.7 43.5 %collective-permute-start.29 = (bf16[128,2048]{1,0:T(8,128)(2,1)}, bf16[128,2048]{1,0:T(8,128)(2,1)S(1)}, u32[]{:S(2)}, u32[]{:S(2)}) collective-permute-start(bf16[128,2048]{1,0:T(8,128)(2,1)} %get-tuple-element.131), channel_id=1, source_target_pairs={{0,16},{4,20},{8,24},{12,28},{16,0},{20,4},{24,8},{28,12},{1,17},{... | collective-permute-start | bytes 1572872 | tf_op jit(solution)/shard_map/ppermute | solution.py:19
  497.7 26.3 %collective-permute-start.40 = (bf16[512,512]{1,0:T(8,128)(2,1)}, bf16[512,512]{1,0:T(8,128)(2,1)S(1)}, u32[]{:S(2)}, u32[]{:S(2)}) collective-permute-start(bf16[512,512]{1,0:T(8,128)(2,1)} %get-tuple-element.148), channel_id=1, source_target_pairs={{0,1},{1,0},{2,3},{3,2},{4,5},{5,4},{6,7},{7,6},{8,9},{9,8},{10,11... | collective-permute-start | bytes 1572872 | tf_op jit(solution)/shard_map/ppermute | solution.py:19
  499.1 45.9 %collective-permute-start.31 = (bf16[128,2048]{1,0:T(8,128)(2,1)S(1)}, bf16[128,2048]{1,0:T(8,128)(2,1)S(1)}, u32[]{:S(2)}, u32[]{:S(2)}) collective-permute-start(bf16[128,2048]{1,0:T(8,128)(2,1)S(1)} %add_convert_fusion.9), channel_id=1, source_target_pairs={{0,1},{1,0},{2,3},{3,2},{4,5},{5,4},{6,7},{7,6},{8,9},{9,8},{10,11... | collective-permute-start | bytes 1572872 | tf_op jit(solution)/shard_map/ppermute | solution.py:19
  501.4 43.6 %collective-permute-start.35 = (bf16[128,2048]{1,0:T(8,128)(2,1)S(1)}, bf16[128,2048]{1,0:T(8,128)(2,1)S(1)}, u32[]{:S(2)}, u32[]{:S(2)}) collective-permute-start(bf16[128,2048]{1,0:T(8,128)(2,1)S(1)} %add_convert_fusion.6), channel_id=1, source_target_pairs={{0,2},{1,3},{2,0},{3,1},{4,6},{5,7},{6,4},{7,5},{8,10},{9,11},{10,... | collective-permute-start | bytes 1572872 | tf_op jit(solution)/shard_map/ppermute | solution.py:19
  524.0 35.1 %collective-permute-start.39 = (bf16[512,512]{1,0:T(8,128)(2,1)S(1)}, bf16[512,512]{1,0:T(8,128)(2,1)S(1)}, u32[]{:S(2)}, u32[]{:S(2)}) collective-permute-start(bf16[512,512]{1,0:T(8,128)(2,1)S(1)} %copy-done.37), channel_id=1, source_target_pairs={{0,1},{1,0},{2,3},{3,2},{4,5},{5,4},{6,7},{7,6},{8,9},{9,8},{10,11... | collective-permute-start | bytes 1572872 | tf_op jit(solution)/shard_map/ppermute | solution.py:19
  524.2 34.9 %collective-permute-start.41 = (bf16[512,512]{1,0:T(8,128)(2,1)S(1)}, bf16[512,512]{1,0:T(8,128)(2,1)S(1)}, u32[]{:S(2)}, u32[]{:S(2)}) collective-permute-start(bf16[512,512]{1,0:T(8,128)(2,1)S(1)} %add_convert_fusion.4), channel_id=1, source_target_pairs={{0,2},{1,3},{2,0},{3,1},{4,6},{5,7},{6,4},{7,5},{8,10},{9,11},{10,... | collective-permute-start | bytes 1572872 | tf_op jit(solution)/shard_map/ppermute | solution.py:19
  (61 other events, 1187.5 us)
Sparse Core Ops, SparseCore 0:
  14.3 56.5 all-gather.1
  412.1 57.6 reduce-scatter.4
  473.6 77.8 reduce-scatter.2

commit v3 on v2

--- a/solution.py
+++ b/solution.py
@@ -21,27 +21,6 @@
 
 def bits_of(axis):
     return lax.axis_size(axis).bit_length() - 1
-
-
-def gather_pieces(block, axis):
-    held = {0: block}
-    for bit in reversed(range(bits_of(axis))):
-        mask = 1 << bit
-        held.update({d ^ mask: swap(v, axis, mask) for d, v in list(held.items())})
-    return [held[d] for d in range(lax.axis_size(axis))]
-
-
-def gather_columns(block, axis):
-    me = lax.axis_index(axis)
-    size = block.shape[1]
-    whole = jnp.zeros((block.shape[0], size * lax.axis_size(axis)), block.dtype)
-    for d, v in enumerate(gather_pieces(block, axis)):
-        whole = lax.dynamic_update_slice_in_dim(whole, v, (me ^ d) * size, 1)
-    return whole
-
-
-def scatter_terms(pieces, axis):
-    return [pieces[0]] + scatter_terms_of(pieces, axis)
 
 
 def scatter_terms_of(pieces, axis):
@@ -59,21 +38,30 @@
     return lax.optimization_barrier((values, others))[0]
 
 
+def further_terms(pieces, came, axis):
+    return passed_on({d: add_low(pieces[d], v) if d else None for d, v in came.items()}, axis)
+
+
+def passed_on(held, axis):
+    terms = []
+    for bit in range(1, bits_of(axis)):
+        mask = 1 << bit
+        came = {d: swap(held[d ^ mask], axis, mask) for d in held if not d & mask}
+        terms.append(came[0])
+        held = {d: add_low(held[d], v) if d else None for d, v in came.items()}
+    return terms
+
+
+def exchange_near(pieces, axis):
+    return {d: swap(pieces[d ^ 1], axis, 1) for d in range(lax.axis_size(axis) - 2, -1, -2)}
+
+
+def together(*values):
+    return lax.optimization_barrier(values)
+
+
 def add_low(*values):
     return functools.reduce(jnp.add, [v.astype(F32) for v in values]).astype(B16)
-
-
-def swap_columns(rows, axis):
-    count = lax.axis_size(axis)
-    me = lax.axis_index(axis)
-    height, width = rows.shape[0], rows.shape[1] // count
-    whole = jnp.zeros((height * count, width), rows.dtype)
-    for d in range(count):
-        piece = lax.dynamic_slice_in_dim(rows, (me ^ d) * width, width, 1)
-        if d:
-            piece = swap(piece, axis, d)
-        whole = lax.dynamic_update_slice_in_dim(whole, piece, (me ^ d) * height, 0)
-    return whole
 
 
 def sum_everywhere(values, axis):
@@ -109,8 +97,12 @@
     return pltpu.CompilerParams(vmem_limit_bytes=mib << 20)
 
 
-def cost():
-    return pl.CostEstimate(flops=1 << 20, bytes_accessed=1 << 16, transcendentals=0)
+PACE = 3.0
+
+
+def cost(micros):
+    moved = int(micros * PACE * 3.6e6)
+    return pl.CostEstimate(flops=0, bytes_accessed=moved, transcendentals=0)
 
 
 def shaped(shape, dtype):
@@ -245,7 +237,7 @@
         ),
         out_shape=outs,
         compiler_params=params(),
-        cost_estimate=cost(),
+        cost_estimate=cost(26),
     )(
         z, seq.reshape(rows, 1), seq.reshape(1, rows), table, x, gain.reshape(1, width),
         wk, wv, q_gain.reshape(1, head), k_gain.reshape(1, head), wq, wo,
@@ -262,36 +254,48 @@
 
 
 def backward_kernel(
-    tile, parts, z_ref,
-    seq_col, seq_row, x, gain, wk, wv, q_gain, k_gain, wq, wo,
-    q_pre, q_low, k_pre, k_low, v_low, lse, turns, *refs,
+    tile, parts, first_pair, opening, closing, z_ref,
+    seq_col, seq_row, q_gain, wq, wo, q_pre, q_low, k_low, v_low, lse, turns, *refs,
 ):
-    came, refs = refs[:parts], refs[parts:]
-    cols, refs = refs[:parts], refs[parts:]
-    branch, low, along, gains, bias, acc, dkey, dvalue = refs
+    if opening:
+        came, refs = refs[:parts], refs[parts:]
+    else:
+        (branch, acc_in, dkey_in, dvalue_in, gains_in), refs = refs[:5], refs[5:]
+    if closing:
+        (x, gain, wk, wv, k_gain, k_pre), refs = refs[:6], refs[6:]
+        cols, refs = refs[:parts], refs[parts:]
+        low, row_scale, gains, bias, acc, dkey, dvalue = refs
+    else:
+        branch, low, acc, dkey, dvalue, gains, bias = refs
     step = pl.program_id(0)
     last = pl.num_programs(0) - 1
-    rows, width = x.shape
-    head = wk.shape[1]
+    rows = seq_col.shape[0]
+    head = k_low.shape[1]
     per_step = wq.shape[1] // head
     cos, sine = turns[:, :head], turns[:, head:]
 
     @pl.when(step == 0)
     def _():
-        size = came[0].shape[0]
-        for d, piece in enumerate(came):
-            branch[pl.ds(pl.multiple_of((z_ref[0] ^ d) * size, size), size), :] = piece[...]
         query = lax.broadcasted_iota(jnp.int32, (rows, rows), 0)
         key = lax.broadcasted_iota(jnp.int32, (rows, rows), 1)
         same = seq_col[...] == seq_row[...]
         bias[...] = jnp.where(same & (key <= query), 0.0, -1e30)
-        acc[...] = jnp.zeros_like(acc)
-        dkey[...] = jnp.zeros_like(dkey)
-        dvalue[...] = jnp.zeros_like(dvalue)
-        gains[...] = jnp.zeros_like(gains)
-
-    @pl.when(step < last)
-    def _():
+        if opening:
+            size = came[0].shape[0]
+            for d, piece in enumerate(came):
+                at = pl.ds(pl.multiple_of((z_ref[0] ^ d) * size, size), size)
+                branch[at, :] = piece[...]
+            acc[...] = jnp.zeros_like(acc)
+            dkey[...] = jnp.zeros_like(dkey)
+            dvalue[...] = jnp.zeros_like(dvalue)
+            gains[...] = jnp.zeros_like(gains)
+        else:
+            acc[...] = acc_in[...]
+            dkey[...] = dkey_in[...]
+            dvalue[...] = dvalue_in[...]
+            gains[...] = gains_in[...]
+
+    def heads():
         datt = nt_dot(branch[...], wo[...]).astype(B16)
         lane = lax.broadcasted_iota(jnp.int32, (tile, lse.shape[1]), 1)
         for i in range(per_step):
@@ -300,10 +304,8 @@
             for t in range(rows // tile):
                 band = slice(t * tile, (t + 1) * tile)
                 seen = (t + 1) * tile
-                logsum = jnp.sum(
-                    jnp.where(lane == step * per_step + i, lse[band, :], 0.0),
-                    axis=1, keepdims=True,
-                )
+                mine = lane == (first_pair + step) * per_step + i
+                logsum = jnp.sum(jnp.where(mine, lse[band, :], 0.0), axis=1, keepdims=True)
                 scores = (
                     nt_dot(q_low[band, at], k_low[:seen, :]) * head ** (-0.5) + bias[band, :seen]
                 )
@@ -321,6 +323,11 @@
             gains[1:2, :head] += gain_part
         acc[...] += nt_dot(low[...], wq[...])
 
+    if not closing:
+        heads()
+        return
+    pl.when(step < last)(heads)
+
     @pl.when(step == last)
     def _():
         dk = turned_back(dkey[...], cos, sine)
@@ -331,63 +338,132 @@
         acc[...] += nt_dot(low[:, :head], wk[...]) + nt_dot(low[:, head : 2 * head], wv[...])
         values = x[...].astype(F32)
         total = acc[...]
-        along[...] = jnp.sum(total * gain[...] * values, axis=1, keepdims=True)
-        gains[0:1, :] = jnp.sum(total * (values * norm_scale(values)), axis=0, keepdims=True)
+        along = jnp.sum(total * gain[...] * values, axis=1, keepdims=True)
+        gains[3:4, :rows] = jnp.broadcast_to(along, (rows, 128)).T[:1]
+        scale = norm_scale(values)
+        row_scale[...] = scale
+        gains[0:1, :] = jnp.sum(total * (values * scale), axis=0, keepdims=True)
         size = cols[0].shape[1]
         for d, piece in enumerate(cols):
-            piece[...] = acc[:, pl.ds(pl.multiple_of((z_ref[0] ^ d) * size, size), size)].astype(B16)
-
-
-def attention_backward(z, seq, x, gain, wq, wk, wv, q_gain, k_gain, wo, kept, came):
+            at = pl.ds(pl.multiple_of((z_ref[0] ^ d) * size, size), size)
+            piece[:rows, :] = acc[:, at].astype(B16)
+            piece[rows:, :] = jnp.concatenate(
+                [gains[3:4, :rows].reshape(1, rows)]
+                + [gains[0:1, i * size : (i + 1) * size] for i in range(parts)]
+                + [gains[1:2, :size], gains[2:3, :size]]
+                + [jnp.zeros((16 - 3 - parts, size), F32)],
+                axis=0,
+            ).astype(B16)
+
+
+def attention_backward(z, seq, x, gain, wq, wk, wv, q_gain, k_gain, wo, kept, came, held):
+    opening, closing = held is None, held is not None
     rows, width = x.shape
     head = wk.shape[1]
     block = 2 * head
-    steps = wq.shape[1] // block
-    parts = len(came)
+    pairs = wq.shape[1] // block
+    half = pairs // 2
+    first, steps = (0, half) if opening else (half, pairs - half)
+    parts = width // (wo.shape[1] // lax.axis_size("tensor"))
     q_pre, q_low, k_pre, k_low, v_low, lse, turns = kept
     whole = lambda *shape: pl.BlockSpec(shape, lambda g, z: (0,) * len(shape))
-    column = lambda height: pl.BlockSpec(
-        (height, block), lambda g, z: (0, jnp.minimum(g, steps - 1))
-    )
-    outs = [shaped((rows, width // parts), B16)] * parts + [
-        shaped((rows, width), B16),
-        shaped((rows, block * (steps + 1)), B16),
-        shaped((rows, 1), F32),
+    pair_at = lambda g: first + jnp.minimum(g, steps - 1)
+    column = lambda height: pl.BlockSpec((height, block), lambda g, z: (0, pair_at(g)))
+    state = [whole(rows, width), whole(rows, head), whole(rows, head), whole(8, width)]
+    state_shapes = [
+        shaped((rows, width), F32), shaped((rows, head), F32), shaped((rows, head), F32),
         shaped((8, width), F32),
     ]
-    out = pl.pallas_call(
-        functools.partial(backward_kernel, min(rows, 256), parts),
+    ins = [
+        seq.reshape(rows, 1), seq.reshape(1, rows), q_gain.reshape(1, head), wq, wo,
+        q_pre, q_low, k_low, v_low, lse, turns,
+    ]
+    in_specs = [
+        whole(rows, 1), whole(1, rows), whole(1, head), column(width),
+        pl.BlockSpec((block, width), lambda g, z: (pair_at(g), 0)),
+        column(rows), column(rows), whole(rows, head), whole(rows, head), whole(rows, 128),
+        whole(rows, 2 * head),
+    ]
+    low_block = pl.BlockSpec((rows, block), lambda g, z: (0, g))
+    if opening:
+        ins = ins + list(came)
+        in_specs = in_specs + [whole(rows // parts, width)] * parts
+        outs = [shaped((rows, width), B16), shaped((rows, block * steps), B16)] + state_shapes
+        out_specs = [whole(rows, width), low_block] + state
+        scratch = [pltpu.VMEM((rows, rows), F32)]
+    else:
+        ins = ins + list(held) + [
+            x, gain.reshape(1, width), wk, wv, k_gain.reshape(1, head), k_pre,
+        ]
+        in_specs = in_specs + [whole(rows, width)] + state + [
+            whole(rows, width), whole(1, width), whole(width, head), whole(width, head),
+            whole(1, head), whole(rows, head),
+        ]
+        outs = [shaped((rows + 16, width // parts), B16)] * parts + [
+            shaped((rows, block * (steps + 1)), B16), shaped((rows, 1), F32),
+        ]
+        out_specs = [whole(rows + 16, width // parts)] * parts + [low_block, whole(rows, 1)]
+        scratch = [
+            pltpu.VMEM((8, width), F32),
+            pltpu.VMEM((rows, rows), F32), pltpu.VMEM((rows, width), F32),
+            pltpu.VMEM((rows, head), F32), pltpu.VMEM((rows, head), F32),
+        ]
+    return pl.pallas_call(
+        functools.partial(
+            backward_kernel, min(rows, 256), parts, first, opening, closing
+        ),
         grid_spec=pltpu.PrefetchScalarGridSpec(
             num_scalar_prefetch=1,
-            grid=(steps + 1,),
-            in_specs=[
-                whole(rows, 1), whole(1, rows), whole(rows, width), whole(1, width),
-                whole(width, head), whole(width, head), whole(1, head), whole(1, head),
-                column(width),
-                pl.BlockSpec((block, width), lambda g, z: (jnp.minimum(g, steps - 1), 0)),
-                column(rows), column(rows), whole(rows, head), whole(rows, head),
-                whole(rows, head), whole(rows, 128), whole(rows, 2 * head),
-            ] + [whole(rows // parts, width)] * parts,
-            out_specs=[whole(rows, width // parts)] * parts + [
-                whole(rows, width),
-                pl.BlockSpec((rows, block), lambda g, z: (0, g)),
-                whole(rows, 1),
-                whole(8, width),
-            ],
-            scratch_shapes=[
-                pltpu.VMEM((rows, rows), F32), pltpu.VMEM((rows, width), F32),
-                pltpu.VMEM((rows, head), F32), pltpu.VMEM((rows, head), F32),
-            ],
+            grid=(steps + closing,),
+            in_specs=in_specs,
+            out_specs=out_specs,
+            scratch_shapes=scratch,
         ),
         out_shape=outs,
         compiler_params=params(),
-        cost_estimate=cost(),
-    )(
-        z, seq.reshape(rows, 1), seq.reshape(1, rows), x, gain.reshape(1, width), wk, wv,
-        q_gain.reshape(1, head), k_gain.reshape(1, head), wq, wo,
-        q_pre, q_low, k_pre, k_low, v_low, lse, turns, *came,
-    )
-    return out[:parts], out[parts:]
+        cost_estimate=cost(16),
+    )(z, *ins)
+
+
+def grads_in_blocks(order, left, rights):
+    count = order.shape[0]
+    half, high = count // 2, left.shape[1] // count
+    wide = sum(v.shape[1] for v in rights)
+
+    def kernel(order_ref, left_ref, *refs):
+        right_refs, (send, keep, *whole) = refs[: len(rights)], refs[len(rights) :]
+        start = 0
+        for ref in right_refs if whole else ():
+            end = start + ref.shape[1]
+            whole[0][:, start:end] = tn_dot(left_ref[...], ref[...]).astype(B16)
+            start = end
+        for i in range(count):
+            if whole:
+                at = pl.ds(pl.multiple_of(order_ref[i] * high, high), high)
+                (send, keep)[i // half][i % half] = whole[0][at, :]
+                continue
+            at = pl.ds(pl.multiple_of(order_ref[i] * high, high), high)
+            block = left_ref[:, at]
+            out, start = (send, keep)[i // half], 0
+            for ref in right_refs:
+                end = start + ref.shape[1]
+                out[i % half, :, start:end] = tn_dot(block, ref[...]).astype(B16)
+                start = end
+
+    return pl.pallas_call(
+        kernel,
+        in_specs=[SMEM_SPEC] + vmem(1 + len(rights)),
+        out_specs=vmem(2),
+        out_shape=[shaped((half, high, wide), B16)] * 2,
+        scratch_shapes=[pltpu.VMEM((left.shape[1], wide), B16)] if high % 128 else [],
+        compiler_params=params(),
+        cost_estimate=cost(6),
+    )(order, left, *rights)
+
+
+def halves_after(keep, came):
+    half = keep.shape[0] // 2
+    return add_low(keep[:half], came[:half]), add_low(keep[half:], came[half:])
 
 
 def router_kernel(terms, experts, *refs):
@@ -444,7 +520,7 @@
             shaped((own, width), F32), shaped((own, width + extra), B16), shaped((own, extra), F32),
         ],
         compiler_params=params(),
-        cost_estimate=cost(),
+        cost_estimate=cost(3),
     )(z, *terms, x, routes, gain.reshape(1, width), router)
 
 
@@ -497,25 +573,67 @@
         ),
         out_shape=[shaped((own, width), B16), shaped((experts + 8, width), F32)],
         compiler_params=params(),
-        cost_estimate=cost(),
+        cost_estimate=cost(4),
     )(z, *terms, dy, middle, shares, gain.reshape(1, width), router)
 
 
-def expert_kernel(parts, group, slots, hidden, experts, *refs):
+def input_grad_of(z, terms, x, branch, gain, row_scale):
+    rows, width = x.shape
+    size = terms[0].shape[1]
+    below = terms[0].shape[0] - rows
+    count = len(terms)
+
+    def kernel(z_ref, *refs):
+        parts, (x_ref, branch_ref, gain_ref, scale_ref, out, small) = refs[:count], refs[count:]
+        total = parts[0][...].astype(F32)
+        for part in parts[1:]:
+            total = total + part[...].astype(F32)
+        small[...] = total[rows:, :]
+        along = jnp.broadcast_to(total[rows : rows + 1, :rows], (128, rows)).T[:, :1]
+        scale = scale_ref[...]
+        out[...] = branch_ref[...].astype(F32) + scale * (
+            total[:rows, :] * gain_ref[...]
+            - x_ref[...].astype(F32) * (scale * scale * (along * (1.0 / width)))
+        )
+
+    whole = lambda *shape: pl.BlockSpec(shape, lambda g, z: (0,) * len(shape))
+    column = lambda height: pl.BlockSpec((height, size), lambda g, z: (0, z[0]))
+    return pl.pallas_call(
+        kernel,
+        grid_spec=pltpu.PrefetchScalarGridSpec(
+            num_scalar_prefetch=1,
+            grid=(1,),
+            in_specs=[whole(rows + below, size)] * count + [
+                column(rows), column(rows), column(1), whole(rows, 1),
+            ],
+            out_specs=[whole(rows, size), whole(below, size)],
+        ),
+        out_shape=[shaped((rows, size), F32), shaped((below, size), F32)],
+        compiler_params=params(),
+        cost_estimate=cost(3),
+    )(z, *terms, x, branch, gain.reshape(1, width), row_scale)
+
+
+def expert_kernel(places, group, slots, hidden, experts, *refs):
+    parts = len(places)
     z_ref, ids_ref, refs = refs[0], refs[1], refs[2:]
     packed, refs = refs[:parts], refs[parts:]
     dy, refs = refs[0], refs[1:]
-    weights, refs = refs[: 2 * group], refs[2 * group :]
+    weights, refs = refs[: 3 * group], refs[3 * group :]
     backs, refs = refs[:parts], refs[parts:]
     held, dgu_out, act_out, gate_up, down, dgu_buf, act_buf, total, sems, out_sems = refs
     rows, width = dy.shape
     pair = 2 * hidden
+    size = rows // parts
+    extra = held.shape[1] - width
 
     def fetch(d):
         slot = d % slots
+        gate, up, dn = weights[3 * d : 3 * d + 3]
         return [
-            pltpu.make_async_copy(weights[2 * d], gate_up.at[slot], sems.at[0, slot]),
-            pltpu.make_async_copy(weights[2 * d + 1], down.at[slot], sems.at[1, slot]),
+            pltpu.make_async_copy(gate, gate_up.at[slot, :pair], sems.at[0, slot]),
+            pltpu.make_async_copy(up, gate_up.at[slot, pair:], sems.at[1, slot]),
+            pltpu.make_async_copy(dn, down.at[slot], sems.at[2, slot]),
         ]
 
     def store(d):
@@ -524,17 +642,17 @@
             pltpu.make_async_copy(act_buf.at[d % 2], act_out.at[d], out_sems.at[1, d % 2]),
         ]
 
-    for d in range(min(slots, group)):
+    for copy in fetch(0):
+        copy.start()
+    for d in range(1, min(slots, group)):
         for copy in fetch(d):
             copy.start()
-    size = packed[0].shape[0]
-    extra = packed[0].shape[1] - width
 
     def rows_of(d):
         return pl.ds(pl.multiple_of((z_ref[0] ^ d) * size, size), size)
 
-    for d in range(parts):
-        held[rows_of(d), :] = packed[d][...]
+    for i, d in enumerate(places):
+        held[rows_of(d), :] = packed[i][...]
     shares = held[:, width:].astype(F32)
     lane = lax.broadcasted_iota(jnp.int32, (rows, extra), 1)
     first = lax.broadcasted_iota(jnp.int32, (rows, pair), 1) < hidden
@@ -577,27 +695,27 @@
         if d + slots < group:
             for copy in fetch(d + slots):
                 copy.start()
-    for d in range(parts):
-        backs[d][:, :width] = total[rows_of(d), :].astype(B16)
-    held_share = dshares.astype(B16)
-    total[:, :extra] = held_share.astype(F32)
-    for d in range(parts):
-        backs[d][:, width:] = total[rows_of(d), :extra].astype(B16)
+    for i, d in enumerate(places):
+        backs[i][:, :width] = total[rows_of(d), :].astype(B16)
+    total[:, :extra] = dshares
+    for i, d in enumerate(places):
+        backs[i][:, width:] = total[rows_of(d), :extra].astype(B16)
     for d in range(max(0, group - 2), group):
         for copy in store(d):
             copy.wait()
 
 
-def expert_pass(z, ids, packed, dy, weights, experts):
-    rows, width = dy.shape
-    parts = len(packed)
+def expert_pass(z, ids, places, packed, dy, weights, experts):
+    width = dy.shape[1]
+    parts = len(places)
     size, full = packed[0].shape
+    rows = size * parts
     group = len(weights)
-    pair = weights[0][1].shape[0]
+    pair = weights[0][0].shape[0]
     slots = min(group, 4)
     out = pl.pallas_call(
-        functools.partial(expert_kernel, parts, group, slots, pair // 2, experts),
-        in_specs=[SMEM_SPEC, SMEM_SPEC] + vmem(parts + 1) + hbm(2 * group),
+        functools.partial(expert_kernel, tuple(places), group, slots, pair // 2, experts),
+        in_specs=[SMEM_SPEC, SMEM_SPEC] + vmem(parts + 1) + hbm(3 * group),
         out_specs=vmem(parts + 1) + hbm(2),
         out_shape=[shaped((size, full), B16)] * parts + [
             shaped((rows, full), B16),
@@ -610,56 +728,53 @@
             pltpu.VMEM((2, rows, 2 * pair), B16),
             pltpu.VMEM((2, rows, pair), B16),
             pltpu.VMEM((rows, width), F32),
-            pltpu.SemaphoreType.DMA((2, slots)),
+            pltpu.SemaphoreType.DMA((3, slots)),
             pltpu.SemaphoreType.DMA((2, 2)),
         ],
         compiler_params=params(58),
-        cost_estimate=cost(),
-    )(z, ids, *packed, dy, *[w for two in weights for w in two])
-    return out[:parts], out[parts:]
-
-
-def outputs_kernel(parts, sources, group, z_ref, *refs):
+        cost_estimate=cost(31),
+    )(z, ids, *packed, dy, *[w for three in weights for w in three])
+    return dict(zip(places, out[:parts])), out[parts:]
+
+
+def outputs_kernel(parts, sources, group, z_ref, middle, *refs):
     acts, refs = refs[:sources], refs[sources:]
-    downs, refs = refs[:group], refs[group:]
-    outs, total = refs[:-1], refs[-1]
-    size = outs[0].shape[0]
+    downs, outs, total = refs[:group], refs[group:-1], refs[-1]
+    size = outs[0].shape[1]
     for s in range(sources):
         value = nn_dot(acts[s][0], downs[0][...])
         for d in range(1, group):
             value = value + nn_dot(acts[s][d], downs[d][...])
         total[...] = value
+        if s == 0:
+            own = middle.shape[0]
+            total[pl.ds(pl.multiple_of(z_ref[0] * own, own), own), :] += middle[...]
         for d in range(parts):
             at = pl.ds(pl.multiple_of((z_ref[0] ^ d) * size, size), size)
-            outs[s * parts + d][...] = total[at, :].astype(B16)
-
-
-def expert_outputs(z, acts, downs, parts):
+            outs[s * parts + d][...] = total[:, at].astype(B16)
+
+
+def expert_outputs(z, middle, acts, downs, parts):
     group, rows, pair = acts[0].shape
     width = downs[0].shape[1]
-    out = pl.pallas_call(
+    count = len(acts) * parts
+    return pl.pallas_call(
         functools.partial(outputs_kernel, parts, len(acts), group),
-        grid=(1,),
-        in_specs=[SMEM_SPEC]
-        + [pl.BlockSpec((group, rows, pair), lambda g: (0, 0, 0)) for _ in acts]
-        + [pl.BlockSpec((pair, width), lambda g: (0, 0)) for _ in downs],
-        out_specs=[pl.BlockSpec((rows // parts, width), lambda g: (0, 0))] * (len(acts) * parts),
-        out_shape=[shaped((rows // parts, width), B16)] * (len(acts) * parts),
+        in_specs=[SMEM_SPEC] + vmem(1 + len(acts) + group),
+        out_specs=vmem(count),
+        out_shape=[shaped((rows, width // parts), B16)] * count,
         scratch_shapes=[pltpu.VMEM((rows, width), F32)],
         compiler_params=params(),
-        cost_estimate=cost(),
-    )(z, *acts, *downs)
-    return [out[s * parts : (s + 1) * parts] for s in range(len(acts))]
+        cost_estimate=cost(10),
+    )(z, middle, *acts, *downs)
 
 
 def grads_kernel(sources, *refs):
-    ins, refs = refs[: 4 * sources], refs[4 * sources :]
-    came, out = refs[:-1], refs[-1]
-    step = pl.program_id(0)
+    ins, out = refs[:-1], refs[-1]
     width = out.shape[1]
 
     def write(part):
-        total = came[0][...].astype(F32) if came else 0.0
+        total = 0.0
         for s in range(sources):
             held, dy, dgu, act = ins[4 * s : 4 * s + 4]
             if part < 2:
@@ -668,36 +783,61 @@
                 total = total + tn_dot(act[0], dy[...])
         out[...] = total.astype(B16)
 
-    @pl.when(step < 2)
-    def _():
-        write(0)
-
-    @pl.when(step == 2)
-    def _():
-        write(2)
-
-
-def expert_grads(distance, sources, came):
-    held, dy, dgu, act = sources[0]
-    rows, full = held.shape
-    width = dy.shape[1]
-    pair = act.shape[2]
+    step = pl.program_id(0)
+    pl.when(step < 2)(functools.partial(write, 0))
+    pl.when(step == 2)(functools.partial(write, 2))
+
+
+def expert_grads(distance, sources):
+    pair, width = sources[0][3].shape[2], sources[0][1].shape[1]
     whole = lambda *shape: pl.BlockSpec(shape, lambda g: (0,) * len(shape))
-    line = pl.BlockSpec((pair, width), lambda g: (g, 0))
     return pl.pallas_call(
         functools.partial(grads_kernel, len(sources)),
         grid=(3,),
         in_specs=[
-            whole(rows, full),
-            whole(rows, width),
-            pl.BlockSpec((1, rows, pair), lambda g: (distance, 0, jnp.minimum(g, 1))),
-            pl.BlockSpec((1, rows, pair), lambda g: (distance, 0, 0)),
-        ] * len(sources) + [line] * len(came),
-        out_specs=line,
+            spec
+            for held, dy, dgu, act in sources
+            for spec in (
+                whole(*held.shape),
+                whole(*dy.shape),
+                pl.BlockSpec((1, held.shape[0], pair), lambda g: (distance, 0, jnp.minimum(g, 1))),
+                pl.BlockSpec((1, held.shape[0], pair), lambda g: (distance, 0, 0)),
+            )
+        ],
+        out_specs=pl.BlockSpec((pair, width), lambda g: (g, 0)),
         out_shape=shaped((3 * pair, width), B16),
         compiler_params=params(),
-        cost_estimate=cost(),
-    )(*[v for source in sources for v in source], *came)
+        cost_estimate=cost(11),
+    )(*[v for source in sources for v in source])
+
+
+def sum_of_grads(wholes, pieces):
+    rows, width = wholes[0].shape
+    block = min(width, 512)
+    size = pieces[0].shape[0]
+    count = len(wholes)
+    each = rows // 3
+
+    def kernel(*refs):
+        parts, refs = refs[:count], refs[count:]
+        more, outs = refs[:-3], refs[-3:]
+        for i, piece in enumerate(more):
+            total = piece[...].astype(F32)
+            for part in parts:
+                total = total + part[i * size : (i + 1) * size, :].astype(F32)
+            at = i * size % each
+            outs[i * size // each][at : at + size, :] = total
+
+    line = lambda height: pl.BlockSpec((height, block), lambda g: (0, g))
+    return pl.pallas_call(
+        kernel,
+        grid=(width // block,),
+        in_specs=[line(rows)] * count + [line(size)] * len(pieces),
+        out_specs=[line(each)] * 3,
+        out_shape=[shaped((each, width), F32)] * 3,
+        compiler_params=params(),
+        cost_estimate=cost(8),
+    )(*wholes, *pieces)
 
 
 def per_device(
@@ -729,26 +869,22 @@
     pair = local_experts * hidden
     group = 2 << ((expert_size // 2).bit_length() // 2)
     rounds = expert_size // group
+    own_rows = tok_count // tensor_size
+    everyone = list(range(tensor_size))
     z = tensor_pos.astype(jnp.int32).reshape(1)
 
-    gate_up = {
-        0: jnp.concatenate(
-            [
-                jnp.swapaxes(w_gate, 1, 2).reshape(pair, model_width),
-                jnp.swapaxes(w_up, 1, 2).reshape(pair, model_width),
-            ],
-            axis=0,
-        )
-    }
-    down = {0: w_down.reshape(pair, model_width)}
-    for bit in reversed(range(1, group.bit_length() - 1)):
-        for held in (gate_up, down):
+    weights = [
+        {0: jnp.swapaxes(w_gate, 1, 2).reshape(pair, model_width)},
+        {0: jnp.swapaxes(w_up, 1, 2).reshape(pair, model_width)},
+        {0: w_down.reshape(pair, model_width)},
+    ]
+    for held in weights:
+        for bit in reversed(range(1, group.bit_length() - 1)):
             held.update({d ^ (1 << bit): swap(v, "expert", 1 << bit) for d, v in list(held.items())})
     ids = jnp.concatenate(
         [(expert_pos ^ d) * local_experts + jnp.arange(local_experts) for d in range(group)]
     ).astype(jnp.int32)
     dy_own = lax.all_gather(cotangent, "tensor", axis=1, tiled=True)
-    dy_of = [dy_own] + [swap(dy_own, "expert", group * r) for r in range(1, rounds)]
 
     attention = (
         z, sequence_numbers, tokens, attn_gain, w_query, key_projection, value_projection,
@@ -757,7 +893,13 @@
     branch_parts, kept = attention_forward(*attention, tensor_size)
     first_hidden, attended_low = kept[0], kept[6]
     kept = kept[1:6] + kept[7:]
-    terms = scatter_terms(branch_parts, "tensor")
+    branch_came = exchange_near(branch_parts, "tensor")
+    for d in everyone[2::2]:
+        branch_came[d], weights[0] = together(branch_came[d], weights[0])
+    dy_own = after(dy_own, branch_came[2])
+    dy_of = [dy_own] + [swap(dy_own, "expert", group * r) for r in range(1, rounds)]
+    terms = [branch_parts[0], branch_came[0]] + further_terms(branch_parts, branch_came, "tensor")
+    terms, weights[1] = together(terms, weights[1])
 
     router_rows = jnp.swapaxes(w_router, 0, 1)
     spare = -(2 * experts) % 128
@@ -767,124 +909,226 @@
     middle, packed_rows, shares = route_rows(
         z, terms, tokens, routes, moe_gain, router_rows, experts
     )
-    gate_up = after(gate_up, packed_rows)
-    gate_up.update({d ^ 1: swap(v, "expert", 1) for d, v in list(gate_up.items())})
-    packed_own = {0: packed_rows}
-    packed_of = [{0: swap(packed_rows, "expert", group * r)} for r in range(1, rounds)]
-    for bit in reversed(range(bits_of("tensor"))):
-        came = {d ^ (1 << bit): swap(v, "tensor", 1 << bit) for d, v in packed_own.items()}
-        came = after(came, packed_of)
-        packed_own.update(came)
-        for r in range(1, rounds):
-            packed_of[r - 1].update({d: swap(v, "expert", group * r) for d, v in came.items()})
-    down = after(down, packed_own)
-    down.update({d ^ 1: swap(v, "expert", 1) for d, v in list(down.items())})
-    weights = [(gate_up[d], down[d]) for d in range(group)]
-    packed_of = [[p[d] for d in range(tensor_size)] for p in [packed_own] + packed_of]
-    passes = [expert_pass(z, ids, p, d, weights, experts) for p, d in zip(packed_of, dy_of)]
-    back_parts = [passes[0][0]] + [
-        [swap(v, "expert", group * r) for v in passes[r][0]] for r in range(1, rounds)
+    for i in range(2):
+        weights[i] = after(weights[i], packed_rows)
+        weights[i].update({d ^ 1: swap(v, "expert", 1) for d, v in list(weights[i].items())})
+    packed_of = [{0: packed_rows}] + [
+        {0: swap(packed_rows, "expert", group * r)} for r in range(1, rounds)
     ]
-    joined = [add_low(*several) for several in zip(*back_parts)]
-    joined[0] = None
-    back_terms = [part[0] for part in back_parts] + scatter_terms_of(joined, "tensor")
-
-    sources = [(p[1][0], dy, p[1][1], p[1][2]) for p, dy in zip(passes, dy_of)]
-    odd = {d: expert_grads(d, sources, ()) for d in range(group - 1, 0, -2)}
-    odd = {d: swap(v, "expert", 1) for d, v in odd.items()}
-    sums = {d: expert_grads(d, sources, (odd[d + 1],)) for d in range(group - 2, -1, -2)}
-    local_sums = list(sums.values())
-    mask = 2
-    while mask < group:
-        came = {d: swap(sums[d ^ mask], "expert", mask) for d in sums if not d & mask}
-        sums = {
-            d: sums[d].astype(F32) + v.astype(F32) if mask * 2 == group else add_low(sums[d], v)
-            for d, v in came.items()
+    top = bits_of("tensor") - 1
+    first = {1 << bit: swap(packed_rows, "tensor", 1 << bit) for bit in range(top + 1)}
+    first, weights[2] = together(first, weights[2])
+    weights[2].update({d ^ 1: swap(v, "expert", 1) for d, v in list(weights[2].items())})
+    packed_of[0].update(first)
+    for bit in reversed(range(top)):
+        came = {
+            d | 1 << bit: swap(v, "tensor", 1 << bit)
+            for d, v in packed_of[0].items() if d and not d & ((2 << bit) - 1)
         }
-        mask *= 2
+        packed_of[0].update(after(came, [p[0] for p in packed_of[1:]], dy_of[1:]))
+    for r in range(1, rounds):
+        packed_of[r].update(
+            {d: swap(v, "expert", group * r) for d, v in packed_of[0].items() if d}
+        )
+    weights = [[held[d] for held in weights] for d in range(group)]
+
+    far = [d for d in everyone if d & 1][::-1]
+    near = [d for d in everyone if not d & 1][::-1]
+    back, sources = [], []
+    for r in range(rounds):
+        part, extra = expert_pass(
+            after(z, [b[0] for b in back]), ids, everyone,
+            [packed_of[r][d] for d in everyone], dy_of[r], weights, experts,
+        )
+        if r:
+            part = {d: swap(part[d], "expert", group * r) for d in far + near}
+        back.append(part)
+        sources.append((extra[0], dy_of[r], extra[1], extra[2]))
+
+    downs = [w[2] for w in weights]
+    joined = [None] * tensor_size
+    made, odd, high, passed = {}, {}, {}, {}
+    mask = group // 2
+    outs = expert_outputs(
+        z, middle, [source[3] for source in sources], downs, tensor_size
+    )
+    for place in far:
+        joined[place] = add_low(*after([b[place] for b in back], outs[0]))
+    last = [joined[place] for place in far]
+    for d in range(group - 1, mask - 1, -1):
+        made[d] = expert_grads(d, after(sources, last))
+        last = [made[d]]
+        if d == group - 1:
+            for place in near[:-1]:
+                joined[place] = add_low(*after([b[place] for b in back], last))
+                last = last + [joined[place]]
+    for d in range(group - 1, mask - 1, -2):
+        odd[d - 1] = swap(after(made[d], last), "expert", 1)
+    for d in range(group - 2, mask - 1, -2):
+        mine_all, theirs_all = after([made[d], odd[d]], last)
+        high[d] = [
+            add_low(mine_all[i * hidden : (i + 1) * hidden], theirs_all[i * hidden : (i + 1) * hidden])
+            for i in range(3 * local_experts)
+        ]
+        passed[d - mask] = [swap(v, "expert", mask) for v in high[d]]
+    out_own = outs[:tensor_size]
+    out_came = [
+        {d: swap(outs[r * tensor_size + d], "expert", group * r) for d in far + near}
+        for r in range(1, rounds)
+    ]
+
+    def pieces_at(*places):
+        return [v[i] for v in passed.values() for i in places]
+
+    back_terms = [b[0] for b in back] + scatter_terms_of(joined, "tensor")
     shape = (local_experts, hidden, model_width)
-    gate_grad = jnp.swapaxes(sums[0][:pair].reshape(shape), 1, 2)
-    up_grad = jnp.swapaxes(sums[0][pair : 2 * pair].reshape(shape), 1, 2)
-    down_grad = sums[0][2 * pair :].reshape(shape)
-
-    out_parts = expert_outputs(z, [p[1][2] for p in passes], [w[1] for w in weights], tensor_size)
-
-    back_terms = after(back_terms, local_sums, out_parts)
+
+    back_terms = after(
+        back_terms, last, [came[far[0]] for came in out_came]
+    )
     dbranch, row_sums = rows_back(
         z, back_terms, dy_own, middle, shares, moe_gain, router_rows, experts
     )
-    dbranch_pieces = gather_pieces(dbranch, "tensor")
+    def share_step(small, bit):
+        small = small.reshape((small.shape[0], -1, 2, model_width // expert_size))
+        mine = (expert_pos >> bit) & 1
+        send = lax.dynamic_index_in_dim(small, 1 - mine, 2, False)
+        keep = lax.dynamic_index_in_dim(small, mine, 2, False)
+        return keep, swap(send, "expert", 1 << bit)
+
+    row_share = row_sums[: experts + 1]
+    row_keep, row_came = share_step(row_share, 0)
+    lower = list(range(group // 2 - 1, -1, -1))
+    pieces, last = {0: dbranch}, dbranch
+    for bit in reversed(range(bits_of("tensor"))):
+        came = {d ^ (1 << bit): swap(v, "tensor", 1 << bit) for d, v in pieces.items()}
+        share_lower = -(-len(lower) // bits_of("tensor"))
+        place = bits_of("tensor") - 1 - bit
+        for d in lower[place * share_lower : (place + 1) * share_lower]:
+            made[d] = expert_grads(d, after(sources, last))
+            if d & 1:
+                odd[d - 1] = swap(made[d], "expert", 1)
+            last = made[d]
+        came = after(came, last)
+        if bit:
+            came = after(came, [came_r[far[-1]] for came_r in out_came], pieces_at(0))
+        else:
+            came = after(came, pieces_at(1), [came_r[d] for came_r in out_came for d in near if d])
+        pieces.update(came)
+        last = came
+    dbranch_pieces = [pieces[d] for d in everyone]
+    mine = {d: [made[d], odd[d]] for d in range(0, mask, 2)}
+    theirs = passed
+    while mask > 2:
+        sums = {d: add_low(*v, jnp.concatenate(theirs[d], axis=0)) for d, v in mine.items()}
+        mask //= 2
+        theirs = {
+            d - mask: [
+                swap(sums[d][i * hidden : (i + 1) * hidden], "expert", mask)
+                for i in range(3 * local_experts)
+            ]
+            for d in sums if d >= mask
+        }
+        mine = {d: [sums[d]] for d in sums if d < mask}
+    out_parts = [None] * tensor_size
+    for d in far:
+        came = after([came_r[d] for came_r in out_came], dbranch_pieces)
+        out_parts[d] = add_low(out_own[d], *came)
+    out_far = exchange_near(out_parts, "tensor")
+
     branch_low = jnp.zeros((tok_count, model_width), B16)
     for d, v in enumerate(dbranch_pieces):
         at = (tensor_pos ^ d) * v.shape[0]
         branch_low = lax.dynamic_update_slice_in_dim(branch_low, v, at, 0)
-    out_grad = tn_dot(attended_low, branch_low).astype(B16)
-    dbranch_pieces = after(dbranch_pieces, out_grad)
-    col_parts, (_, low, along, gains) = attention_backward(*attention, kept, dbranch_pieces)
-    col_terms = scatter_terms(col_parts, "tensor")
-    along = sum_everywhere(along, "tensor")
-    width = model_width // tensor_size
-    inputs = tokens.astype(F32)
-    scale = lax.rsqrt(jnp.mean(inputs * inputs, axis=-1, keepdims=True) + EPS)
-
-    def columns(values):
-        return lax.dynamic_slice_in_dim(values, tensor_pos * width, width, values.ndim - 1)
-
-    cols = functools.reduce(jnp.add, [t.astype(F32) for t in col_terms])
-    input_grad = columns(branch_low).astype(F32) + scale * (
-        cols * columns(attn_gain)
-        - columns(inputs) * (scale * scale * (along * (1.0 / model_width)))
-    )
-
-    out_parts = after(out_parts, dbranch_pieces)
-    out_parts = out_parts[:1] + [
-        [swap(v, "expert", group * r) for v in out_parts[r]] for r in range(1, rounds)
-    ]
-    joined = [add_low(*several) for several in zip(*out_parts)]
-    joined[0] = None
-    out_terms = [part[0] for part in out_parts] + scatter_terms_of(joined, "tensor")
-    mixed = functools.reduce(jnp.add, [t.astype(F32) for t in out_terms])
-    block_out = swap_columns((middle + mixed).astype(B16), "tensor")
-
-    def over_experts(values, dim):
-        return lax.psum_scatter(
-            values.astype(B16), "expert", scatter_dimension=dim, tiled=True
-        ).astype(F32)
-
-    out_weight_grad = over_experts(out_grad, 1)
-    qkv = over_experts(tn_dot(first_hidden, low), 0)
+    order = expert_pos ^ jnp.asarray(
+        list(range(1, expert_size, 2)) + list(range(0, expert_size, 2)), jnp.int32
+    )
+    far_bits = list(reversed(range(1, bits_of("expert"))))
+    wo_send, wo_keep = grads_in_blocks(order, branch_low, [attended_low])
+    wo_came = swap(wo_send, "expert", 1)
+    dbranch_pieces = after(dbranch_pieces, wo_keep)
+    branch_low, low_first, *held = attention_backward(*attention, kept, dbranch_pieces, None)
+    wo_keep, wo_send = halves_after(wo_keep, wo_came)
+    held, out_came, out_far, theirs[0][2], wo_send, wo_keep = together(
+        held, out_came, out_far, theirs[0][2], wo_send, wo_keep
+    )
+    wo_came = swap(wo_send, "expert", 1 << far_bits[0])
+    for d in near:
+        if d:
+            out_parts[d] = add_low(out_own[d], *[came_r[d] for came_r in out_came])
+    out_terms = [out_own[0]] + [came_r[0] for came_r in out_came]
+    out_came = out_far
+    out_sums = {d: add_low(out_parts[d], v) if d else None for d, v in out_came.items()}
+    row_keep, row_came = share_step(row_keep + row_came, 1)
+    held = after(held, out_sums)
+    out_terms = out_terms + [out_came[0]] + passed_on(out_sums, "tensor")
+    *cols_out, low_last, row_scale = attention_backward(
+        *attention, kept, None, [branch_low] + held
+    )
+    col_parts = cols_out
+    for bit in range(2, bits_of("expert")):
+        row_keep, row_came = share_step(row_keep + row_came, bit)
+    low_last, theirs[0][3], wo_came, out_terms = together(
+        low_last, theirs[0][3], wo_came, out_terms
+    )
+    row_share = (row_keep + row_came).reshape(experts + 1, -1)
+    for bit in far_bits[1:]:
+        wo_keep, wo_send = halves_after(wo_keep, wo_came)
+        wo_came = swap(wo_send, "expert", 1 << bit)
+    col_came = exchange_near(col_parts, "tensor")
+    q_send, q_keep = grads_in_blocks(order, first_hidden, [low_first, low_last])
+    q_came = swap(q_send, "expert", 1)
+    q_keep, q_send = halves_after(q_keep, q_came)
+    q_came = swap(q_send, "expert", 1 << far_bits[0])
+    col_came = after(col_came, theirs[0][4], q_send)
+    gate_flat, up_flat, down_flat = sum_of_grads(mine[0], theirs[0])
+    gate_grad = jnp.swapaxes(gate_flat.reshape(shape), 1, 2)
+    up_grad = jnp.swapaxes(up_flat.reshape(shape), 1, 2)
+    down_grad = down_flat.reshape(shape)
+    col_terms = [col_parts[0], col_came[0]] + further_terms(col_parts, col_came, "tensor")
+    for bit in far_bits[1:]:
+        q_keep, q_send = halves_after(q_keep, q_came)
+        q_came = swap(q_send, "expert", 1 << bit)
+    out_weight_grad = (wo_keep[0].astype(F32) + wo_came[0].astype(F32)).T
+    col_terms = after(col_terms, q_came, wo_came, gate_flat, row_share)
+    input_grad, small = input_grad_of(z, col_terms, tokens, branch_low, attn_gain, row_scale)
+    gains = small[1 : 1 + tensor_size].reshape(1, model_width)
+    qkv = q_keep[0].astype(F32) + q_came[0].astype(F32)
     q_size = w_query.shape[1]
+
+    def share_of_sum(small):
+        small = small.reshape((small.shape[0],) + (2,) * bits_of("expert") + (-1,))
+        for bit in range(bits_of("expert")):
+            dim = small.ndim - 2
+            mine = (expert_pos >> bit) & 1
+            send = lax.dynamic_index_in_dim(small, 1 - mine, dim, False)
+            keep = lax.dynamic_index_in_dim(small, mine, dim, False)
+            small = keep + swap(send, "expert", 1 << bit)
+        return small
 
     columns_each = model_width // expert_size
     head_each = head_dim // expert_size
     spread = jnp.pad(
-        gains[1:3, :head_dim].reshape(2, expert_size, head_each),
+        small[1 + tensor_size : 3 + tensor_size, :head_dim].reshape(2, expert_size, head_each),
         ((0, 0), (0, 0), (0, columns_each - head_each)),
     )
-    small = jnp.concatenate(
-        [row_sums[: experts + 1], gains[:1], spread.reshape(2, model_width)], axis=0
-    )
-    small = small.reshape((small.shape[0],) + (2,) * bits_of("expert") + (columns_each,))
-    for bit in range(bits_of("expert")):
-        dim = small.ndim - 2
-        mine = (expert_pos >> bit) & 1
-        send = lax.dynamic_index_in_dim(small, 1 - mine, dim, False)
-        keep = lax.dynamic_index_in_dim(small, mine, dim, False)
-        small = keep + swap(send, "expert", 1 << bit)
-    small = sum_everywhere(small, "tensor")
+    small = share_of_sum(jnp.concatenate([gains, spread.reshape(2, model_width)], axis=0))
+    row_share = sum_everywhere(after(row_share, input_grad), "tensor")
+    mixed = functools.reduce(jnp.add, [t.astype(F32) for t in out_terms])
+    block_out = mixed.astype(B16)
 
     return (
         block_out,
         input_grad,
-        small[experts + 1],
+        small[0],
         qkv[:, :q_size],
         qkv[:, q_size : q_size + head_dim],
         qkv[:, q_size + head_dim :],
-        small[experts + 2, :head_each],
-        small[experts + 3, :head_each],
+        small[1, :head_each],
+        small[2, :head_each],
         out_weight_grad,
-        small[experts],
-        jnp.swapaxes(small[:experts], 0, 1),
+        row_share[experts],
+        jnp.swapaxes(row_share[:experts], 0, 1),
         gate_grad,
         up_grad,
         down_grad,

time: 611 us -> 521 us (0.85)
  waiting for transfers between devices: 289 us -> 183 us
  Pallas kernels: 183 us -> 215 us
  matrix products: 11.7 us -> 0 us
  local copies, waits for them, and re-layouts: 23.8 us -> 17.1 us
    ppermute x50 -> x62, waiting for transfers between devices: 289 us -> 182 us  [swap(): return lax.ppermute(values, axis, [(i, i ^ mask) for i in range(count)])]
    pallas_call x3 -> x8, Pallas kernels: 91.5 us -> 124 us  [the longest x2 63.2 us: expert_pass(): pl.pallas_call(functools.partial(expert_kernel, tuple(places), group, slo...]
    convert_element_type x8 -> x13, other arithmetic: 3.45 us -> 20.5 us  [add_low(): functools.reduce(jnp.add, [v.astype(F32) for v in values]).astype(B16)]
    dot_general x2 -> x0, matrix products: 11.7 us -> none  [tn_dot(): lax.dot_general(left, right, (((0,), (0,)), ((), ())), preferred_element_...]
    ppermute x50 -> x62, starting transfers between devices: 59.5 us -> 56.6 us  [swap(): return lax.ppermute(values, axis, [(i, i ^ mask) for i in range(count)])]
  transfers between devices with their start and end apart: 53 -> 63, of which waited for: 27 -> 29; matrix products, arithmetic and copies ran while one was open for 6% -> 7% of each run, Pallas kernels for 23% -> 30%
where the time goes in v3:
time: 521 us; the launch traced here: 516 us
  Pallas kernels  215 us (41%)
  waiting for transfers between devices  183 us (35%)
  starting transfers between devices  56.6 us (11%)
  other arithmetic  28.7 us (6%)
  local copies, waits for them, and re-layouts  17.1 us (3%)
  between operations  15.2 us (3%)
    ppermute x62, waiting for transfers between devices, swap(): return lax.ppermute(values, axis, [(i, i ^ mask) for i in range(count)])  182 us
    pallas_call x2, Pallas kernels, expert_pass(): pl.pallas_call(functools.partial(expert_kernel, tuple(places), group, slo...  63.2 us
    ppermute x62, starting transfers between devices, swap(): return lax.ppermute(values, axis, [(i, i ^ mask) for i in range(count)])  56.6 us
    pallas_call x4, Pallas kernels, expert_grads(): pl.pallas_call(functools.partial(grads_kernel, len(sources)), grid=(3,),...  43.3 us
    pallas_call x2, Pallas kernels, attention_backward(): pl.pallas_call(functools.partial(backward_kernel, min(rows, 256), parts,...  35.7 us
    pallas_call x1, Pallas kernels, attention_forward(): pl.pallas_call(functools.partial(forward_kernel, min(rows, 256)), grid_sp...  25.9 us
    convert_element_type x13, other arithmetic, add_low(): functools.reduce(jnp.add, [v.astype(F32) for v in values]).astype(B16)  20.5 us
    pallas_call x1, Pallas kernels, expert_outputs(): pl.pallas_call(functools.partial(outputs_kernel, parts, len(acts), group)...  14.5 us
  transfers between devices with their start and end apart: 63, of which 29 were waited for; matrix products, arithmetic and copies ran while one was open for 7% of the time, Pallas kernels for 30%

profile of v3, /device:TPU:0, one launch (start us, length us, event | category | flops | bytes accessed | tf_op | source)
XLA Modules:
  0.0 516.2 jit_solution(12910622510125361406)
XLA Ops:
  12.5 25.9 %shard_map.281 = (bf16[128,2048]{1,0:T(8,128)(2,1)}, bf16[128,2048]{1,0:T(8,128)(2,1)}, bf16[128,2048]{1,0:T(8,128)(2,1)}, bf16[128,2048]{1,0:T(8,128)(2,1)}, bf...) custom-call(s32[1]{0:T(128)} %bitcast.z_ref.refs_0_, ...), custom_call_target="tpu_custom_call" | custom-call | bytes 280800000 | tf_op jit(solution)/shard_map/pallas_call | solution.py:221
  42.5 25.4 %collective-permute-done.1 = bf16[128,2048]{1,0:T(8,128)(2,1)S(1)} collective-permute-done((bf16[128,2048]{1,0:T(8,128)(2,1)}, bf16[128,2048]{1,0:T(8,128)(2,1)S(1)}, u32[]{:S(2)}, u32[]{:S(2)}) %collective-permute-start.1) | collective-permute-done | bytes 524320 | tf_op jit(solution)/shard_map/ppermute | solution.py:19
  74.2 11.9 %collective-permute-done.refs_1_ = bf16[128,2048]{1,0:T(8,128)(2,1)S(1)} collective-permute-done((bf16[128,2048]{1,0:T(8,128)(2,1)}, bf16[128,2048]{1,0:T(8,128)(2,1)S(1)}, u32[]{:S(2)}, u32[]{:S(2)}) %collective-permute-start) | collective-permute-done | bytes 524320 | tf_op jit(solution)/shard_map/ppermute | solution.py:19
  86.1 10.1 %collective-permute-done.3.refs_2_ = bf16[128,2048]{1,0:T(8,128)(2,1)S(1)} collective-permute-done((bf16[128,2048]{1,0:T(8,128)(2,1)}, bf16[128,2048]{1,0:T(8,128)(2,1)S(1)}, u32[]{:S(2)}, u32[]{:S(2)}) %collective-permute-start.3) | collective-permute-done | bytes 524320 | tf_op jit(solution)/shard_map/ppermute | solution.py:19
  97.0 3.5 shard_map.282
  103.4 9.6 %collective-permute-done.7.refs_15_.refs_4_ = bf16[384,2048]{1,0:T(8,128)(2,1)} collective-permute-done((bf16[384,2048]{1,0:T(8,128)(2,1)}, bf16[384,2048]{1,0:T(8,128)(2,1)}, u32[]{:S(2)}, u32[]{:S(2)}) %collective-permute-start.7) | collective-permute-done | bytes 1572896 | tf_op jit(solution)/shard_map/ppermute | solution.py:19
  114.8 10.9 %collective-permute-done.5.refs_3_ = bf16[128,2176]{1,0:T(8,128)(2,1)S(1)} collective-permute-done((bf16[128,2176]{1,0:T(8,128)(2,1)}, bf16[128,2176]{1,0:T(8,128)(2,1)S(1)}, u32[]{:S(2)}, u32[]{:S(2)}) %collective-permute-start.5) | collective-permute-done | bytes 557088 | tf_op jit(solution)/shard_map/ppermute | solution.py:19
  130.8 8.9 %collective-permute-done.8.refs_5_ = bf16[128,2176]{1,0:T(8,128)(2,1)} collective-permute-done((bf16[128,2176]{1,0:T(8,128)(2,1)}, bf16[128,2176]{1,0:T(8,128)(2,1)}, u32[]{:S(2)}, u32[]{:S(2)}) %collective-permute-start.8) | collective-permute-done | bytes 557088 | tf_op jit(solution)/shard_map/ppermute | solution.py:19
  148.0 31.4 %shard_map.283 = (bf16[128,2176]{1,0:T(8,128)(2,1)}, bf16[128,2176]{1,0:T(8,128)(2,1)}, bf16[128,2176]{1,0:T(8,128)(2,1)}, bf16[128,2176]{1,0:T(8,128)(2,1)}, bf...) custom-call(s32[1]{0:T(128)} %bitcast.z_ref.refs_0_, s32[8]{0:T(128)} %pad_add_fusion.refs_1_, ...), custom_call_target="tpu_custom_call" | custom-call | bytes 334800000 | tf_op jit(solution)/shard_map/pallas_call | solution.py:716
  179.5 31.9 %shard_map.284 = (bf16[128,2176]{1,0:T(8,128)(2,1)}, bf16[128,2176]{1,0:T(8,128)(2,1)}, bf16[128,2176]{1,0:T(8,128)(2,1)}, bf16[128,2176]{1,0:T(8,128)(2,1)}, bf...) custom-call(s32[1]{0:T(128)} %bitcast.z_ref.refs_0_, s32[8]{0:T(128)} %pad_add_fusion.refs_1_, ...), custom_call_target="tpu_custom_call" | custom-call | bytes 334800000 | tf_op jit(solution)/shard_map/pallas_call | solution.py:716
  214.3 14.5 %shard_map.285 = (bf16[512,512]{1,0:T(8,128)(2,1)}, bf16[512,512]{1,0:T(8,128)(2,1)}, bf16[512,512]{1,0:T(8,128)(2,1)}, bf16[512,512]{1,0:T(8,128)(2,1)}, bf16[5...) custom-call(s32[1]{0:T(128)} %bitcast.z_ref.refs_0_, ...), custom_call_target="tpu_custom_call" | custom-call | bytes 108000000 | tf_op jit(solution)/shard_map/pallas_call | solution.py:761
  228.7 10.3 %collective-permute-done.21 = bf16[128,2176]{1,0:T(8,128)(2,1)S(1)} collective-permute-done((bf16[128,2176]{1,0:T(8,128)(2,1)}, bf16[128,2176]{1,0:T(8,128)(2,1)S(1)}, u32[]{:S(2)}, u32[]{:S(2)}) %collective-permute-start.21) | collective-permute-done | bytes 557088 | tf_op jit(solution)/shard_map/ppermute | solution.py:19
  240.0 10.8 %shard_map.286 = bf16[1152,2048]{1,0:T(8,128)(2,1)} custom-call(bf16[512,2176]{1,0:T(8,128)(2,1)} %get-tuple-element.268.refs_0_, bf16[512,2048]{1,0:T(8,128)(2,1)} %all-gather.2.cloned.1.call-done.refs_6_.refs_1_.refs_4_, bf16[4,512,768]{2,1,0:T(8,128)(2,1)} %get-tuple-element.270.refs_2_, bf16[4,512,384]{2,1,0:T(8,128)(2,1)} %get-tuple-element.271.refs_0_.refs_3_, ...), custom_call_target="tpu_custom_call" | custom-call | bytes 118800000 | tf_op jit(solution)/shard_map/pallas_call | solution.py:794
  252.4 11.0 %shard_map.287 = bf16[1152,2048]{1,0:T(8,128)(2,1)} custom-call(bf16[512,2176]{1,0:T(8,128)(2,1)} %get-tuple-element.268.refs_0_, bf16[512,2048]{1,0:T(8,128)(2,1)} %all-gather.2.cloned.1.call-done.refs_6_.refs_1_.refs_4_, bf16[4,512,768]{2,1,0:T(8,128)(2,1)} %get-tuple-element.270.refs_2_, bf16[4,512,384]{2,1,0:T(8,128)(2,1)} %get-tuple-element.271.refs_0_.refs_3_, ...), custom_call_target="tpu_custom_call" | custom-call | bytes 118800000 | tf_op jit(solution)/shard_map/pallas_call | solution.py:794
  267.8 3.6 collective-permute-done.31
  271.4 4.2 add_convert_fusion.4
  278.5 11.5 %collective-permute-done.20.refs_1_ = bf16[128,2176]{1,0:T(8,128)(2,1)S(1)} collective-permute-done((bf16[128,2176]{1,0:T(8,128)(2,1)S(1)}, bf16[128,2176]{1,0:T(8,128)(2,1)S(1)}, u32[]{:S(2)}, u32[]{:S(2)}) %collective-permute-start.20) | collective-permute-done | bytes 557088 | tf_op jit(solution)/shard_map/ppermute | solution.py:19
  294.0 4.1 shard_map.288
  302.8 10.7 %shard_map.289 = bf16[1152,2048]{1,0:T(8,128)(2,1)} custom-call(bf16[512,2176]{1,0:T(8,128)(2,1)} %get-tuple-element.268.refs_0_, bf16[512,2048]{1,0:T(8,128)(2,1)} %all-gather.2.cloned.1.call-done.refs_6_.refs_1_.refs_4_, bf16[4,512,768]{2,1,0:T(8,128)(2,1)} %get-tuple-element.270.refs_2_, bf16[4,512,384]{2,1,0:T(8,128)(2,1)} %get-tuple-element.271.refs_0_.refs_3_, ...), custom_call_target="tpu_custom_call" | custom-call | bytes 118800000 | tf_op jit(solution)/shard_map/pallas_call | solution.py:794
  313.5 7.9 %collective-permute-done.29.refs_2_ = bf16[128,2048]{1,0:T(8,128)(2,1)S(1)} collective-permute-done((bf16[128,2048]{1,0:T(8,128)(2,1)}, bf16[128,2048]{1,0:T(8,128)(2,1)S(1)}, u32[]{:S(2)}, u32[]{:S(2)}) %collective-permute-start.29) | collective-permute-done | bytes 524320 | tf_op jit(solution)/shard_map/ppermute | solution.py:19
  324.3 10.9 %shard_map.290.refs_0_ = bf16[1152,2048]{1,0:T(8,128)(2,1)} custom-call(bf16[512,2176]{1,0:T(8,128)(2,1)} %get-tuple-element.268.refs_0_, bf16[512,2048]{1,0:T(8,128)(2,1)} %all-gather.2.cloned.1.call-done.refs_6_.refs_1_.refs_4_, bf16[4,512,768]{2,1,0:T(8,128)(2,1)} %get-tuple-element.270.refs_2_, bf16[4,512,384]{2,1,0:T(8,128)(2,1)} %get-tuple-element.271.refs_0_.refs_3_, ...), custom_call_target="tpu_custom_call" | custom-call | bytes 118800000 | tf_op jit(solution)/shard_map/pallas_call | solution.py:794
  337.9 5.7 %shard_map.291 = (bf16[4,256,1024]{2,1,0:T(8,128)(2,1)}, bf16[4,256,1024]{2,1,0:T(8,128)(2,1)}) custom-call(s32[8]{0:T(128)} %broadcast_xor_fusion.order_ref, bf16[512,2048]{1,0:T(8,128)(2,1)} %copy-done.1, bf16[512,1024]{1,0:T(8,128)(2,1)} %get-tuple-element.281.refs_0_), custom_call_target="tpu_custom_call" | custom-call | bytes 64800000 | tf_op jit(solution)/shard_map/pallas_call | solution.py:453
  350.1 15.0 %shard_map.292 = (bf16[512,2048]{1,0:T(8,128)(2,1)}, bf16[512,512]{1,0:T(8,128)(2,1)}, f32[512,2048]{1,0:T(8,128)}, f32[512,128]{1,0:T(8,128)}, f32[512,128]{1,0:T(8,128)}, /*index=5*/f32[8,2048]{1,0:T(8,128)}) custom-call(s32[1]{0:T(128)} %bitcast.z_ref.refs_0_, s32[512,1]{1,0:T(8,128)} %copy.43.seq_col, s32[1,512]{1,0:T(1,128)} %bitcast.90, ...), custom_call_target="tpu_custom_call" | custom-call | bytes 172800000 | tf_op jit(solution)/shard_map/pallas_call | solution.py:411
  366.2 6.2 %collective-permute-done.37 = bf16[512,512]{1,0:T(8,128)(2,1)} collective-permute-done((bf16[512,512]{1,0:T(8,128)(2,1)}, bf16[512,512]{1,0:T(8,128)(2,1)}, u32[]{:S(2)}, u32[]{:S(2)}) %collective-permute-start.37) | collective-permute-done | bytes 524320 | tf_op jit(solution)/shard_map/ppermute | solution.py:19
  378.6 20.7 %shard_map.293 = (bf16[528,512]{1,0:T(8,128)(2,1)}, bf16[528,512]{1,0:T(8,128)(2,1)}, bf16[528,512]{1,0:T(8,128)(2,1)}, bf16[528,512]{1,0:T(8,128)(2,1)}, bf16[512,768]{1,0:T(8,128)(2,1)}, /*index=5*/f32[512,1]{1,0:T(8,128)}) custom-call(s32[1]{0:T(128)} %bitcast.z_ref.refs_0_, s32[512,1]{1,0:T(8,128)} %copy.43.seq_col, s32[1,512]{1,0:T(1,128)} %bitcast.91, ...), custom_call_target="tpu_custom_call" | custom-call | bytes 172800000 | tf_op jit(solution)/shard_map/pallas_call | solution.py:411
  400.4 7.0 %shard_map.294 = (bf16[4,256,1280]{2,1,0:T(8,128)(2,1)}, bf16[4,256,1280]{2,1,0:T(8,128)(2,1)}) custom-call(s32[8]{0:T(128)} %broadcast_xor_fusion.order_ref, bf16[512,2048]{1,0:T(8,128)(2,1)} %get-tuple-element.321.left_ref, bf16[512,512]{1,0:T(8,128)(2,1)} %get-tuple-element.322.refs_0_, bf16[512,768]{1,0:T(8,128)(2,1)} %get-tuple-element.323.refs_1_), custom_call_target="tpu_custom_call" | custom-call | bytes 64800000 | tf_op jit(solution)/shard_map/pallas_call | solution.py:453
  408.0 4.6 collective-permute-done.47
  412.6 4.2 add_convert_fusion
  422.4 17.1 %collective-permute-done.55 = f32[17,2,256]{2,1,0:T(2,128)S(1)} collective-permute-done((f32[17,2,256]{2,1,0:T(2,128)S(1)}, f32[17,2,256]{2,1,0:T(2,128)S(1)}, u32[]{:S(2)}, u32[]{:S(2)}) %collective-permute-start.55) | collective-permute-done | bytes 34848 | tf_op jit(solution)/shard_map/ppermute | solution.py:19
  442.1 11.7 %collective-permute-done.45 = bf16[528,512]{1,0:T(8,128)(2,1)} collective-permute-done((bf16[528,512]{1,0:T(8,128)(2,1)}, bf16[528,512]{1,0:T(8,128)(2,1)}, u32[]{:S(2)}, u32[]{:S(2)}) %collective-permute-start.45) | collective-permute-done | bytes 540704 | tf_op jit(solution)/shard_map/ppermute | solution.py:19
  462.3 8.9 %shard_map.295 = (f32[384,2048]{1,0:T(8,128)}, f32[384,2048]{1,0:T(8,128)}, f32[384,2048]{1,0:T(8,128)}) custom-call(bf16[1152,2048]{1,0:T(8,128)(2,1)} %shard_map.290.refs_0_, bf16[1152,2048]{1,0:T(8,128)(2,1)} %collective-permute-done.52.refs_1_, bf16[192,2048]{1,0:T(8,128)(2,1)} %collective-permute-done.32.refs_2_, bf16[192,2048]{1,0:T(8,128)(2,1)} %copy-done.16, ...), custom_call_target="tpu_custom_call" | custom-call | bytes 86400000 | tf_op jit(solution)/shard_map/pallas_call | solution.py:832
  473.5 12.7 %collective-permute-done.51 = bf16[1,256,1024]{2,1,0:T(8,128)(2,1)S(1)} collective-permute-done((bf16[1,256,1024]{2,1,0:T(8,128)(2,1)}, bf16[1,256,1024]{2,1,0:T(8,128)(2,1)S(1)}, u32[]{:S(2)}, u32[]{:S(2)}) %collective-permute-start.51) | collective-permute-done | bytes 524320 | tf_op jit(solution)/shard_map/ppermute | solution.py:19
  (279 shorter events, 118.2 us)
Async XLA Ops:
  7.2 64.6 %all-gather.2.cloned.1.call-start = ((), (), s32[]{:S(2)}) async-start(), calls=%async_computation | async-start | bytes 2621440 | tf_op jit(solution)/shard_map/all_gather | solution.py:887
  7.9 60.0 %collective-permute-start.2 = (bf16[384,2048]{1,0:T(8,128)(2,1)}, bf16[384,2048]{1,0:T(8,128)(2,1)S(1)}, u32[]{:S(2)}, u32[]{:S(2)}) collective-permute-start(bf16[384,2048]{1,0:T(8,128)(2,1)} %bitcast.66), channel_id=1, source_target_pairs={{0,8},{4,12},{8,0},{12,4},{16,24},{20,28},{24,16},{28,20},{1,9},{5... | collective-permute-start | bytes 4718600 | tf_op jit(solution)/shard_map/ppermute | solution.py:19
  10.9 75.2 %collective-permute-start.4 = (bf16[384,2048]{1,0:T(8,128)(2,1)}, bf16[384,2048]{1,0:T(8,128)(2,1)}, u32[]{:S(2)}, u32[]{:S(2)}) collective-permute-start(bf16[384,2048]{1,0:T(8,128)(2,1)} %bitcast.70), channel_id=1, source_target_pairs={{0,8},{4,12},{8,0},{12,4},{16,24},{20,28},{24,16},{28,20},{1,9},{5... | collective-permute-start | bytes 4718600 | tf_op jit(solution)/shard_map/ppermute | solution.py:19
  38.5 29.4 %collective-permute-start.1 = (bf16[128,2048]{1,0:T(8,128)(2,1)}, bf16[128,2048]{1,0:T(8,128)(2,1)S(1)}, u32[]{:S(2)}, u32[]{:S(2)}) collective-permute-start(bf16[128,2048]{1,0:T(8,128)(2,1)} %get-tuple-element.188), channel_id=1, source_target_pairs={{0,1},{1,0},{2,3},{3,2},{4,5},{5,4},{6,7},{7,6},{8,9},{9,8},{10,11... | collective-permute-start | bytes 1572872 | tf_op jit(solution)/shard_map/ppermute | solution.py:19
  40.6 72.5 %collective-permute-start.7 = (bf16[384,2048]{1,0:T(8,128)(2,1)}, bf16[384,2048]{1,0:T(8,128)(2,1)}, u32[]{:S(2)}, u32[]{:S(2)}) collective-permute-start(bf16[384,2048]{1,0:T(8,128)(2,1)} %bitcast.14.refs_9_.refs_2_), channel_id=1, source_target_pairs={{0,8},{4,12},{8,0},{12,4},{16,24},{20,28},{24,16},{28,20},{1,9},{5... | collective-permute-start | bytes 4718600 | tf_op jit(solution)/shard_map/ppermute | solution.py:19
  42.1 44.0 %collective-permute-start = (bf16[128,2048]{1,0:T(8,128)(2,1)}, bf16[128,2048]{1,0:T(8,128)(2,1)S(1)}, u32[]{:S(2)}, u32[]{:S(2)}) collective-permute-start(bf16[128,2048]{1,0:T(8,128)(2,1)} %get-tuple-element.186), channel_id=1, source_target_pairs={{0,1},{1,0},{2,3},{3,2},{4,5},{5,4},{6,7},{7,6},{8,9},{9,8},{10,11... | collective-permute-start | bytes 1572872 | tf_op jit(solution)/shard_map/ppermute | solution.py:19
  70.2 25.9 %collective-permute-start.3 = (bf16[128,2048]{1,0:T(8,128)(2,1)}, bf16[128,2048]{1,0:T(8,128)(2,1)S(1)}, u32[]{:S(2)}, u32[]{:S(2)}) collective-permute-start(bf16[128,2048]{1,0:T(8,128)(2,1)} %add_convert_fusion.24), channel_id=1, source_target_pairs={{0,2},{1,3},{2,0},{3,1},{4,6},{5,7},{6,4},{7,5},{8,10},{9,11},{10,... | collective-permute-start | bytes 1572872 | tf_op jit(solution)/shard_map/ppermute | solution.py:19
  71.8 68.5 %collective-permute-start.10 = (bf16[512,2048]{1,0:T(8,128)(2,1)}, bf16[512,2048]{1,0:T(8,128)(2,1)S(1)}, u32[]{:S(2)}, u32[]{:S(2)}) collective-permute-start(bf16[512,2048]{1,0:T(8,128)(2,1)} %all-gather.2.cloned.1.call-done.refs_6_.refs_1_.refs_4_), channel_id=1, source_target_pairs={{0,16},{4,20},{8,24},{12,28},{16,0},{20,4},{24,8},{28,12},{1,17},{... | collective-permute-start | bytes 6291464 | tf_op jit(solution)/shard_map/ppermute | solution.py:19
  100.5 25.2 %collective-permute-start.5 = (bf16[128,2176]{1,0:T(8,128)(2,1)}, bf16[128,2176]{1,0:T(8,128)(2,1)S(1)}, u32[]{:S(2)}, u32[]{:S(2)}) collective-permute-start(bf16[128,2176]{1,0:T(8,128)(2,1)} %get-tuple-element.193.refs_2_), channel_id=1, source_target_pairs={{0,1},{1,0},{2,3},{3,2},{4,5},{5,4},{6,7},{7,6},{8,9},{9,8},{10,11... | collective-permute-start | bytes 1671176 | tf_op jit(solution)/shard_map/ppermute | solution.py:19
  100.5 26.6 %collective-permute-start.6 = (bf16[128,2176]{1,0:T(8,128)(2,1)}, bf16[128,2176]{1,0:T(8,128)(2,1)}, u32[]{:S(2)}, u32[]{:S(2)}) collective-permute-start(bf16[128,2176]{1,0:T(8,128)(2,1)} %get-tuple-element.193.refs_2_), channel_id=1, source_target_pairs={{0,2},{1,3},{2,0},{3,1},{4,6},{5,7},{6,4},{7,5},{8,10},{9,11},{10,... | collective-permute-start | bytes 1671176 | tf_op jit(solution)/shard_map/ppermute | solution.py:19
  103.4 36.3 %collective-permute-start.12 = (bf16[384,2048]{1,0:T(8,128)(2,1)S(1)}, bf16[384,2048]{1,0:T(8,128)(2,1)S(1)}, u32[]{:S(2)}, u32[]{:S(2)}) collective-permute-start(bf16[384,2048]{1,0:T(8,128)(2,1)S(1)} %bitcast.73), channel_id=1, source_target_pairs={{0,4},{4,0},{8,12},{12,8},{16,20},{20,16},{24,28},{28,24},{1,5},{5... | collective-permute-start | bytes 4718600 | tf_op jit(solution)/shard_map/ppermute | solution.py:19
  140.3 39.0 %collective-permute-start.18 = (bf16[128,2176]{1,0:T(8,128)(2,1)}, bf16[128,2176]{1,0:T(8,128)(2,1)}, u32[]{:S(2)}, u32[]{:S(2)}) collective-permute-start(bf16[128,2176]{1,0:T(8,128)(2,1)} %collective-permute-done.6.refs_4_), channel_id=1, source_target_pairs={{0,16},{4,20},{8,24},{12,28},{16,0},{20,4},{24,8},{28,12},{1,17},{... | collective-permute-start | bytes 1671176 | tf_op jit(solution)/shard_map/ppermute | solution.py:19
  141.1 38.2 %collective-permute-start.17 = (bf16[128,2176]{1,0:T(8,128)(2,1)S(1)}, bf16[128,2176]{1,0:T(8,128)(2,1)}, u32[]{:S(2)}, u32[]{:S(2)}) collective-permute-start(bf16[128,2176]{1,0:T(8,128)(2,1)S(1)} %collective-permute-done.5.refs_3_), channel_id=1, source_target_pairs={{0,16},{4,20},{8,24},{12,28},{16,0},{20,4},{24,8},{28,12},{1,17},{... | collective-permute-start | bytes 1671176 | tf_op jit(solution)/shard_map/ppermute | solution.py:19
  145.7 33.8 %collective-permute-start.19 = (bf16[128,2176]{1,0:T(8,128)(2,1)}, bf16[128,2176]{1,0:T(8,128)(2,1)}, u32[]{:S(2)}, u32[]{:S(2)}) collective-permute-start(bf16[128,2176]{1,0:T(8,128)(2,1)} %collective-permute-done.8.refs_5_), channel_id=1, source_target_pairs={{0,16},{4,20},{8,24},{12,28},{16,0},{20,4},{24,8},{28,12},{1,17},{... | collective-permute-start | bytes 1671176 | tf_op jit(solution)/shard_map/ppermute | solution.py:19
  212.2 26.8 %collective-permute-start.21 = (bf16[128,2176]{1,0:T(8,128)(2,1)}, bf16[128,2176]{1,0:T(8,128)(2,1)S(1)}, u32[]{:S(2)}, u32[]{:S(2)}) collective-permute-start(bf16[128,2176]{1,0:T(8,128)(2,1)} %get-tuple-element.212), channel_id=1, source_target_pairs={{0,16},{4,20},{8,24},{12,28},{16,0},{20,4},{24,8},{28,12},{1,17},{... | collective-permute-start | bytes 1671176 | tf_op jit(solution)/shard_map/ppermute | solution.py:19
  213.5 37.3 %collective-permute-start.23 = (bf16[128,2176]{1,0:T(8,128)(2,1)}, bf16[128,2176]{1,0:T(8,128)(2,1)S(1)}, u32[]{:S(2)}, u32[]{:S(2)}) collective-permute-start(bf16[128,2176]{1,0:T(8,128)(2,1)} %get-tuple-element.220), channel_id=1, source_target_pairs={{0,16},{4,20},{8,24},{12,28},{16,0},{20,4},{24,8},{28,12},{1,17},{... | collective-permute-start | bytes 1671176 | tf_op jit(solution)/shard_map/ppermute | solution.py:19
  264.4 25.6 %collective-permute-start.20 = (bf16[128,2176]{1,0:T(8,128)(2,1)S(1)}, bf16[128,2176]{1,0:T(8,128)(2,1)S(1)}, u32[]{:S(2)}, u32[]{:S(2)}) collective-permute-start(bf16[128,2176]{1,0:T(8,128)(2,1)S(1)} %copy-done.46), channel_id=1, source_target_pairs={{0,16},{4,20},{8,24},{12,28},{16,0},{20,4},{24,8},{28,12},{1,17},{... | collective-permute-start | bytes 1671176 | tf_op jit(solution)/shard_map/ppermute | solution.py:19
  265.6 25.4 %collective-permute-start.22 = (bf16[128,2176]{1,0:T(8,128)(2,1)S(1)}, bf16[128,2176]{1,0:T(8,128)(2,1)S(1)}, u32[]{:S(2)}, u32[]{:S(2)}) collective-permute-start(bf16[128,2176]{1,0:T(8,128)(2,1)S(1)} %add_convert_fusion.15), channel_id=1, source_target_pairs={{0,1},{1,0},{2,3},{3,2},{4,5},{5,4},{6,7},{7,6},{8,9},{9,8},{10,11... | collective-permute-start | bytes 1671176 | tf_op jit(solution)/shard_map/ppermute | solution.py:19
  266.2 27.0 %collective-permute-start.26 = (bf16[128,2176]{1,0:T(8,128)(2,1)S(1)}, bf16[128,2176]{1,0:T(8,128)(2,1)S(1)}, u32[]{:S(2)}, u32[]{:S(2)}) collective-permute-start(bf16[128,2176]{1,0:T(8,128)(2,1)S(1)} %add_convert_fusion.12), channel_id=1, source_target_pairs={{0,2},{1,3},{2,0},{3,1},{4,6},{5,7},{6,4},{7,5},{8,10},{9,11},{10,... | collective-permute-start | bytes 1671176 | tf_op jit(solution)/shard_map/ppermute | solution.py:19
  275.6 46.6 %collective-permute-start.32 = (bf16[192,2048]{1,0:T(8,128)(2,1)S(1)}, bf16[192,2048]{1,0:T(8,128)(2,1)}, u32[]{:S(2)}, u32[]{:S(2)}) collective-permute-start(bf16[192,2048]{1,0:T(8,128)(2,1)S(1)} %get-tuple-element.393), channel_id=1, source_target_pairs={{0,8},{4,12},{8,0},{12,4},{16,24},{20,28},{24,16},{28,20},{1,9},{5... | collective-permute-start | bytes 2359304 | tf_op jit(solution)/shard_map/ppermute | solution.py:19
  298.1 23.3 %collective-permute-start.29 = (bf16[128,2048]{1,0:T(8,128)(2,1)}, bf16[128,2048]{1,0:T(8,128)(2,1)S(1)}, u32[]{:S(2)}, u32[]{:S(2)}) collective-permute-start(bf16[128,2048]{1,0:T(8,128)(2,1)} %get-tuple-element.283.refs_0_), channel_id=1, source_target_pairs={{0,2},{1,3},{2,0},{3,1},{4,6},{5,7},{6,4},{7,5},{8,10},{9,11},{10,... | collective-permute-start | bytes 1572872 | tf_op jit(solution)/shard_map/ppermute | solution.py:19
  298.4 23.0 %collective-permute-start.30 = (bf16[512,512]{1,0:T(8,128)(2,1)S(1)}, bf16[512,512]{1,0:T(8,128)(2,1)S(1)}, u32[]{:S(2)}, u32[]{:S(2)}) collective-permute-start(bf16[512,512]{1,0:T(8,128)(2,1)S(1)} %copy-done.47), channel_id=1, source_target_pairs={{0,16},{4,20},{8,24},{12,28},{16,0},{20,4},{24,8},{28,12},{1,17},{... | collective-permute-start | bytes 1572872 | tf_op jit(solution)/shard_map/ppermute | solution.py:19
  299.8 35.5 %collective-permute-start.34 = (bf16[192,2048]{1,0:T(8,128)(2,1)}, bf16[192,2048]{1,0:T(8,128)(2,1)S(1)}, u32[]{:S(2)}, u32[]{:S(2)}) collective-permute-start(bf16[192,2048]{1,0:T(8,128)(2,1)} %get-tuple-element.392), channel_id=1, source_target_pairs={{0,8},{4,12},{8,0},{12,4},{16,24},{20,28},{24,16},{28,20},{1,9},{5... | collective-permute-start | bytes 2359304 | tf_op jit(solution)/shard_map/ppermute | solution.py:19
  301.2 33.9 %collective-permute-start.28 = (bf16[128,2048]{1,0:T(8,128)(2,1)}, bf16[128,2048]{1,0:T(8,128)(2,1)S(1)}, u32[]{:S(2)}, u32[]{:S(2)}) collective-permute-start(bf16[128,2048]{1,0:T(8,128)(2,1)} %get-tuple-element.283.refs_0_), channel_id=1, source_target_pairs={{0,1},{1,0},{2,3},{3,2},{4,5},{5,4},{6,7},{7,6},{8,9},{9,8},{10,11... | collective-permute-start | bytes 1572872 | tf_op jit(solution)/shard_map/ppermute | solution.py:19
  372.4 28.0 %collective-permute-start.42 = (bf16[2,256,1024]{2,1,0:T(8,128)(2,1)S(1)}, bf16[2,256,1024]{2,1,0:T(8,128)(2,1)S(1)}, u32[]{:S(2)}, u32[]{:S(2)}) collective-permute-start(bf16[2,256,1024]{2,1,0:T(8,128)(2,1)S(1)} %get-tuple-element.311), channel_id=1, source_target_pairs={{0,16},{4,20},{8,24},{12,28},{16,0},{20,4},{24,8},{28,12},{1,17},{... | collective-permute-start | bytes 3145736 | tf_op jit(solution)/shard_map/ppermute | solution.py:19
  373.4 25.9 %collective-permute-start.41 = (bf16[192,2048]{1,0:T(8,128)(2,1)}, bf16[192,2048]{1,0:T(8,128)(2,1)S(1)}, u32[]{:S(2)}, u32[]{:S(2)}) collective-permute-start(bf16[192,2048]{1,0:T(8,128)(2,1)} %get-tuple-element.390), channel_id=1, source_target_pairs={{0,8},{4,12},{8,0},{12,4},{16,24},{20,28},{24,16},{28,20},{1,9},{5... | collective-permute-start | bytes 2359304 | tf_op jit(solution)/shard_map/ppermute | solution.py:19
  375.2 25.1 %collective-permute-start.43 = (bf16[512,512]{1,0:T(8,128)(2,1)S(1)}, bf16[512,512]{1,0:T(8,128)(2,1)S(1)}, u32[]{:S(2)}, u32[]{:S(2)}) collective-permute-start(bf16[512,512]{1,0:T(8,128)(2,1)S(1)} %add_convert_fusion.20), channel_id=1, source_target_pairs={{0,2},{1,3},{2,0},{3,1},{4,6},{5,7},{6,4},{7,5},{8,10},{9,11},{10,... | collective-permute-start | bytes 1572872 | tf_op jit(solution)/shard_map/ppermute | solution.py:19
  407.3 55.0 %collective-permute-start.52 = (bf16[1152,2048]{1,0:T(8,128)(2,1)}, bf16[1152,2048]{1,0:T(8,128)(2,1)}, u32[]{:S(2)}, u32[]{:S(2)}) collective-permute-start(bf16[1152,2048]{1,0:T(8,128)(2,1)} %shard_map.289), channel_id=1, source_target_pairs={{0,4},{4,0},{8,12},{12,8},{16,20},{20,16},{24,28},{28,24},{1,5},{5... | collective-permute-start | bytes 14155784 | tf_op jit(solution)/shard_map/ppermute | solution.py:19
  416.7 40.4 %collective-permute-start.49 = (bf16[2,256,1280]{2,1,0:T(8,128)(2,1)}, bf16[2,256,1280]{2,1,0:T(8,128)(2,1)}, u32[]{:S(2)}, u32[]{:S(2)}) collective-permute-start(bf16[2,256,1280]{2,1,0:T(8,128)(2,1)} %get-tuple-element.395), channel_id=1, source_target_pairs={{0,16},{4,20},{8,24},{12,28},{16,0},{20,4},{24,8},{28,12},{1,17},{... | collective-permute-start | bytes 3932168 | tf_op jit(solution)/shard_map/ppermute | solution.py:19
  456.0 30.3 %collective-permute-start.48 = (bf16[528,512]{1,0:T(8,128)(2,1)}, bf16[528,512]{1,0:T(8,128)(2,1)}, u32[]{:S(2)}, u32[]{:S(2)}) collective-permute-start(bf16[528,512]{1,0:T(8,128)(2,1)} %add_convert_fusion.16), channel_id=1, source_target_pairs={{0,2},{1,3},{2,0},{3,1},{4,6},{5,7},{6,4},{7,5},{8,10},{9,11},{10,... | collective-permute-start | bytes 1622024 | tf_op jit(solution)/shard_map/ppermute | solution.py:19
  459.2 27.0 %collective-permute-start.50 = (bf16[1,256,1280]{2,1,0:T(8,128)(2,1)}, bf16[1,256,1280]{2,1,0:T(8,128)(2,1)}, u32[]{:S(2)}, u32[]{:S(2)}) collective-permute-start(bf16[1,256,1280]{2,1,0:T(8,128)(2,1)} %add_convert_fusion.11), channel_id=1, source_target_pairs={{0,8},{4,12},{8,0},{12,4},{16,24},{20,28},{24,16},{28,20},{1,9},{5... | collective-permute-start | bytes 1966088 | tf_op jit(solution)/shard_map/ppermute | solution.py:19
  461.6 24.6 %collective-permute-start.51 = (bf16[1,256,1024]{2,1,0:T(8,128)(2,1)}, bf16[1,256,1024]{2,1,0:T(8,128)(2,1)S(1)}, u32[]{:S(2)}, u32[]{:S(2)}) collective-permute-start(bf16[1,256,1024]{2,1,0:T(8,128)(2,1)} %add_convert_fusion.18), channel_id=1, source_target_pairs={{0,8},{4,12},{8,0},{12,4},{16,24},{20,28},{24,16},{28,20},{1,9},{5... | collective-permute-start | bytes 1572872 | tf_op jit(solution)/shard_map/ppermute | solution.py:19
  (82 other events, 1085.7 us)
Sparse Core Ops, SparseCore 0:
  9.6 58.8 all-gather.1

commit v4 on v3

--- a/solution.py
+++ b/solution.py
@@ -989,15 +989,7 @@
     dbranch, row_sums = rows_back(
         z, back_terms, dy_own, middle, shares, moe_gain, router_rows, experts
     )
-    def share_step(small, bit):
-        small = small.reshape((small.shape[0], -1, 2, model_width // expert_size))
-        mine = (expert_pos >> bit) & 1
-        send = lax.dynamic_index_in_dim(small, 1 - mine, 2, False)
-        keep = lax.dynamic_index_in_dim(small, mine, 2, False)
-        return keep, swap(send, "expert", 1 << bit)
-
-    row_share = row_sums[: experts + 1]
-    row_keep, row_came = share_step(row_share, 0)
+    row_sums = row_sums[: experts + 1]
     lower = list(range(group // 2 - 1, -1, -1))
     pieces, last = {0: dbranch}, dbranch
     for bit in reversed(range(bits_of("tensor"))):
@@ -1059,19 +1051,15 @@
     out_terms = [out_own[0]] + [came_r[0] for came_r in out_came]
     out_came = out_far
     out_sums = {d: add_low(out_parts[d], v) if d else None for d, v in out_came.items()}
-    row_keep, row_came = share_step(row_keep + row_came, 1)
     held = after(held, out_sums)
     out_terms = out_terms + [out_came[0]] + passed_on(out_sums, "tensor")
     *cols_out, low_last, row_scale = attention_backward(
         *attention, kept, None, [branch_low] + held
     )
     col_parts = cols_out
-    for bit in range(2, bits_of("expert")):
-        row_keep, row_came = share_step(row_keep + row_came, bit)
     low_last, theirs[0][3], wo_came, out_terms = together(
         low_last, theirs[0][3], wo_came, out_terms
     )
-    row_share = (row_keep + row_came).reshape(experts + 1, -1)
     for bit in far_bits[1:]:
         wo_keep, wo_send = halves_after(wo_keep, wo_came)
         wo_came = swap(wo_send, "expert", 1 << bit)
@@ -1080,17 +1068,19 @@
     q_came = swap(q_send, "expert", 1)
     q_keep, q_send = halves_after(q_keep, q_came)
     q_came = swap(q_send, "expert", 1 << far_bits[0])
-    col_came = after(col_came, theirs[0][4], q_send)
+    col_came = after(col_came, theirs[0][4], q_send, wo_came)
     gate_flat, up_flat, down_flat = sum_of_grads(mine[0], theirs[0])
     gate_grad = jnp.swapaxes(gate_flat.reshape(shape), 1, 2)
     up_grad = jnp.swapaxes(up_flat.reshape(shape), 1, 2)
     down_grad = down_flat.reshape(shape)
-    col_terms = [col_parts[0], col_came[0]] + further_terms(col_parts, col_came, "tensor")
+    col_sums = {d: add_low(col_parts[d], v) if d else None for d, v in col_came.items()}
+    q_came = after(q_came, col_sums)
+    col_terms = [col_parts[0], col_came[0]] + passed_on(col_sums, "tensor")
     for bit in far_bits[1:]:
         q_keep, q_send = halves_after(q_keep, q_came)
         q_came = swap(q_send, "expert", 1 << bit)
     out_weight_grad = (wo_keep[0].astype(F32) + wo_came[0].astype(F32)).T
-    col_terms = after(col_terms, q_came, wo_came, gate_flat, row_share)
+    col_terms = after(col_terms, q_came, gate_flat)
     input_grad, small = input_grad_of(z, col_terms, tokens, branch_low, attn_gain, row_scale)
     gains = small[1 : 1 + tensor_size].reshape(1, model_width)
     qkv = q_keep[0].astype(F32) + q_came[0].astype(F32)
@@ -1112,8 +1102,10 @@
         small[1 + tensor_size : 3 + tensor_size, :head_dim].reshape(2, expert_size, head_each),
         ((0, 0), (0, 0), (0, columns_each - head_each)),
     )
-    small = share_of_sum(jnp.concatenate([gains, spread.reshape(2, model_width)], axis=0))
-    row_share = sum_everywhere(after(row_share, input_grad), "tensor")
+    small = share_of_sum(
+        jnp.concatenate([gains, spread.reshape(2, model_width), row_sums], axis=0)
+    )
+    row_share = sum_everywhere(small[3:], "tensor")
     mixed = functools.reduce(jnp.add, [t.astype(F32) for t in out_terms])
     block_out = mixed.astype(B16)
 

time: 521 us -> 518 us (level)
  waiting for transfers between devices: 183 us -> 191 us
    ppermute x62 -> x59, waiting for transfers between devices: 182 us -> 190 us  [swap(): return lax.ppermute(values, axis, [(i, i ^ mask) for i in range(count)])]
    ppermute x62 -> x59, starting transfers between devices: 56.6 us -> 52 us  [swap(): return lax.ppermute(values, axis, [(i, i ^ mask) for i in range(count)])]
  transfers between devices with their start and end apart: 63 -> 60, of which waited for: 29 -> 34; matrix products, arithmetic and copies ran while one was open for 7% -> 6% of each run, Pallas kernels for 30% -> 30%
where the time goes in v4:
time: 518 us; the launch traced here: 513 us
  Pallas kernels  215 us (42%)
  waiting for transfers between devices  191 us (37%)
  starting transfers between devices  52 us (10%)
  other arithmetic  24.9 us (5%)
  between operations  15.2 us (3%)
  local copies, waits for them, and re-layouts  14.8 us (3%)
    ppermute x59, waiting for transfers between devices, swap(): return lax.ppermute(values, axis, [(i, i ^ mask) for i in range(count)])  190 us
    pallas_call x2, Pallas kernels, expert_pass(): pl.pallas_call(functools.partial(expert_kernel, tuple(places), group, slo...  63.3 us
    ppermute x59, starting transfers between devices, swap(): return lax.ppermute(values, axis, [(i, i ^ mask) for i in range(count)])  52 us
    pallas_call x4, Pallas kernels, expert_grads(): pl.pallas_call(functools.partial(grads_kernel, len(sources)), grid=(3,),...  43.5 us
    pallas_call x2, Pallas kernels, attention_backward(): pl.pallas_call(functools.partial(backward_kernel, min(rows, 256), parts,...  35.1 us
    pallas_call x1, Pallas kernels, attention_forward(): pl.pallas_call(functools.partial(forward_kernel, min(rows, 256)), grid_sp...  26 us
    convert_element_type x13, other arithmetic, add_low(): functools.reduce(jnp.add, [v.astype(F32) for v in values]).astype(B16)  18.5 us
    pallas_call x1, Pallas kernels, expert_outputs(): pl.pallas_call(functools.partial(outputs_kernel, parts, len(acts), group)...  14.4 us
  transfers between devices with their start and end apart: 60, of which 34 were waited for; matrix products, arithmetic and copies ran while one was open for 6% of the time, Pallas kernels for 30%

profile of v4, /device:TPU:0, one launch (start us, length us, event | category | flops | bytes accessed | tf_op | source)
XLA Modules:
  0.0 512.6 jit_solution(6440109796663099194)
XLA Ops:
  12.5 26.0 %shard_map.281 = (bf16[128,2048]{1,0:T(8,128)(2,1)}, bf16[128,2048]{1,0:T(8,128)(2,1)}, bf16[128,2048]{1,0:T(8,128)(2,1)}, bf16[128,2048]{1,0:T(8,128)(2,1)}, bf...) custom-call(s32[1]{0:T(128)} %bitcast.z_ref.refs_0_, ...), custom_call_target="tpu_custom_call" | custom-call | bytes 280800000 | tf_op jit(solution)/shard_map/pallas_call | solution.py:221
  42.6 25.4 %collective-permute-done.1 = bf16[128,2048]{1,0:T(8,128)(2,1)S(1)} collective-permute-done((bf16[128,2048]{1,0:T(8,128)(2,1)}, bf16[128,2048]{1,0:T(8,128)(2,1)S(1)}, u32[]{:S(2)}, u32[]{:S(2)}) %collective-permute-start.1) | collective-permute-done | bytes 524320 | tf_op jit(solution)/shard_map/ppermute | solution.py:19
  74.2 11.9 %collective-permute-done.refs_1_ = bf16[128,2048]{1,0:T(8,128)(2,1)S(1)} collective-permute-done((bf16[128,2048]{1,0:T(8,128)(2,1)}, bf16[128,2048]{1,0:T(8,128)(2,1)S(1)}, u32[]{:S(2)}, u32[]{:S(2)}) %collective-permute-start) | collective-permute-done | bytes 524320 | tf_op jit(solution)/shard_map/ppermute | solution.py:19
  86.1 10.0 %collective-permute-done.3.refs_2_ = bf16[128,2048]{1,0:T(8,128)(2,1)S(1)} collective-permute-done((bf16[128,2048]{1,0:T(8,128)(2,1)}, bf16[128,2048]{1,0:T(8,128)(2,1)S(1)}, u32[]{:S(2)}, u32[]{:S(2)}) %collective-permute-start.3) | collective-permute-done | bytes 524320 | tf_op jit(solution)/shard_map/ppermute | solution.py:19
  103.4 9.6 %collective-permute-done.7.refs_15_.refs_4_ = bf16[384,2048]{1,0:T(8,128)(2,1)} collective-permute-done((bf16[384,2048]{1,0:T(8,128)(2,1)}, bf16[384,2048]{1,0:T(8,128)(2,1)}, u32[]{:S(2)}, u32[]{:S(2)}) %collective-permute-start.7) | collective-permute-done | bytes 1572896 | tf_op jit(solution)/shard_map/ppermute | solution.py:19
  114.8 10.9 %collective-permute-done.5.refs_3_ = bf16[128,2176]{1,0:T(8,128)(2,1)S(1)} collective-permute-done((bf16[128,2176]{1,0:T(8,128)(2,1)}, bf16[128,2176]{1,0:T(8,128)(2,1)S(1)}, u32[]{:S(2)}, u32[]{:S(2)}) %collective-permute-start.5) | collective-permute-done | bytes 557088 | tf_op jit(solution)/shard_map/ppermute | solution.py:19
  130.8 8.9 %collective-permute-done.8.refs_5_ = bf16[128,2176]{1,0:T(8,128)(2,1)} collective-permute-done((bf16[128,2176]{1,0:T(8,128)(2,1)}, bf16[128,2176]{1,0:T(8,128)(2,1)}, u32[]{:S(2)}, u32[]{:S(2)}) %collective-permute-start.8) | collective-permute-done | bytes 557088 | tf_op jit(solution)/shard_map/ppermute | solution.py:19
  147.9 31.4 %shard_map.283 = (bf16[128,2176]{1,0:T(8,128)(2,1)}, bf16[128,2176]{1,0:T(8,128)(2,1)}, bf16[128,2176]{1,0:T(8,128)(2,1)}, bf16[128,2176]{1,0:T(8,128)(2,1)}, bf...) custom-call(s32[1]{0:T(128)} %bitcast.z_ref.refs_0_, s32[8]{0:T(128)} %pad_add_fusion.refs_1_, ...), custom_call_target="tpu_custom_call" | custom-call | bytes 334800000 | tf_op jit(solution)/shard_map/pallas_call | solution.py:716
  179.5 31.9 %shard_map.284 = (bf16[128,2176]{1,0:T(8,128)(2,1)}, bf16[128,2176]{1,0:T(8,128)(2,1)}, bf16[128,2176]{1,0:T(8,128)(2,1)}, bf16[128,2176]{1,0:T(8,128)(2,1)}, bf...) custom-call(s32[1]{0:T(128)} %bitcast.z_ref.refs_0_, s32[8]{0:T(128)} %pad_add_fusion.refs_1_, ...), custom_call_target="tpu_custom_call" | custom-call | bytes 334800000 | tf_op jit(solution)/shard_map/pallas_call | solution.py:716
  214.3 14.4 %shard_map.285 = (bf16[512,512]{1,0:T(8,128)(2,1)}, bf16[512,512]{1,0:T(8,128)(2,1)}, bf16[512,512]{1,0:T(8,128)(2,1)}, bf16[512,512]{1,0:T(8,128)(2,1)}, bf16[5...) custom-call(s32[1]{0:T(128)} %bitcast.z_ref.refs_0_, ...), custom_call_target="tpu_custom_call" | custom-call | bytes 108000000 | tf_op jit(solution)/shard_map/pallas_call | solution.py:761
  228.7 10.4 %collective-permute-done.21 = bf16[128,2176]{1,0:T(8,128)(2,1)S(1)} collective-permute-done((bf16[128,2176]{1,0:T(8,128)(2,1)}, bf16[128,2176]{1,0:T(8,128)(2,1)S(1)}, u32[]{:S(2)}, u32[]{:S(2)}) %collective-permute-start.21) | collective-permute-done | bytes 557088 | tf_op jit(solution)/shard_map/ppermute | solution.py:19
  240.8 10.7 %shard_map.286 = bf16[1152,2048]{1,0:T(8,128)(2,1)} custom-call(bf16[512,2176]{1,0:T(8,128)(2,1)} %get-tuple-element.268.refs_0_, bf16[512,2048]{1,0:T(8,128)(2,1)} %all-gather.2.cloned.1.call-done.refs_6_.refs_1_.refs_4_, bf16[4,512,768]{2,1,0:T(8,128)(2,1)} %get-tuple-element.270.refs_2_, bf16[4,512,384]{2,1,0:T(8,128)(2,1)} %get-tuple-element.271.refs_0_.refs_3_, ...), custom_call_target="tpu_custom_call" | custom-call | bytes 118800000 | tf_op jit(solution)/shard_map/pallas_call | solution.py:794
  253.2 11.3 %shard_map.287 = bf16[1152,2048]{1,0:T(8,128)(2,1)} custom-call(bf16[512,2176]{1,0:T(8,128)(2,1)} %get-tuple-element.268.refs_0_, bf16[512,2048]{1,0:T(8,128)(2,1)} %all-gather.2.cloned.1.call-done.refs_6_.refs_1_.refs_4_, bf16[4,512,768]{2,1,0:T(8,128)(2,1)} %get-tuple-element.270.refs_2_, bf16[4,512,384]{2,1,0:T(8,128)(2,1)} %get-tuple-element.271.refs_0_.refs_3_, ...), custom_call_target="tpu_custom_call" | custom-call | bytes 118800000 | tf_op jit(solution)/shard_map/pallas_call | solution.py:794
  268.8 3.6 collective-permute-done.31
  272.5 4.2 add_convert_fusion.4
  279.6 11.5 %collective-permute-done.20.refs_1_ = bf16[128,2176]{1,0:T(8,128)(2,1)S(1)} collective-permute-done((bf16[128,2176]{1,0:T(8,128)(2,1)}, bf16[128,2176]{1,0:T(8,128)(2,1)S(1)}, u32[]{:S(2)}, u32[]{:S(2)}) %collective-permute-start.20) | collective-permute-done | bytes 557088 | tf_op jit(solution)/shard_map/ppermute | solution.py:19
  294.8 4.0 shard_map.288
  303.9 10.7 %shard_map.289 = bf16[1152,2048]{1,0:T(8,128)(2,1)} custom-call(bf16[512,2176]{1,0:T(8,128)(2,1)} %get-tuple-element.268.refs_0_, bf16[512,2048]{1,0:T(8,128)(2,1)} %all-gather.2.cloned.1.call-done.refs_6_.refs_1_.refs_4_, bf16[4,512,768]{2,1,0:T(8,128)(2,1)} %get-tuple-element.270.refs_2_, bf16[4,512,384]{2,1,0:T(8,128)(2,1)} %get-tuple-element.271.refs_0_.refs_3_, ...), custom_call_target="tpu_custom_call" | custom-call | bytes 118800000 | tf_op jit(solution)/shard_map/pallas_call | solution.py:794
  314.6 7.9 %collective-permute-done.29.refs_2_ = bf16[128,2048]{1,0:T(8,128)(2,1)S(1)} collective-permute-done((bf16[128,2048]{1,0:T(8,128)(2,1)}, bf16[128,2048]{1,0:T(8,128)(2,1)S(1)}, u32[]{:S(2)}, u32[]{:S(2)}) %collective-permute-start.29) | collective-permute-done | bytes 524320 | tf_op jit(solution)/shard_map/ppermute | solution.py:19
  325.2 10.8 %shard_map.290.refs_0_ = bf16[1152,2048]{1,0:T(8,128)(2,1)} custom-call(bf16[512,2176]{1,0:T(8,128)(2,1)} %get-tuple-element.268.refs_0_, bf16[512,2048]{1,0:T(8,128)(2,1)} %all-gather.2.cloned.1.call-done.refs_6_.refs_1_.refs_4_, bf16[4,512,768]{2,1,0:T(8,128)(2,1)} %get-tuple-element.270.refs_2_, bf16[4,512,384]{2,1,0:T(8,128)(2,1)} %get-tuple-element.271.refs_0_.refs_3_, ...), custom_call_target="tpu_custom_call" | custom-call | bytes 118800000 | tf_op jit(solution)/shard_map/pallas_call | solution.py:794
  338.6 5.7 %shard_map.291 = (bf16[4,256,1024]{2,1,0:T(8,128)(2,1)}, bf16[4,256,1024]{2,1,0:T(8,128)(2,1)}) custom-call(s32[8]{0:T(128)} %broadcast_xor_fusion.order_ref, bf16[512,2048]{1,0:T(8,128)(2,1)} %copy-done.1, bf16[512,1024]{1,0:T(8,128)(2,1)} %get-tuple-element.281.refs_0_), custom_call_target="tpu_custom_call" | custom-call | bytes 64800000 | tf_op jit(solution)/shard_map/pallas_call | solution.py:453
  350.4 14.9 %shard_map.292 = (bf16[512,2048]{1,0:T(8,128)(2,1)}, bf16[512,512]{1,0:T(8,128)(2,1)}, f32[512,2048]{1,0:T(8,128)}, f32[512,128]{1,0:T(8,128)}, f32[512,128]{1,0:T(8,128)}, /*index=5*/f32[8,2048]{1,0:T(8,128)}) custom-call(s32[1]{0:T(128)} %bitcast.z_ref.refs_0_, s32[512,1]{1,0:T(8,128)} %copy.39.seq_col, s32[1,512]{1,0:T(1,128)} %bitcast.72, ...), custom_call_target="tpu_custom_call" | custom-call | bytes 172800000 | tf_op jit(solution)/shard_map/pallas_call | solution.py:411
  366.4 6.3 %collective-permute-done.37 = bf16[512,512]{1,0:T(8,128)(2,1)} collective-permute-done((bf16[512,512]{1,0:T(8,128)(2,1)}, bf16[512,512]{1,0:T(8,128)(2,1)}, u32[]{:S(2)}, u32[]{:S(2)}) %collective-permute-start.37) | collective-permute-done | bytes 524320 | tf_op jit(solution)/shard_map/ppermute | solution.py:19
  378.7 20.2 %shard_map.293 = (bf16[528,512]{1,0:T(8,128)(2,1)}, bf16[528,512]{1,0:T(8,128)(2,1)}, bf16[528,512]{1,0:T(8,128)(2,1)}, bf16[528,512]{1,0:T(8,128)(2,1)}, bf16[512,768]{1,0:T(8,128)(2,1)}, /*index=5*/f32[512,1]{1,0:T(8,128)}) custom-call(s32[1]{0:T(128)} %bitcast.z_ref.refs_0_, s32[512,1]{1,0:T(8,128)} %copy.39.seq_col, s32[1,512]{1,0:T(1,128)} %bitcast.73, ...), custom_call_target="tpu_custom_call" | custom-call | bytes 172800000 | tf_op jit(solution)/shard_map/pallas_call | solution.py:411
  400.8 7.0 %shard_map.294 = (bf16[4,256,1280]{2,1,0:T(8,128)(2,1)}, bf16[4,256,1280]{2,1,0:T(8,128)(2,1)}) custom-call(s32[8]{0:T(128)} %broadcast_xor_fusion.order_ref, bf16[512,2048]{1,0:T(8,128)(2,1)} %get-tuple-element.321.left_ref, bf16[512,512]{1,0:T(8,128)(2,1)} %get-tuple-element.322.refs_0_, bf16[512,768]{1,0:T(8,128)(2,1)} %get-tuple-element.323.refs_1_), custom_call_target="tpu_custom_call" | custom-call | bytes 64800000 | tf_op jit(solution)/shard_map/pallas_call | solution.py:453
  409.8 6.7 %collective-permute-done.47 = bf16[4,256,1280]{2,1,0:T(8,128)(2,1)S(1)} collective-permute-done((bf16[4,256,1280]{2,1,0:T(8,128)(2,1)}, bf16[4,256,1280]{2,1,0:T(8,128)(2,1)S(1)}, u32[]{:S(2)}, u32[]{:S(2)}) %collective-permute-start.47) | collective-permute-done | bytes 2621472 | tf_op jit(solution)/shard_map/ppermute | solution.py:19
  422.4 5.4 %collective-permute-done.46.refs_6_ = bf16[192,2048]{1,0:T(8,128)(2,1)S(1)} collective-permute-done((bf16[192,2048]{1,0:T(8,128)(2,1)S(1)}, bf16[192,2048]{1,0:T(8,128)(2,1)S(1)}, u32[]{:S(2)}, u32[]{:S(2)}) %collective-permute-start.46) | collective-permute-done | bytes 786464 | tf_op jit(solution)/shard_map/ppermute | solution.py:19
  429.4 5.9 %collective-permute-done.44.refs_1_ = bf16[528,512]{1,0:T(8,128)(2,1)S(1)} collective-permute-done((bf16[528,512]{1,0:T(8,128)(2,1)S(1)}, bf16[528,512]{1,0:T(8,128)(2,1)S(1)}, u32[]{:S(2)}, u32[]{:S(2)}) %collective-permute-start.44) | collective-permute-done | bytes 540704 | tf_op jit(solution)/shard_map/ppermute | solution.py:19
  436.1 9.7 %collective-permute-done.45 = bf16[528,512]{1,0:T(8,128)(2,1)S(1)} collective-permute-done((bf16[528,512]{1,0:T(8,128)(2,1)S(1)}, bf16[528,512]{1,0:T(8,128)(2,1)S(1)}, u32[]{:S(2)}, u32[]{:S(2)}) %collective-permute-start.45) | collective-permute-done | bytes 540704 | tf_op jit(solution)/shard_map/ppermute | solution.py:19
  453.9 5.7 %collective-permute-done.53.refs_7_ = bf16[192,2048]{1,0:T(8,128)(2,1)} collective-permute-done((bf16[192,2048]{1,0:T(8,128)(2,1)S(1)}, bf16[192,2048]{1,0:T(8,128)(2,1)}, u32[]{:S(2)}, u32[]{:S(2)}) %collective-permute-start.53) | collective-permute-done | bytes 786464 | tf_op jit(solution)/shard_map/ppermute | solution.py:19
  459.6 9.0 %shard_map.295 = (f32[384,2048]{1,0:T(8,128)}, f32[384,2048]{1,0:T(8,128)}, f32[384,2048]{1,0:T(8,128)}) custom-call(bf16[1152,2048]{1,0:T(8,128)(2,1)} %shard_map.290.refs_0_, bf16[1152,2048]{1,0:T(8,128)(2,1)} %collective-permute-done.52.refs_1_, bf16[192,2048]{1,0:T(8,128)(2,1)} %copy-done.17, bf16[192,2048]{1,0:T(8,128)(2,1)} %collective-permute-done.34.refs_3_, ...), custom_call_target="tpu_custom_call" | custom-call | bytes 86400000 | tf_op jit(solution)/shard_map/pallas_call | solution.py:832
  468.6 10.7 %collective-permute-done.49.refs_2_ = bf16[528,512]{1,0:T(8,128)(2,1)} collective-permute-done((bf16[528,512]{1,0:T(8,128)(2,1)}, bf16[528,512]{1,0:T(8,128)(2,1)}, u32[]{:S(2)}, u32[]{:S(2)}) %collective-permute-start.49) | collective-permute-done | bytes 540704 | tf_op jit(solution)/shard_map/ppermute | solution.py:19
  (274 shorter events, 124.8 us)
Async XLA Ops:
  7.2 64.6 %all-gather.2.cloned.1.call-start = ((), (), s32[]{:S(2)}) async-start(), calls=%async_computation | async-start | bytes 2621440 | tf_op jit(solution)/shard_map/all_gather | solution.py:887
  7.9 60.0 %collective-permute-start.2 = (bf16[384,2048]{1,0:T(8,128)(2,1)}, bf16[384,2048]{1,0:T(8,128)(2,1)S(1)}, u32[]{:S(2)}, u32[]{:S(2)}) collective-permute-start(bf16[384,2048]{1,0:T(8,128)(2,1)} %bitcast.51), channel_id=1, source_target_pairs={{0,8},{4,12},{8,0},{12,4},{16,24},{20,28},{24,16},{28,20},{1,9},{5... | collective-permute-start | bytes 4718600 | tf_op jit(solution)/shard_map/ppermute | solution.py:19
  10.9 75.2 %collective-permute-start.4 = (bf16[384,2048]{1,0:T(8,128)(2,1)}, bf16[384,2048]{1,0:T(8,128)(2,1)}, u32[]{:S(2)}, u32[]{:S(2)}) collective-permute-start(bf16[384,2048]{1,0:T(8,128)(2,1)} %bitcast.55), channel_id=1, source_target_pairs={{0,8},{4,12},{8,0},{12,4},{16,24},{20,28},{24,16},{28,20},{1,9},{5... | collective-permute-start | bytes 4718600 | tf_op jit(solution)/shard_map/ppermute | solution.py:19
  38.5 29.4 %collective-permute-start.1 = (bf16[128,2048]{1,0:T(8,128)(2,1)}, bf16[128,2048]{1,0:T(8,128)(2,1)S(1)}, u32[]{:S(2)}, u32[]{:S(2)}) collective-permute-start(bf16[128,2048]{1,0:T(8,128)(2,1)} %get-tuple-element.188), channel_id=1, source_target_pairs={{0,1},{1,0},{2,3},{3,2},{4,5},{5,4},{6,7},{7,6},{8,9},{9,8},{10,11... | collective-permute-start | bytes 1572872 | tf_op jit(solution)/shard_map/ppermute | solution.py:19
  40.6 72.4 %collective-permute-start.7 = (bf16[384,2048]{1,0:T(8,128)(2,1)}, bf16[384,2048]{1,0:T(8,128)(2,1)}, u32[]{:S(2)}, u32[]{:S(2)}) collective-permute-start(bf16[384,2048]{1,0:T(8,128)(2,1)} %bitcast.14.refs_9_.refs_2_), channel_id=1, source_target_pairs={{0,8},{4,12},{8,0},{12,4},{16,24},{20,28},{24,16},{28,20},{1,9},{5... | collective-permute-start | bytes 4718600 | tf_op jit(solution)/shard_map/ppermute | solution.py:19
  42.1 44.0 %collective-permute-start = (bf16[128,2048]{1,0:T(8,128)(2,1)}, bf16[128,2048]{1,0:T(8,128)(2,1)S(1)}, u32[]{:S(2)}, u32[]{:S(2)}) collective-permute-start(bf16[128,2048]{1,0:T(8,128)(2,1)} %get-tuple-element.186), channel_id=1, source_target_pairs={{0,1},{1,0},{2,3},{3,2},{4,5},{5,4},{6,7},{7,6},{8,9},{9,8},{10,11... | collective-permute-start | bytes 1572872 | tf_op jit(solution)/shard_map/ppermute | solution.py:19
  70.3 25.9 %collective-permute-start.3 = (bf16[128,2048]{1,0:T(8,128)(2,1)}, bf16[128,2048]{1,0:T(8,128)(2,1)S(1)}, u32[]{:S(2)}, u32[]{:S(2)}) collective-permute-start(bf16[128,2048]{1,0:T(8,128)(2,1)} %add_convert_fusion.24), channel_id=1, source_target_pairs={{0,2},{1,3},{2,0},{3,1},{4,6},{5,7},{6,4},{7,5},{8,10},{9,11},{10,... | collective-permute-start | bytes 1572872 | tf_op jit(solution)/shard_map/ppermute | solution.py:19
  71.8 68.4 %collective-permute-start.10 = (bf16[512,2048]{1,0:T(8,128)(2,1)}, bf16[512,2048]{1,0:T(8,128)(2,1)S(1)}, u32[]{:S(2)}, u32[]{:S(2)}) collective-permute-start(bf16[512,2048]{1,0:T(8,128)(2,1)} %all-gather.2.cloned.1.call-done.refs_6_.refs_1_.refs_4_), channel_id=1, source_target_pairs={{0,16},{4,20},{8,24},{12,28},{16,0},{20,4},{24,8},{28,12},{1,17},{... | collective-permute-start | bytes 6291464 | tf_op jit(solution)/shard_map/ppermute | solution.py:19
  100.5 25.2 %collective-permute-start.5 = (bf16[128,2176]{1,0:T(8,128)(2,1)}, bf16[128,2176]{1,0:T(8,128)(2,1)S(1)}, u32[]{:S(2)}, u32[]{:S(2)}) collective-permute-start(bf16[128,2176]{1,0:T(8,128)(2,1)} %get-tuple-element.193.refs_2_), channel_id=1, source_target_pairs={{0,1},{1,0},{2,3},{3,2},{4,5},{5,4},{6,7},{7,6},{8,9},{9,8},{10,11... | collective-permute-start | bytes 1671176 | tf_op jit(solution)/shard_map/ppermute | solution.py:19
  100.5 26.6 %collective-permute-start.6 = (bf16[128,2176]{1,0:T(8,128)(2,1)}, bf16[128,2176]{1,0:T(8,128)(2,1)}, u32[]{:S(2)}, u32[]{:S(2)}) collective-permute-start(bf16[128,2176]{1,0:T(8,128)(2,1)} %get-tuple-element.193.refs_2_), channel_id=1, source_target_pairs={{0,2},{1,3},{2,0},{3,1},{4,6},{5,7},{6,4},{7,5},{8,10},{9,11},{10,... | collective-permute-start | bytes 1671176 | tf_op jit(solution)/shard_map/ppermute | solution.py:19
  103.4 36.3 %collective-permute-start.12 = (bf16[384,2048]{1,0:T(8,128)(2,1)S(1)}, bf16[384,2048]{1,0:T(8,128)(2,1)S(1)}, u32[]{:S(2)}, u32[]{:S(2)}) collective-permute-start(bf16[384,2048]{1,0:T(8,128)(2,1)S(1)} %bitcast.58), channel_id=1, source_target_pairs={{0,4},{4,0},{8,12},{12,8},{16,20},{20,16},{24,28},{28,24},{1,5},{5... | collective-permute-start | bytes 4718600 | tf_op jit(solution)/shard_map/ppermute | solution.py:19
  140.3 39.1 %collective-permute-start.18 = (bf16[128,2176]{1,0:T(8,128)(2,1)}, bf16[128,2176]{1,0:T(8,128)(2,1)}, u32[]{:S(2)}, u32[]{:S(2)}) collective-permute-start(bf16[128,2176]{1,0:T(8,128)(2,1)} %collective-permute-done.6.refs_4_), channel_id=1, source_target_pairs={{0,16},{4,20},{8,24},{12,28},{16,0},{20,4},{24,8},{28,12},{1,17},{... | collective-permute-start | bytes 1671176 | tf_op jit(solution)/shard_map/ppermute | solution.py:19
  141.1 38.3 %collective-permute-start.17 = (bf16[128,2176]{1,0:T(8,128)(2,1)S(1)}, bf16[128,2176]{1,0:T(8,128)(2,1)}, u32[]{:S(2)}, u32[]{:S(2)}) collective-permute-start(bf16[128,2176]{1,0:T(8,128)(2,1)S(1)} %collective-permute-done.5.refs_3_), channel_id=1, source_target_pairs={{0,16},{4,20},{8,24},{12,28},{16,0},{20,4},{24,8},{28,12},{1,17},{... | collective-permute-start | bytes 1671176 | tf_op jit(solution)/shard_map/ppermute | solution.py:19
  145.7 33.8 %collective-permute-start.19 = (bf16[128,2176]{1,0:T(8,128)(2,1)}, bf16[128,2176]{1,0:T(8,128)(2,1)}, u32[]{:S(2)}, u32[]{:S(2)}) collective-permute-start(bf16[128,2176]{1,0:T(8,128)(2,1)} %collective-permute-done.8.refs_5_), channel_id=1, source_target_pairs={{0,16},{4,20},{8,24},{12,28},{16,0},{20,4},{24,8},{28,12},{1,17},{... | collective-permute-start | bytes 1671176 | tf_op jit(solution)/shard_map/ppermute | solution.py:19
  212.2 26.9 %collective-permute-start.21 = (bf16[128,2176]{1,0:T(8,128)(2,1)}, bf16[128,2176]{1,0:T(8,128)(2,1)S(1)}, u32[]{:S(2)}, u32[]{:S(2)}) collective-permute-start(bf16[128,2176]{1,0:T(8,128)(2,1)} %get-tuple-element.212), channel_id=1, source_target_pairs={{0,16},{4,20},{8,24},{12,28},{16,0},{20,4},{24,8},{28,12},{1,17},{... | collective-permute-start | bytes 1671176 | tf_op jit(solution)/shard_map/ppermute | solution.py:19
  213.5 38.0 %collective-permute-start.23 = (bf16[128,2176]{1,0:T(8,128)(2,1)}, bf16[128,2176]{1,0:T(8,128)(2,1)S(1)}, u32[]{:S(2)}, u32[]{:S(2)}) collective-permute-start(bf16[128,2176]{1,0:T(8,128)(2,1)} %get-tuple-element.220), channel_id=1, source_target_pairs={{0,16},{4,20},{8,24},{12,28},{16,0},{20,4},{24,8},{28,12},{1,17},{... | collective-permute-start | bytes 1671176 | tf_op jit(solution)/shard_map/ppermute | solution.py:19
  265.4 25.7 %collective-permute-start.20 = (bf16[128,2176]{1,0:T(8,128)(2,1)}, bf16[128,2176]{1,0:T(8,128)(2,1)S(1)}, u32[]{:S(2)}, u32[]{:S(2)}) collective-permute-start(bf16[128,2176]{1,0:T(8,128)(2,1)} %get-tuple-element.210), channel_id=1, source_target_pairs={{0,16},{4,20},{8,24},{12,28},{16,0},{20,4},{24,8},{28,12},{1,17},{... | collective-permute-start | bytes 1671176 | tf_op jit(solution)/shard_map/ppermute | solution.py:19
  266.6 25.5 %collective-permute-start.22 = (bf16[128,2176]{1,0:T(8,128)(2,1)}, bf16[128,2176]{1,0:T(8,128)(2,1)S(1)}, u32[]{:S(2)}, u32[]{:S(2)}) collective-permute-start(bf16[128,2176]{1,0:T(8,128)(2,1)} %add_convert_fusion.15), channel_id=1, source_target_pairs={{0,1},{1,0},{2,3},{3,2},{4,5},{5,4},{6,7},{7,6},{8,9},{9,8},{10,11... | collective-permute-start | bytes 1671176 | tf_op jit(solution)/shard_map/ppermute | solution.py:19
  267.5 27.3 %collective-permute-start.26 = (bf16[128,2176]{1,0:T(8,128)(2,1)}, bf16[128,2176]{1,0:T(8,128)(2,1)}, u32[]{:S(2)}, u32[]{:S(2)}) collective-permute-start(bf16[128,2176]{1,0:T(8,128)(2,1)} %add_convert_fusion.12), channel_id=1, source_target_pairs={{0,2},{1,3},{2,0},{3,1},{4,6},{5,7},{6,4},{7,5},{8,10},{9,11},{10,... | collective-permute-start | bytes 1671176 | tf_op jit(solution)/shard_map/ppermute | solution.py:19
  276.6 45.8 %collective-permute-start.32 = (bf16[192,2048]{1,0:T(8,128)(2,1)S(1)}, bf16[192,2048]{1,0:T(8,128)(2,1)S(1)}, u32[]{:S(2)}, u32[]{:S(2)}) collective-permute-start(bf16[192,2048]{1,0:T(8,128)(2,1)S(1)} %get-tuple-element.379), channel_id=1, source_target_pairs={{0,8},{4,12},{8,0},{12,4},{16,24},{20,28},{24,16},{28,20},{1,9},{5... | collective-permute-start | bytes 2359304 | tf_op jit(solution)/shard_map/ppermute | solution.py:19
  298.8 23.6 %collective-permute-start.29 = (bf16[128,2048]{1,0:T(8,128)(2,1)}, bf16[128,2048]{1,0:T(8,128)(2,1)S(1)}, u32[]{:S(2)}, u32[]{:S(2)}) collective-permute-start(bf16[128,2048]{1,0:T(8,128)(2,1)} %get-tuple-element.283.refs_0_), channel_id=1, source_target_pairs={{0,2},{1,3},{2,0},{3,1},{4,6},{5,7},{6,4},{7,5},{8,10},{9,11},{10,... | collective-permute-start | bytes 1572872 | tf_op jit(solution)/shard_map/ppermute | solution.py:19
  300.3 36.4 %collective-permute-start.34 = (bf16[192,2048]{1,0:T(8,128)(2,1)}, bf16[192,2048]{1,0:T(8,128)(2,1)}, u32[]{:S(2)}, u32[]{:S(2)}) collective-permute-start(bf16[192,2048]{1,0:T(8,128)(2,1)} %get-tuple-element.378), channel_id=1, source_target_pairs={{0,8},{4,12},{8,0},{12,4},{16,24},{20,28},{24,16},{28,20},{1,9},{5... | collective-permute-start | bytes 2359304 | tf_op jit(solution)/shard_map/ppermute | solution.py:19
  301.7 34.4 %collective-permute-start.28 = (bf16[128,2048]{1,0:T(8,128)(2,1)}, bf16[128,2048]{1,0:T(8,128)(2,1)S(1)}, u32[]{:S(2)}, u32[]{:S(2)}) collective-permute-start(bf16[128,2048]{1,0:T(8,128)(2,1)} %get-tuple-element.283.refs_0_), channel_id=1, source_target_pairs={{0,1},{1,0},{2,3},{3,2},{4,5},{5,4},{6,7},{7,6},{8,9},{9,8},{10,11... | collective-permute-start | bytes 1572872 | tf_op jit(solution)/shard_map/ppermute | solution.py:19
  372.7 28.1 %collective-permute-start.42 = (bf16[2,256,1024]{2,1,0:T(8,128)(2,1)S(1)}, bf16[2,256,1024]{2,1,0:T(8,128)(2,1)S(1)}, u32[]{:S(2)}, u32[]{:S(2)}) collective-permute-start(bf16[2,256,1024]{2,1,0:T(8,128)(2,1)S(1)} %get-tuple-element.311), channel_id=1, source_target_pairs={{0,16},{4,20},{8,24},{12,28},{16,0},{20,4},{24,8},{28,12},{1,17},{... | collective-permute-start | bytes 3145736 | tf_op jit(solution)/shard_map/ppermute | solution.py:19
  374.1 24.8 %collective-permute-start.41 = (bf16[192,2048]{1,0:T(8,128)(2,1)S(1)}, bf16[192,2048]{1,0:T(8,128)(2,1)S(1)}, u32[]{:S(2)}, u32[]{:S(2)}) collective-permute-start(bf16[192,2048]{1,0:T(8,128)(2,1)S(1)} %copy-done.21), channel_id=1, source_target_pairs={{0,8},{4,12},{8,0},{12,4},{16,24},{20,28},{24,16},{28,20},{1,9},{5... | collective-permute-start | bytes 2359304 | tf_op jit(solution)/shard_map/ppermute | solution.py:19
  376.1 24.6 %collective-permute-start.43 = (bf16[512,512]{1,0:T(8,128)(2,1)S(1)}, bf16[512,512]{1,0:T(8,128)(2,1)S(1)}, u32[]{:S(2)}, u32[]{:S(2)}) collective-permute-start(bf16[512,512]{1,0:T(8,128)(2,1)S(1)} %add_convert_fusion.20), channel_id=1, source_target_pairs={{0,2},{1,3},{2,0},{3,1},{4,6},{5,7},{6,4},{7,5},{8,10},{9,11},{10,... | collective-permute-start | bytes 1572872 | tf_op jit(solution)/shard_map/ppermute | solution.py:19
  407.7 46.1 %collective-permute-start.52 = (bf16[1152,2048]{1,0:T(8,128)(2,1)}, bf16[1152,2048]{1,0:T(8,128)(2,1)}, u32[]{:S(2)}, u32[]{:S(2)}) collective-permute-start(bf16[1152,2048]{1,0:T(8,128)(2,1)} %shard_map.289), channel_id=1, source_target_pairs={{0,4},{4,0},{8,12},{12,8},{16,20},{20,16},{24,28},{28,24},{1,5},{5... | collective-permute-start | bytes 14155784 | tf_op jit(solution)/shard_map/ppermute | solution.py:19
  419.0 31.0 %collective-permute-start.50 = (bf16[2,256,1280]{2,1,0:T(8,128)(2,1)S(1)}, bf16[2,256,1280]{2,1,0:T(8,128)(2,1)}, u32[]{:S(2)}, u32[]{:S(2)}) collective-permute-start(bf16[2,256,1280]{2,1,0:T(8,128)(2,1)S(1)} %get-tuple-element.381), channel_id=1, source_target_pairs={{0,16},{4,20},{8,24},{12,28},{16,0},{20,4},{24,8},{28,12},{1,17},{... | collective-permute-start | bytes 3932168 | tf_op jit(solution)/shard_map/ppermute | solution.py:19
  420.2 25.6 %collective-permute-start.45 = (bf16[528,512]{1,0:T(8,128)(2,1)S(1)}, bf16[528,512]{1,0:T(8,128)(2,1)S(1)}, u32[]{:S(2)}, u32[]{:S(2)}) collective-permute-start(bf16[528,512]{1,0:T(8,128)(2,1)S(1)} %copy-done.49), channel_id=1, source_target_pairs={{0,1},{1,0},{2,3},{3,2},{4,5},{5,4},{6,7},{7,6},{8,9},{9,8},{10,11... | collective-permute-start | bytes 1622024 | tf_op jit(solution)/shard_map/ppermute | solution.py:19
  435.3 24.3 %collective-permute-start.53 = (bf16[192,2048]{1,0:T(8,128)(2,1)S(1)}, bf16[192,2048]{1,0:T(8,128)(2,1)}, u32[]{:S(2)}, u32[]{:S(2)}) collective-permute-start(bf16[192,2048]{1,0:T(8,128)(2,1)S(1)} %copy-done.18), channel_id=1, source_target_pairs={{0,8},{4,12},{8,0},{12,4},{16,24},{20,28},{24,16},{28,20},{1,9},{5... | collective-permute-start | bytes 2359304 | tf_op jit(solution)/shard_map/ppermute | solution.py:19
  452.1 27.3 %collective-permute-start.51 = (bf16[1,256,1280]{2,1,0:T(8,128)(2,1)}, bf16[1,256,1280]{2,1,0:T(8,128)(2,1)}, u32[]{:S(2)}, u32[]{:S(2)}) collective-permute-start(bf16[1,256,1280]{2,1,0:T(8,128)(2,1)} %add_convert_fusion.11), channel_id=1, source_target_pairs={{0,8},{4,12},{8,0},{12,4},{16,24},{20,28},{24,16},{28,20},{1,9},{5... | collective-permute-start | bytes 1966088 | tf_op jit(solution)/shard_map/ppermute | solution.py:19
  453.7 25.6 %collective-permute-start.49 = (bf16[528,512]{1,0:T(8,128)(2,1)}, bf16[528,512]{1,0:T(8,128)(2,1)}, u32[]{:S(2)}, u32[]{:S(2)}) collective-permute-start(bf16[528,512]{1,0:T(8,128)(2,1)} %add_convert_fusion.16), channel_id=1, source_target_pairs={{0,2},{1,3},{2,0},{3,1},{4,6},{5,7},{6,4},{7,5},{8,10},{9,11},{10,... | collective-permute-start | bytes 1622024 | tf_op jit(solution)/shard_map/ppermute | solution.py:19
  (83 other events, 1071.6 us)
Sparse Core Ops, SparseCore 0:
  9.6 58.8 all-gather.1
